TPU v7x, 32 devices: a whole 2x2x4 slice. The times are simulated.
32 devices in a mesh: chan: 16 (over z, y, x), tm: 2 (over core).
Axes of the slice: x: 2, y: 2, z: 4, core: 2. Of those that a mesh axis runs over, the one named last changes fastest.
Arguments:
- samples: bfloat16 [128, 524288], P('chan', 'tm'), may hold values from -8 to 8
- taps: float32 [16, 4096], replicated, may hold values from -0.0234375 to 0.0234375
- steering: float32 [8, 128], replicated, may hold values from -6 to 6
- interferer_ids: int32 [2048, 4], P(('chan', 'tm')), may hold values from 0 to 7, all different within a row
- ranks: int32 [2048], P(('chan', 'tm')), may hold values from 0 to 4
Outputs:
- covariance: float32 [2048, 2, 128, 128], P(('chan', 'tm'))
Inputs may be any that keep to these rules, and one draw needn't show every extreme that they name: `interferer_ids`: the 4 entries of one channel's row name different directions.
All inputs are finite; a program needn't handle non-finite values.
Results may differ from a plain program's by a relative error of at most 0.00075.
Values may be sent and summed in bfloat16 or wider, within the bound.
No kernel may reach another device: no remote copies, remote signals or barrier semaphores. Data moves between devices by JAX's collectives and lax.ppermute only.
A program may use at most 128 MiB of HBM per device.

v0:
```python
import math

import jax
import jax.numpy as jnp
from jax import lax
from jax.sharding import PartitionSpec as P

first_radix = 64
epsilon = 1e-06
highest = lax.Precision.HIGHEST


def shifted(shard, axis, by):
    peers = lax.axis_size(axis)
    pairs = [(i, i + by) for i in range(peers) if 0 <= i + by < peers]
    return lax.ppermute(shard, axis, pairs)


def phase_table(height, width, period):
    left = lax.broadcasted_iota(jnp.int32, (height, width), 0)
    right = lax.broadcasted_iota(jnp.int32, (height, width), 1)
    turns = left * right % period
    angle = turns.astype(jnp.float32) * (2.0 * math.pi / period)
    return (jnp.cos(angle), jnp.sin(angle))


def channelize(samples, taps):
    antennas, width = samples.shape
    tap_count, length = taps.shape
    frames = width // length
    blocks = samples.reshape(antennas, frames, length)
    carried = shifted(blocks[:, frames - tap_count + 1 :, :], "tm", 1)
    padded = jnp.concatenate([carried, blocks], axis=1)
    filtered = jnp.zeros((antennas, frames, length), jnp.float32)
    for tap_index in range(tap_count):
        filtered = filtered + taps[tap_index] * padded[:, tap_index : tap_index + frames, :].astype(
            jnp.float32
        )
    quarter = length // first_radix
    shaped = filtered.reshape(antennas, frames, first_radix, quarter)
    first_cos, first_sin = phase_table(first_radix, first_radix, first_radix)
    section_real = jnp.einsum("afpq,pk->afqk", shaped, first_cos, precision=highest)
    section_imag = -jnp.einsum("afpq,pk->afqk", shaped, first_sin, precision=highest)
    twist_cos, twist_sin = phase_table(quarter, first_radix, length)
    turned_real = section_real * twist_cos + section_imag * twist_sin
    turned_imag = section_imag * twist_cos - section_real * twist_sin
    second_cos, second_sin = phase_table(quarter, quarter // 2, quarter)
    spec_real = jnp.einsum("afqk,qm->amkf", turned_real, second_cos, precision=highest)
    spec_real = spec_real + jnp.einsum("afqk,qm->amkf", turned_imag, second_sin, precision=highest)
    spec_imag = jnp.einsum("afqk,qm->amkf", turned_imag, second_cos, precision=highest)
    spec_imag = spec_imag - jnp.einsum("afqk,qm->amkf", turned_real, second_sin, precision=highest)
    spectra = jnp.stack([spec_real, spec_imag], axis=1).astype(jnp.bfloat16)
    return spectra.reshape(antennas, 2, length // 2, frames)


def partial_gram(piece):
    block = piece[:, :, 0]
    outer = jnp.einsum("arcf,bscf->crasb", block, block, preferred_element_type=jnp.float32)
    real_part = outer[:, 0, :, 0, :] + outer[:, 1, :, 1, :]
    imag_part = outer[:, 1, :, 0, :] - outer[:, 0, :, 1, :]
    return jnp.stack([real_part, imag_part], axis=1)


def orthonormal(vectors):
    found = []
    for column in range(vectors.shape[1]):
        residue = vectors[:, column, :]
        for earlier in found:
            residue = residue - earlier * jnp.sum(earlier * residue, axis=-1, keepdims=True)
        found.append(
            residue / jnp.sqrt(jnp.sum(residue * residue, axis=-1, keepdims=True) + epsilon)
        )
    return jnp.stack(found, axis=1)


def project_out(gram, chosen, counted, steering, frame_total):
    count, slots = chosen.shape
    directions = steering.shape[0]
    onehot = (
        chosen[:, :, None] == lax.broadcasted_iota(jnp.int32, (count, slots, directions), 2)
    ).astype(jnp.float32)
    live = (lax.broadcasted_iota(jnp.int32, (count, slots), 1) < counted[:, None]).astype(
        jnp.float32
    )
    vectors = jnp.einsum("crn,na->cra", onehot, steering, precision=highest) * live[:, :, None]
    basis = orthonormal(vectors)
    left = jnp.einsum("cra,csab->csrb", basis, gram, precision=highest)
    right = jnp.einsum("csab,crb->csar", gram, basis, precision=highest)
    core = jnp.einsum("csrb,ctb->csrt", left, basis, precision=highest)
    inner = jnp.einsum("csrt,ctb->csrb", core, basis, precision=highest)
    suppressed_output = gram - jnp.einsum("cra,csrb->csab", basis, left, precision=highest)
    suppressed_output = suppressed_output - jnp.einsum(
        "csar,crb->csab", right, basis, precision=highest
    )
    suppressed_output = suppressed_output + jnp.einsum(
        "cra,csrb->csab", basis, inner, precision=highest
    )
    return suppressed_output / frame_total


def per_device(samples, taps, steering, interferer_ids, ranks):
    spectra = channelize(samples, taps)
    antennas, layers, channels, frames = spectra.shape
    groups = lax.axis_size("chan")
    spectra = spectra.reshape(antennas, layers, groups, channels // groups, frames)
    grams = partial_gram(lax.all_to_all(spectra, "chan", split_axis=2, concat_axis=0, tiled=True))
    owned = lax.psum_scatter(grams, "tm", scatter_dimension=0, tiled=True)
    frame_total = frames * lax.axis_size("tm")
    return project_out(owned, interferer_ids, ranks, steering, frame_total)


def solution(mesh):
    in_specs = (P("chan", "tm"), P(), P(), P(("chan", "tm"), None), P(("chan", "tm")))
    out_specs = P(("chan", "tm"), None, None, None)
    return jax.shard_map(
        per_device, mesh=mesh, in_specs=in_specs, out_specs=out_specs, check_vma=False
    )
```

profile of v0, /device:TPU:0, one launch (start us, length us, event | category | flops | bytes accessed | tf_op | source)
XLA Modules:
  0.0 506.4 jit_solution(18265749781006836214)
XLA Ops:
  6.5 0.0 copy-start
  6.5 0.0 reduce-scatter.5.cloned.1.call-start
  6.5 1.3 slice.160
  7.8 2.4 collective-permute-start
  10.2 0.1 fusion.73
  10.4 2.3 fusion.116
  12.7 0.0 collective-permute-done
  12.7 32.6 %multiply_add_fusion.1 = f32[8,64,4096]{2,0,1:T(8,128)S(1)} fusion(bf16[8,64,4096]{2,0,1:T(8,128)(2,1)} %bitcast.185, bf16[8,15,4096]{2,0,1:T(8,128)(2,1)S(1)} %collective-permute-done, f32[4096]{0:T(1024)S(1)} %bitcast.200, f32[4096]{0:T(1024)S(1)} %bitcast.201, f32[4096]{0:T(1024)S(1)} %bitcast.187, f32[4096]{0:T(1024)S(1)} %bitcast.188, ...), kind=kLoop, calls=%fused_computation.31 | loop fusion | flops 130023424 | bytes 13828096 | tf_op jit(solution)/shard_map/add | solution.py:36
  45.4 8.3 %copy.38 = f32[8,64,4096]{2,1,0:T(8,128)} copy(f32[8,64,4096]{2,0,1:T(8,128)S(1)} %multiply_add_fusion.1) | data formatting | bytes 16777216 | tf_op jit(solution)/shard_map/add | solution.py:36
  53.6 14.2 %reshape.249 = f32[8,64,64,64]{3,2,1,0:T(8,128)} reshape(f32[8,64,4096]{2,1,0:T(8,128)} %copy.38) | data formatting | bytes 16777216 | tf_op jit(solution)/shard_map/reshape | solution.py:40
  67.8 0.0 copy-start.1
  67.8 32.0 %fusion.51 = f32[8,64,64,64]{3,2,1,0:T(8,128)} fusion(f32[8,64,64,64]{3,2,1,0:T(8,128)} %reshape.249), kind=kOutput, calls=%fused_computation.99 | convolution fusion | flops 1610670080 | bytes 16777216 | tf_op jit(solution)/shard_map/afpq,pk->afqk/dot_general | solution.py:42
  99.8 0.0 copy-done.1
  99.8 29.3 %fusion.49 = f32[8,64,64,64]{3,2,1,0:T(8,128)} fusion(f32[8,64,64,64]{3,2,1,0:T(8,128)S(1)} %copy-done.1), kind=kOutput, calls=%fused_computation.97 | convolution fusion | flops 1610670080 | bytes 16777216 | tf_op jit(solution)/shard_map/afpq,pk->afqk/dot_general | solution.py:43
  129.1 19.7 %fusion.6 = f32[32,8,64,64]{3,0,2,1:T(8,128)} fusion(f32[8,64,64,64]{3,2,1,0:T(8,128)} %fusion.51, f32[8,64,64,64]{3,2,1,0:T(8,128)} %fusion.49, f32[64,64]{1,0:T(8,128)S(1)} %get-tuple-element.36, f32[64,64]{1,0:T(8,128)S(1)} %get-tuple-element.37), kind=kOutput, calls=%fused_computation.32 | convolution fusion | flops 813723648 | bytes 21004288 | tf_op jit(solution)/shard_map/afqk,qm->amkf/dot_general | solution.py:51
  148.8 19.5 %fusion.7 = f32[32,8,64,64]{3,0,2,1:T(8,128)} fusion(f32[8,64,64,64]{3,2,1,0:T(8,128)} %fusion.51, f32[8,64,64,64]{3,2,1,0:T(8,128)} %fusion.49, f32[64,64]{1,0:T(8,128)S(1)} %get-tuple-element.36, f32[64,64]{1,0:T(8,128)S(1)} %get-tuple-element.37), kind=kOutput, calls=%fused_computation.33 | convolution fusion | flops 813723648 | bytes 21004288 | tf_op jit(solution)/shard_map/afqk,qm->amkf/dot_general | solution.py:48
  168.3 20.3 %fusion.11 = bf16[8,32,64,64]{2,1,3,0:T(8,128)(2,1)} fusion(f32[32,8,64,64]{3,0,2,1:T(8,128)} %fusion.6, f32[8,64,64,64]{3,2,1,0:T(8,128)} %fusion.51, f32[8,64,64,64]{3,2,1,0:T(8,128)} %fusion.49, f32[64,64]{1,0:T(8,128)S(1)} %get-tuple-element.36, f32[64,64]{1,0:T(8,128)S(1)} %get-tuple-element.37), kind=kOutput, calls=%fused_computation.37 | convolution fusion | flops 815820800 | bytes 23101440 | tf_op jit(solution)/shard_map/afqk,qm->amkf/dot_general | solution.py:50
  188.6 5.0 stack.22
  193.6 1.9 copy.42
  195.5 20.1 %fusion.10 = bf16[8,32,64,64]{2,1,3,0:T(8,128)(2,1)} fusion(f32[32,8,64,64]{3,0,2,1:T(8,128)} %fusion.7, f32[8,64,64,64]{3,2,1,0:T(8,128)} %fusion.51, f32[8,64,64,64]{3,2,1,0:T(8,128)} %fusion.49, f32[64,64]{1,0:T(8,128)S(1)} %get-tuple-element.36, f32[64,64]{1,0:T(8,128)S(1)} %get-tuple-element.37), kind=kOutput, calls=%fused_computation.36 | convolution fusion | flops 815820800 | bytes 23101440 | tf_op jit(solution)/shard_map/afqk,qm->amkf/dot_general | solution.py:49
  215.6 5.0 stack.10
  220.7 0.6 copy.41
  221.2 2.0 pad_maximum_fusion.2
  223.3 102.0 %all_to_all.15 = bf16[8,2,16,128,64]{3,4,1,0,2:T(8,128)(2,1)} all-to-all(bf16[8,2,16,128,64]{3,4,1,0,2:T(8,128)(2,1)S(1)} %pad_maximum_fusion.2), channel_id=1, replica_groups=mesh['chan'=16,'tm'=2] {'chan'}, dimensions={2} | all-to-all | bytes 8388608 | tf_op jit(solution)/shard_map/all_to_all | solution.py:106
  325.2 7.3 %copy.66 = bf16[128,2,128,64,1]{0,3,4,1,2:T(8,128)(2,1)} copy(bf16[128,2,128,64,1]{2,3,1,0,4:T(8,128)(2,1)} %bitcast.181) | data formatting | bytes 8388608 | tf_op jit(solution)/shard_map/squeeze | solution.py:57
  332.5 7.4 %copy.67 = bf16[128,2,128,64,1]{0,3,1,4,2:T(8,128)(2,1)} copy(bf16[128,2,128,64,1]{2,3,1,0,4:T(8,128)(2,1)} %bitcast.182) | data formatting | bytes 8388608 | tf_op jit(solution)/shard_map/squeeze | solution.py:57
  340.0 19.1 %convolution_bitcast_fusion = f32[128,2,128,2,128]{2,4,1,3,0:T(8,128)} fusion(bf16[128,2,128,64,1]{0,3,4,1,2:T(8,128)(2,1)} %copy.66, bf16[128,2,128,64,1]{0,3,1,4,2:T(8,128)(2,1)} %copy.67), kind=kOutput, calls=%fused_computation.18 | convolution fusion | flops 1073741824 | bytes 41943040 | tf_op jit(solution)/shard_map/arcf,bscf->crasb/dot_general | solution.py:58
  359.0 11.9 %fusion = f32[128,1,128,128]{2,3,0,1:T(8,128)} fusion(f32[128,2,128,2,128]{2,4,1,3,0:T(8,128)} %convolution_bitcast_fusion), kind=kLoop, calls=%fused_computation.20 | loop fusion | flops 2097152 | bytes 25165824 | tf_op jit(solution)/shard_map/sub | solution.py:60
  370.9 11.7 %fusion.2 = f32[128,1,128,128]{2,3,0,1:T(8,128)} fusion(f32[128,2,128,2,128]{2,4,1,3,0:T(8,128)} %convolution_bitcast_fusion), kind=kLoop, calls=%fused_computation.23 | loop fusion | flops 2097152 | bytes 25165824 | tf_op jit(solution)/shard_map/add | solution.py:59
  382.6 6.5 %pad_maximum_fusion = f32[128,2,128,128]{2,3,0,1:T(8,128)S(1)} fusion(f32[128,1,128,128]{2,3,0,1:T(8,128)} %fusion, f32[128,1,128,128]{2,3,0,1:T(8,128)} %fusion.2), kind=kLoop, calls=%fused_computation.15 | loop fusion | flops 4194304 | bytes 33554432 | tf_op jit(solution)/shard_map/stack | solution.py:61
  389.2 1.6 copy.89
  390.8 11.9 %copy.131 = f32[16,8,256,128]{3,1,2,0:T(8,128)} copy(f32[16,8,256,128]{3,2,1,0:T(8,128)S(1)} %bitcast.180) | data formatting | bytes 33554432
  402.7 0.0 copy-start.3
  402.7 0.0 copy-start.2
  402.7 0.0 reduce-scatter.5.cloned.1.call-update
  402.7 0.6 copy-done.3
  403.4 0.0 copy-done
  403.4 0.0 copy-done.2
  403.4 0.3 convolution_multiply_fusion
  403.7 0.1 fusion.56
  403.8 0.2 fusion.55
  404.0 0.2 fusion.53
  404.2 0.2 multiply_reduce_fusion.2
  404.5 0.2 multiply_reduce_fusion.3
  404.7 0.2 multiply_reduce_fusion.1
  404.9 0.2 multiply_reduce_fusion
  405.1 0.2 subtract_divide_fusion
  405.3 22.2 %reduce-scatter.5.cloned.1.call-done = f32[64,32768]{1,0:T(8,128)} async-done(((f32[128,32768]{1,0:T(8,128)}), f32[64,32768]{1,0:T(8,128)}) %reduce-scatter.5.cloned.1.call-update) | async-done | bytes 8388624
  427.5 4.9 copy.94
  432.3 7.2 %convolution_bitcast_fusion.1 = f32[64,2,4,128]{3,2,1,0:T(4,128)S(1)} fusion(f32[64,4,128,1]{2,0,1,3:T(8,128)S(1)} %get-tuple-element.35, f32[64,2,128,128]{3,2,1,0:T(8,128)S(1)} %bitcast.176), kind=kOutput, calls=%fused_computation.66 | convolution fusion | flops 100663296 | bytes 8781824 | tf_op jit(solution)/shard_map/cra,csab->csrb/dot_general | solution.py:87
  439.5 4.7 fusion.38
  444.2 0.6 fusion.36
  444.9 15.0 %fusion.29 = f32[64,2,128,128]{3,2,0,1:T(8,128)S(1)} fusion(f32[64,2,4,128]{3,2,1,0:T(4,128)S(1)} %convolution_bitcast_fusion.1, f32[64,4,128]{2,0,1:T(8,128)S(1)} %get-tuple-element.34), kind=kOutput, calls=%fused_computation.71 | convolution fusion | flops 100663296 | bytes 8781824 | tf_op jit(solution)/shard_map/cra,csrb->csab/dot_general | solution.py:91
  459.9 0.7 fusion.26
  460.5 16.8 %fusion.31 = f32[64,2,128,128]{3,2,0,1:T(8,128)} fusion(f32[64,2,4,128]{3,2,0,1:T(4,128)S(1)} %fusion.26, f32[64,4,128]{2,0,1:T(8,128)S(1)} %get-tuple-element.34), kind=kOutput, calls=%fused_computation.74 | convolution fusion | flops 100663296 | bytes 8781824 | tf_op jit(solution)/shard_map/cra,csrb->csab/dot_general | solution.py:95
  477.3 13.0 %fusion.5 = f32[64,2,128,128]{2,3,0,1:T(8,128)} fusion(f32[64,2,128,128]{2,3,1,0:T(8,128)S(1)} %bitcast.178, f32[64,2,128,128]{3,2,0,1:T(8,128)} %fusion.31, f32[64,2,128,128]{3,2,0,1:T(8,128)S(1)} %fusion.29, f32[64,2,128,4]{2,3,1,0:T(4,128)S(1)} %fusion.38, f32[64,4,128]{2,0,1:T(8,128)S(1)} %get-tuple-element.34), kind=kOutput, calls=%fused_computation.28 | convolution fusion | flops 109051904 | bytes 33947648 | tf_op jit(solution)/shard_map/csar,crb->csab/dot_general | solution.py:92
  490.3 9.0 %copy.59 = f32[64,2,128,128]{3,2,1,0:T(8,128)} copy(f32[64,2,128,128]{2,3,0,1:T(8,128)} %fusion.5) | data formatting | bytes 16777216 | tf_op jit(solution)/shard_map/div | solution.py:98
  (6 shorter events, 0.1 us)
Async XLA Ops:
  6.5 396.8 %copy-start = (f32[8,128]{1,0:T(8,128)S(1)}, f32[8,128]{1,0:T(8,128)}, u32[]{:S(2)}) copy-start(f32[8,128]{1,0:T(8,128)} %param.7) | copy-start | bytes 12292
  6.5 420.9 %reduce-scatter.5.cloned.1.call-start = ((), (), s32[]{:S(2)}) async-start(), calls=%async_computation.2 | async-start | bytes 25165824
  7.8 4.9 collective-permute-start
  67.8 32.0 %copy-start.1 = (f32[8,64,64,64]{3,2,1,0:T(8,128)S(1)}, f32[8,64,64,64]{3,2,1,0:T(8,128)}, u32[]{:S(2)}) copy-start(f32[8,64,64,64]{3,2,1,0:T(8,128)} %reshape.249) | copy-start | bytes 25165828
  402.7 0.7 copy-start.3
  402.7 0.7 copy-start.2
Sparse Core Ops, SparseCore 0:
  402.9 24.5 reduce-scatter.4
where the time goes:
time: 514 us; the launch traced here: 506 us
  matrix products  218 us (42%)
  blocking collectives  102 us (20%)
  local copies, waits for them, and re-layouts  81.3 us (16%)
  other arithmetic  66.5 us (13%)
  waiting for transfers between devices  22.2 us (4%)
  between operations  13.8 us (3%)
    all_to_all x1, blocking collectives, per_device(): lax.all_to_all(spectra, 'chan', split_axis=2, concat_axis=0, tiled=True)  102 us
    add x1, other arithmetic, channelize(): filtered + taps[tap_index] * padded[:, tap_index:tap_index + frames, :].a...  32.6 us
    dot_general x1, matrix products, channelize(): jnp.einsum('afpq,pk->afqk', shaped, first_cos, precision=highest)  32 us
    dot_general x1, matrix products, channelize(): jnp.einsum('afpq,pk->afqk', shaped, first_sin, precision=highest)  29.3 us
    unnamed x2, waiting for transfers between devices  22.2 us
    dot_general x1, matrix products, channelize(): jnp.einsum('afqk,qm->amkf', turned_imag, second_cos, precision=highest)  20.3 us
    dot_general x1, matrix products, channelize(): jnp.einsum('afqk,qm->amkf', turned_imag, second_sin, precision=highest)  20.1 us
    dot_general x1, matrix products, channelize(): jnp.einsum('afqk,qm->amkf', turned_real, second_sin, precision=highest)  19.7 us
  transfers between devices with their start and end apart: 2, of which 1 were waited for; matrix products, arithmetic and copies ran while one was open for 1% of the time, Pallas kernels for 0%

commit v1 on v0

v1 whole, which is shorter than its diff:
```python
import functools
import math

import jax
import jax.numpy as jnp
import ml_dtypes
import numpy as np
from jax import lax
from jax.experimental import pallas as pl
from jax.experimental.pallas import tpu as pltpu
from jax.sharding import PartitionSpec as P

lanes = 128
octet = 8
frame_block = 16
epsilon = 1e-06
highest = lax.Precision.HIGHEST
f32 = jnp.float32
bf16 = jnp.bfloat16
vmem_bytes = 56 * 1024 * 1024


def real_transform(x):
    size = len(x)
    if size == 2:
        return [(x[0] + x[1], None), (x[0] - x[1], None)]
    even = real_transform(x[0::2])
    odd = real_transform(x[1::2])
    half = size // 2
    bins = [None] * (half + 1)
    bins[0] = (even[0][0] + odd[0][0], None)
    bins[half] = (even[0][0] - odd[0][0], None)
    bins[half // 2] = (even[half // 2][0], -odd[half // 2][0])
    for k in range(1, half // 2):
        er, ei = even[k]
        o_r, oi = odd[k]
        c = math.cos(2 * math.pi * k / size)
        s = math.sin(2 * math.pi * k / size)
        if 4 * k == half:
            tr = (o_r + oi) * c
            ti = (oi - o_r) * c
        else:
            tr = o_r * c + oi * s
            ti = oi * c - o_r * s
        bins[k] = (er + tr, ei + ti)
        bins[half - k] = (er - tr, ti - ei)
    return bins


def split_two(x):
    high = x.astype(bf16)
    low = (x - high.astype(f32)).astype(bf16)
    return high, low


def split_three(x):
    high = x.astype(bf16).astype(f32)
    rest = x - high
    middle = rest.astype(bf16).astype(f32)
    return high, middle, rest - middle


def filter_kernel(length, before_ref, block_ref, taps_ref, *rest):
    high_ref, low_ref, filtered, sections = rest[-4:]
    tap_count = taps_ref.shape[0]
    radix = length // lanes

    @pl.loop(0, radix)
    def _(part):
        spot = pl.multiple_of(part * lanes, lanes)
        taps = [
            jnp.broadcast_to(taps_ref[pl.ds(t, 1), pl.ds(spot, lanes)], (octet, lanes))
            for t in range(tap_count)
        ]

        def sample(frame):
            ref = block_ref if frame >= 0 else before_ref
            place = pl.multiple_of(spot + frame % frame_block * length, lanes)
            return ref[:, pl.ds(place, lanes)].astype(f32)

        window = [sample(frame) for frame in range(1 - tap_count, 0)]
        for frame in range(frame_block):
            window.append(sample(frame))
            total = taps[0] * window[0]
            for t in range(1, tap_count):
                total = total + taps[t] * window[t]
            filtered[part, frame] = total
            window.pop(0)

    @pl.loop(0, frame_block)
    def _(frame):
        bins = real_transform([filtered[part, frame] for part in range(radix)])
        rows = pl.ds(frame, octet, stride=frame_block)
        sections[0, rows, :] = bins[0][0]
        sections[1, rows, :] = bins[radix // 2][0]
        for k in range(1, radix // 2):
            sections[2 * k, rows, :] = bins[k][0]
            sections[2 * k + 1, rows, :] = bins[k][1]

    def parts_of(group):
        shape = (octet, frame_block, lanes)
        real = sections[2 * group].reshape(shape)
        imag = sections[2 * group + 1].reshape(shape)
        return split_two(real), split_two(imag)

    reals, imags = parts_of(0)
    for ref, real, imag in zip((high_ref, low_ref), reals, imags):
        for turn in range(2):
            ref[0, :, turn, :, :lanes] = real
            ref[0, :, turn, :, lanes:] = imag

    @pl.loop(1, radix // 2)
    def _(group):
        reals, imags = parts_of(group)
        for ref, real, imag in zip((high_ref, low_ref), reals, imags):
            ref[group, :, 0, :, :lanes] = real
            ref[group, :, 0, :, lanes:] = imag
            ref[group, :, 1, :, :lanes] = imag
            ref[group, :, 1, :, lanes:] = -real


def filter_sections(before, samples, taps, first, steps, previous=None):
    length = taps.shape[1]
    frames = samples.shape[1] // length
    groups = length // lanes // 2
    width = frame_block * length
    shape = jax.ShapeDtypeStruct((groups, octet, 2, frames, 2 * lanes), bf16)
    block = pl.BlockSpec(
        (groups, octet, 2, frame_block, 2 * lanes), lambda i: (0, 0, 0, i + first, 0)
    )
    in_specs = [
        pl.BlockSpec((octet, width), lambda i: (0, i)),
        pl.BlockSpec((octet, width), lambda i: (0, i + first)),
        pl.BlockSpec(taps.shape, lambda i: (0, 0)),
    ]
    operands = [before, samples, taps]
    aliases = {}
    if previous is not None:
        in_specs += [pl.BlockSpec(memory_space=pl.ANY)] * 2
        operands += previous
        aliases = {3: 0, 4: 1}
    return pl.pallas_call(
        functools.partial(filter_kernel, length),
        grid=(steps,),
        in_specs=in_specs,
        out_specs=[block, block],
        out_shape=[shape, shape],
        scratch_shapes=[
            pltpu.VMEM((length // lanes, frame_block, octet, lanes), f32),
            pltpu.VMEM((length // lanes, frame_block * octet, lanes), f32),
        ],
        input_output_aliases=aliases,
        compiler_params=pltpu.CompilerParams(vmem_limit_bytes=vmem_bytes),
        cost_estimate=pl.CostEstimate(
            flops=steps * 80_000_000, bytes_accessed=steps * 6_000_000, transcendentals=0
        ),
        name="filter_sections",
    )(*operands)


def phase_tables(length):
    radix = length // lanes
    kept = lanes // 2
    q = np.arange(lanes)
    m = np.arange(kept)

    def angles(k):
        return 2 * np.pi * ((np.outer(k + radix * m, q)) % length) / length

    zero = np.zeros((kept, lanes))
    first, middle = angles(0), angles(radix // 2)
    tables = [np.block([[np.cos(first), zero], [zero, np.cos(middle)]])]
    for k in range(1, radix // 2):
        one, other = angles(k), angles(radix - k)
        tables.append(np.block([[np.cos(one), np.sin(one)], [np.cos(other), -np.sin(other)]]))
    tables.append(np.block([[-np.sin(first), zero], [zero, -np.sin(middle)]]))
    tables = np.stack(tables).astype(np.float32)
    high = tables.astype(ml_dtypes.bfloat16)
    low = (tables - high.astype(np.float32)).astype(ml_dtypes.bfloat16)
    return high, low


def contract_last(left, right):
    return lax.dot_general(left, right, (((1,), (1,)), ((), ())), preferred_element_type=f32)


def channel_kernel(
    with_zero, high_ref, low_ref, mh_ref, ml_ref, ih_ref, il_ref, out_ref, turned
):
    frames = high_ref.shape[3]
    kept = mh_ref.shape[1] // 2
    lane = lax.broadcasted_iota(jnp.int32, (1, lanes), 1)
    imaginary = lane >= frames

    def product(a, table_high, table_low):
        rows = (2 * lanes, 2 * lanes)
        high = high_ref[0, 2 * a : 2 * a + 2].reshape(rows)
        low = low_ref[0, 2 * a : 2 * a + 2].reshape(rows)
        total = contract_last(table_high, high) + contract_last(table_high, low)
        return total + contract_last(table_low, high)

    def body(zero):
        flip = jnp.where(imaginary, -1.0, 1.0)
        for a in range(octet // 2):
            total = product(a, mh_ref[0], ml_ref[0])
            if zero:
                other = product(a, ih_ref[0], il_ref[0])
            for side in range(2):
                piece = total[:, side * lanes : (side + 1) * lanes]
                if zero:
                    piece = jnp.where(imaginary, other[:, side * lanes : (side + 1) * lanes], piece)
                    lower = piece[kept:]
                else:
                    lower = piece[kept:] * flip
                turned[0, pl.ds(2 * a + side, kept, stride=octet), :] = piece[:kept]
                turned[1, pl.ds(2 * a + side, kept, stride=octet), :] = lower
        for half in range(2):
            out_ref[:, half] = turned[half].reshape(kept, octet, lanes).astype(bf16)

    if with_zero:
        step = pl.program_id(0)

        @pl.when(step == 0)
        def _():
            body(True)

        @pl.when(step != 0)
        def _():
            body(False)
    else:
        body(False)


def channels_of(sections, tables, first, count):
    high, low = sections
    groups, _, _, frames, _ = high.shape
    kept = tables[0].shape[1] // 2
    section = pl.BlockSpec((1, octet, 2, frames, 2 * lanes), lambda i: (i + first, 0, 0, 0, 0))
    table = pl.BlockSpec((1, 2 * kept, 2 * lanes), lambda i: (i + first, 0, 0))
    extra = pl.BlockSpec((1, 2 * kept, 2 * lanes), lambda i: (groups, 0, 0))
    return pl.pallas_call(
        functools.partial(channel_kernel, first == 0),
        grid=(count,),
        in_specs=[section, section, table, table, extra, extra],
        out_specs=pl.BlockSpec((kept, 2, octet, lanes), lambda i: (0, i, 0, 0)),
        out_shape=jax.ShapeDtypeStruct((kept, 2 * count, octet, lanes), bf16),
        scratch_shapes=[pltpu.VMEM((2, kept * octet, lanes), f32)],
        compiler_params=pltpu.CompilerParams(vmem_limit_bytes=vmem_bytes),
        cost_estimate=pl.CostEstimate(
            flops=count * 400_000_000, bytes_accessed=count * 1_500_000, transcendentals=0
        ),
        name="channels_of",
    )(high, low, *tables, *tables)


def covariance_kernel(place, scale, x_ref, q_ref, *rest):
    out_ref, ready, done = rest[-3:]
    step = pl.program_id(0)
    steps = pl.num_programs(0)
    slot = lax.rem(step, 2)
    octets, shards, count = x_ref.shape[:3]
    antennas = octets * octet
    half = lanes // 2
    sign = jnp.where(lax.broadcasted_iota(jnp.int32, (1, lanes), 1) < half, 1.0, -1.0)

    def copies(at, which):
        return [
            pltpu.make_async_copy(
                ready.at[which, j], out_ref.at[place(at * count + j)], done.at[which, j]
            )
            for j in range(count)
        ]

    @pl.when(step >= 2)
    def _():
        for copy in copies(step - 2, slot):
            copy.wait()

    for j in range(count):
        pieces = [x_ref[:, t, j].astype(f32).reshape(antennas, lanes) for t in range(shards)]
        x = jnp.concatenate(pieces, axis=1)
        q = q_ref[place(step * count + j)]
        qh, qm, ql = split_three(q)
        left = jnp.concatenate([qh, qm, ql, jnp.zeros_like(q)], axis=0).astype(bf16)
        z = jnp.dot(left, x.astype(bf16), preferred_element_type=f32)
        z = z[:octet] + z[octet : 2 * octet] + z[2 * octet : 3 * octet]
        zh, zm, zl = split_three(z)
        left = jnp.concatenate([qh, qh, qm, qm, qh, ql], axis=0).astype(bf16)
        right = jnp.concatenate([zh, zm, zh, zm, zl, zh], axis=0).astype(bf16)
        y = x - lax.dot_general(left, right, (((0,), (0,)), ((), ())), preferred_element_type=f32)
        high, low = split_two(y)

        def turned(v):
            v = v.astype(f32)
            parts = [
                pltpu.roll(v[:, t * lanes : (t + 1) * lanes], half, 1) * sign for t in range(shards)
            ]
            return jnp.concatenate(parts, axis=1).astype(bf16)

        both = contract_last(
            jnp.concatenate([high, turned(high)], axis=0), jnp.concatenate([high, low], axis=0)
        )
        rest_ = contract_last(jnp.concatenate([low, turned(low)], axis=0), high)
        total = (both[:, :antennas] + (both[:, antennas:] + rest_)) * scale
        ready[slot, j] = total.reshape(2, antennas, antennas)

    for copy in copies(step, slot):
        copy.start()

    @pl.when(step == steps - 1)
    def _():
        @pl.when(step >= 1)
        def _():
            for copy in copies(step - 1, 1 - slot):
                copy.wait()

        for copy in copies(step, slot):
            copy.wait()


def covariances(received, basis, place, frame_total, total, previous):
    octets, shards, channels = received.shape[:3]
    antennas = octets * octet
    count = math.gcd(channels, 4)
    in_specs = [
        pl.BlockSpec((octets, shards, count, octet, lanes), lambda i: (0, 0, i, 0, 0)),
        pl.BlockSpec(basis.shape, lambda i: (0, 0, 0)),
    ]
    operands = [received, basis]
    aliases = {}
    if previous is not None:
        in_specs.append(pl.BlockSpec(memory_space=pl.ANY))
        operands.append(previous)
        aliases = {2: 0}
    return pl.pallas_call(
        functools.partial(covariance_kernel, place, 1.0 / frame_total),
        grid=(channels // count,),
        in_specs=in_specs,
        out_specs=pl.BlockSpec(memory_space=pl.ANY),
        out_shape=jax.ShapeDtypeStruct((total, 2, antennas, antennas), f32),
        scratch_shapes=[
            pltpu.VMEM((2, count, 2, antennas, antennas), f32),
            pltpu.SemaphoreType.DMA((2, count)),
        ],
        input_output_aliases=aliases,
        compiler_params=pltpu.CompilerParams(vmem_limit_bytes=vmem_bytes),
        cost_estimate=pl.CostEstimate(
            flops=channels * 60_000_000, bytes_accessed=channels * 250_000, transcendentals=0
        ),
        name="covariances",
    )(*operands)


def orthonormal(vectors):
    found = []
    for column in range(vectors.shape[1]):
        residue = vectors[:, column, :]
        for earlier in found:
            residue = residue - earlier * jnp.sum(earlier * residue, axis=-1, keepdims=True)
        found.append(
            residue / jnp.sqrt(jnp.sum(residue * residue, axis=-1, keepdims=True) + epsilon)
        )
    return jnp.stack(found, axis=1)


def basis_of(chosen, counted, steering):
    count, slots = chosen.shape
    directions = steering.shape[0]
    onehot = (
        chosen[:, :, None] == lax.broadcasted_iota(jnp.int32, (count, slots, directions), 2)
    ).astype(f32)
    live = (lax.broadcasted_iota(jnp.int32, (count, slots), 1) < counted[:, None]).astype(f32)
    vectors = jnp.einsum("crn,na->cra", onehot, steering, precision=highest) * live[:, :, None]
    basis = orthonormal(vectors)
    return jnp.pad(basis, ((0, 0), (0, octet - slots), (0, 0)))


def per_device(samples, taps, steering, interferer_ids, ranks):
    antennas, width = samples.shape
    length = taps.shape[1]
    frames = width // length
    radix = length // lanes
    groups = radix // 2
    kept = lanes // 2
    shards = lax.axis_size("tm")
    spread = lax.axis_size("chan")
    devices = spread * shards
    owned = interferer_ids.shape[0]
    frame_total = frames * shards

    padded = samples
    if antennas < octet:
        padded = jnp.pad(samples, ((0, octet - antennas), (0, 0)))
    edge = lax.ppermute(
        padded[:, width - frame_block * length :],
        "tm",
        [(i, i + 1) for i in range(shards - 1)],
    )
    steps = frames // frame_block
    sections = filter_sections(padded, padded, taps, 1, steps - 1)
    sections = filter_sections(edge, padded, taps, 0, 1, sections)
    tables = [jnp.asarray(table) for table in phase_tables(length)]
    basis = basis_of(interferer_ids, ranks, steering)

    whole_runs = owned % radix == 0
    cuts = chunk_counts if whole_runs else (groups,)
    first = 0
    out = None
    for count in cuts:
        spectra = channels_of(sections, tables, first, count)
        bins = [
            k
            for g in range(first, first + count)
            for k in (g, radix - g if g else groups)
        ]
        runs = owned // radix
        if whole_runs:
            spectra = spectra.reshape(devices, runs * 2 * count, octet, lanes)

            def place(index, first=first, count=count):
                run = index // (2 * count)
                column = index - run * (2 * count)
                group = first + column // 2
                mirrored = jnp.where(group == 0, groups, radix - group)
                return run * radix + jnp.where(column % 2 == 0, group, mirrored)
        else:
            spectra = spectra[:, np.argsort(bins)].reshape(devices, owned, octet, lanes)

            def place(index):
                return index
        if antennas < octet:
            spectra = spectra[:, :, :antennas]
        received = lax.all_to_all(spectra, ("chan", "tm"), split_axis=0, concat_axis=0, tiled=True)
        channels = received.shape[1]
        received = received.reshape(spread, shards, channels, antennas, lanes)
        if antennas < octet:
            received = received.transpose(1, 2, 0, 3, 4).reshape(
                shards, channels, spread * antennas // octet, octet, lanes
            ).transpose(2, 0, 1, 3, 4)
        out = covariances(received, basis, place, frame_total, owned, out)
        first += count
    return out


chunk_counts = (2, 4, 5, 4, 1)


def solution(mesh):
    in_specs = (P("chan", "tm"), P(), P(), P(("chan", "tm"), None), P(("chan", "tm")))
    out_specs = P(("chan", "tm"), None, None, None)
    return jax.shard_map(
        per_device, mesh=mesh, in_specs=in_specs, out_specs=out_specs, check_vma=False
    )
```

time: 514 us -> 196 us (0.38); the launches traced: 506 us -> 195 us
  matrix products: 218 us -> 0.29 us
  blocking collectives: 102 us -> 0 us
  Pallas kernels: 0 us -> 88.3 us
  local copies, waits for them, and re-layouts: 81.3 us -> 3.16 us
  other arithmetic: 66.5 us -> 2.94 us
  waiting for transfers between devices: 22.2 us -> 77.5 us
  starting transfers between devices: 2.42 us -> 23 us
  between operations: 13.8 us -> 0.23 us
    dot_general x15 -> x1, matrix products: 218 us -> 0.29 us  [basis_of(): jnp.einsum('crn,na->cra', onehot, steering, precision=highest)]
    all_to_all x1 -> x0, blocking collectives: 102 us -> none  [per_device(): lax.all_to_all(spectra, 'chan', split_axis=2, concat_axis=0, tiled=True)]
    pallas_call x0 -> x12, Pallas kernels: none -> 88.3 us  [the longest x5 36.7 us: covariances(): pl.pallas_call(functools.partial(covariance_kernel, place, 1.0 / frame_to...]
    all_to_all x0 -> x5, waiting for transfers between devices: none -> 77.5 us  [per_device(): lax.all_to_all(spectra, ('chan', 'tm'), split_axis=0, concat_axis=0, tile...]
    add x2 -> x0, other arithmetic: 44.3 us -> none  [the longest x1 32.6 us: channelize(): filtered + taps[tap_index] * padded[:, tap_index:tap_index + frames, :].a...]
    unnamed x2 -> x0, waiting for transfers between devices: 22.2 us -> none
    all_to_all x0 -> x5, starting transfers between devices: none -> 20.6 us  [per_device(): lax.all_to_all(spectra, ('chan', 'tm'), split_axis=0, concat_axis=0, tile...]
    unnamed x11 -> x18, local copies, waits for them, and re-layouts: 19 us -> 1.78 us
  transfers between devices with their start and end apart: 2 -> 6, of which waited for: 1 -> 4; matrix products, arithmetic and copies ran while one was open for 1% -> 2% of each run, Pallas kernels for 0% -> 37%
where the time goes in v1:
time: 196 us; the launch traced here: 195 us
  Pallas kernels  88.3 us (45%)
  waiting for transfers between devices  77.5 us (40%)
  starting transfers between devices  23 us (12%)
  local copies, waits for them, and re-layouts  3.16 us (2%)
  other arithmetic  2.94 us (2%)
    all_to_all x5, waiting for transfers between devices, per_device(): lax.all_to_all(spectra, ('chan', 'tm'), split_axis=0, concat_axis=0, tile...  77.5 us
    pallas_call x5, Pallas kernels, covariances(): pl.pallas_call(functools.partial(covariance_kernel, place, 1.0 / frame_to...  36.7 us
    pallas_call x2, Pallas kernels, filter_sections(): pl.pallas_call(functools.partial(filter_kernel, length), grid=(steps,), i...  26.9 us
    pallas_call x5, Pallas kernels, channels_of(): pl.pallas_call(functools.partial(channel_kernel, first == 0), grid=(count...  24.7 us
    all_to_all x5, starting transfers between devices, per_device(): lax.all_to_all(spectra, ('chan', 'tm'), split_axis=0, concat_axis=0, tile...  20.6 us
  transfers between devices with their start and end apart: 6, of which 4 were waited for; matrix products, arithmetic and copies ran while one was open for 2% of the time, Pallas kernels for 37%

profile of v1, /device:TPU:0, one launch (start us, length us, event | category | flops | bytes accessed | tf_op | source)
XLA Modules:
  0.0 195.4 jit_solution(8650558602309893909)
XLA Ops:
  0.0 0.0 copy-start
  0.0 1.3 slice.15
  1.3 2.4 %collective-permute-start = (bf16[8,65536]{1,0:T(8,128)(2,1)S(1)}, bf16[8,65536]{1,0:T(8,128)(2,1)S(1)}, u32[]{:S(2)}, u32[]{:S(2)}) collective-permute-start(bf16[8,65536]{1,0:T(8,128)(2,1)S(1)} %slice.15), channel_id=1, source_target_pairs={{0,1},{2,3},{4,5},{6,7},{8,9},{10,11},{12,13},{14,15},{16,17},{18,... | collective-permute-start | bytes 3145736 | tf_op jit(solution)/shard_map/ppermute | solution.py:394
  3.7 18.4 %filter_sections.2 = (bf16[16,8,2,64,256]{4,3,2,1,0:T(8,128)(2,1)}, bf16[16,8,2,64,256]{4,3,2,1,0:T(8,128)(2,1)}) custom-call(bf16[8,262144]{1,0:T(8,128)(2,1)} %block_ref.3, bf16[8,262144]{1,0:T(8,128)(2,1)} %block_ref.3, f32[16,4096]{1,0:T(8,128)} %taps_ref.3), custom_call_target="tpu_custom_call" | custom-call | flops 240000000 | bytes 18000000 | tf_op jit(solution)/shard_map/filter_sections/pallas_call | solution.py:142
  22.1 0.0 collective-permute-done.before_ref
  22.1 0.0 copy-start.6
  22.1 1.1 copy-done.6
  23.2 8.5 %filter_sections.3 = (bf16[16,8,2,64,256]{4,3,2,1,0:T(8,128)(2,1)}, bf16[16,8,2,64,256]{4,3,2,1,0:T(8,128)(2,1)}) custom-call(bf16[8,65536]{1,0:T(8,128)(2,1)} %copy-done.6, bf16[8,262144]{1,0:T(8,128)(2,1)} %block_ref.3, f32[16,4096]{1,0:T(8,128)} %taps_ref.3, ...), custom_call_target="tpu_custom_call", output_to_operand_aliasing={{0}: (3, {}), {1}: (4, {})} | custom-call | flops 80000000 | bytes 6000000 | tf_op jit(solution)/shard_map/filter_sections/pallas_call | solution.py:142
  31.7 4.0 %channels_of.9 = bf16[64,4,8,128]{3,2,1,0:T(8,128)(2,1)} custom-call(bf16[16,8,2,64,256]{4,3,2,1,0:T(8,128)(2,1)} %get-tuple-element.11.high_ref, bf16[16,8,2,64,256]{4,3,2,1,0:T(8,128)(2,1)} %get-tuple-element.12.low_ref, bf16[17,128,256]{2,1,0:T(8,128)(2,1)} %constant.10.clone.mh_ref.ih_ref, bf16[17,128,256]{2,1,0:T(8,128)(2,1)} %constant.11.clone.ml_ref.il_ref, ...), custom_call_target="tpu_custom_call" | custom-call | flops 800000000 | bytes 3000000 | tf_op jit(solution)/shard_map/channels_of/pallas_call | solution.py:241
  35.6 6.7 %all-to-all-start.4 = ((bf16[32,8,8,128]{3,2,1,0:T(8,128)(2,1)}), bf16[32,8,8,128]{3,2,1,0:T(8,128)(2,1)S(1)}, u32[]{:S(2)}, u32[]{:S(2)}) async-start(bf16[32,8,8,128]{3,2,1,0:T(8,128)(2,1)} %bitcast.77), calls=%async_computation.4 | async-start | bytes 1048576 | tf_op jit(solution)/shard_map/all_to_all | solution.py:433
  42.3 5.6 %channels_of.6 = bf16[64,8,8,128]{3,2,1,0:T(8,128)(2,1)} custom-call(bf16[16,8,2,64,256]{4,3,2,1,0:T(8,128)(2,1)} %get-tuple-element.11.high_ref, bf16[16,8,2,64,256]{4,3,2,1,0:T(8,128)(2,1)} %get-tuple-element.12.low_ref, bf16[17,128,256]{2,1,0:T(8,128)(2,1)} %constant.10.clone.mh_ref.ih_ref, bf16[17,128,256]{2,1,0:T(8,128)(2,1)} %constant.11.clone.ml_ref.il_ref, ...), custom_call_target="tpu_custom_call" | custom-call | flops 1600000000 | bytes 6000000 | tf_op jit(solution)/shard_map/channels_of/pallas_call | solution.py:241
  48.0 9.9 %all-to-all-done.4 = bf16[32,8,8,128]{3,2,1,0:T(8,128)(2,1)S(1)} async-done(((bf16[32,8,8,128]{3,2,1,0:T(8,128)(2,1)}), bf16[32,8,8,128]{3,2,1,0:T(8,128)(2,1)S(1)}, u32[]{:S(2)}, u32[]{:S(2)}) %all-to-all-start.4) | async-done | bytes 524320 | tf_op jit(solution)/shard_map/all_to_all | solution.py:433
  57.9 0.0 copy-start.4
  57.9 3.1 %all-to-all-start.1 = ((bf16[32,16,8,128]{3,2,1,0:T(8,128)(2,1)}), bf16[32,16,8,128]{3,2,1,0:T(8,128)(2,1)S(1)}, u32[]{:S(2)}, u32[]{:S(2)}) async-start(bf16[32,16,8,128]{3,2,1,0:T(8,128)(2,1)} %bitcast.74), calls=%async_computation.1 | async-start | bytes 2097152 | tf_op jit(solution)/shard_map/all_to_all | solution.py:433
  61.0 5.6 %channels_of.8 = bf16[64,8,8,128]{3,2,1,0:T(8,128)(2,1)} custom-call(bf16[16,8,2,64,256]{4,3,2,1,0:T(8,128)(2,1)} %get-tuple-element.11.high_ref, bf16[16,8,2,64,256]{4,3,2,1,0:T(8,128)(2,1)} %get-tuple-element.12.low_ref, bf16[17,128,256]{2,1,0:T(8,128)(2,1)} %constant.10.clone.mh_ref.ih_ref, bf16[17,128,256]{2,1,0:T(8,128)(2,1)} %constant.11.clone.ml_ref.il_ref, ...), custom_call_target="tpu_custom_call" | custom-call | flops 1600000000 | bytes 6000000 | tf_op jit(solution)/shard_map/channels_of/pallas_call | solution.py:241
  66.6 0.0 copy-done.4
  66.6 20.6 %all-to-all-done.1 = bf16[32,16,8,128]{3,2,1,0:T(8,128)(2,1)S(1)} async-done(((bf16[32,16,8,128]{3,2,1,0:T(8,128)(2,1)}), bf16[32,16,8,128]{3,2,1,0:T(8,128)(2,1)S(1)}, u32[]{:S(2)}, u32[]{:S(2)}) %all-to-all-start.1) | async-done | bytes 1048608 | tf_op jit(solution)/shard_map/all_to_all | solution.py:433
  87.2 0.0 copy-start.2
  87.2 3.6 %all-to-all-start.3 = ((bf16[32,16,8,128]{3,2,1,0:T(8,128)(2,1)}), bf16[32,16,8,128]{3,2,1,0:T(8,128)(2,1)S(1)}, u32[]{:S(2)}, u32[]{:S(2)}) async-start(bf16[32,16,8,128]{3,2,1,0:T(8,128)(2,1)} %bitcast.75), calls=%async_computation.3 | async-start | bytes 2097152 | tf_op jit(solution)/shard_map/all_to_all | solution.py:433
  90.8 0.0 copy-start.8
  90.8 0.0 copy-start.7
  90.9 6.8 %channels_of.7 = bf16[64,10,8,128]{3,2,1,0:T(8,128)(2,1)} custom-call(bf16[16,8,2,64,256]{4,3,2,1,0:T(8,128)(2,1)} %get-tuple-element.11.high_ref, bf16[16,8,2,64,256]{4,3,2,1,0:T(8,128)(2,1)} %get-tuple-element.12.low_ref, bf16[17,128,256]{2,1,0:T(8,128)(2,1)} %constant.10.clone.mh_ref.ih_ref, bf16[17,128,256]{2,1,0:T(8,128)(2,1)} %constant.11.clone.ml_ref.il_ref, ...), custom_call_target="tpu_custom_call" | custom-call | flops 2000000000 | bytes 7500000 | tf_op jit(solution)/shard_map/channels_of/pallas_call | solution.py:241
  97.7 0.0 copy-done.2
  97.7 19.4 %all-to-all-done.3 = bf16[32,16,8,128]{3,2,1,0:T(8,128)(2,1)S(1)} async-done(((bf16[32,16,8,128]{3,2,1,0:T(8,128)(2,1)}), bf16[32,16,8,128]{3,2,1,0:T(8,128)(2,1)S(1)}, u32[]{:S(2)}, u32[]{:S(2)}) %all-to-all-start.3) | async-done | bytes 1048608 | tf_op jit(solution)/shard_map/all_to_all | solution.py:433
  117.1 0.0 copy-start.3
  117.1 3.6 %all-to-all-start.2 = ((bf16[32,20,8,128]{3,2,1,0:T(8,128)(2,1)}), bf16[32,20,8,128]{3,2,1,0:T(8,128)(2,1)S(1)}, u32[]{:S(2)}, u32[]{:S(2)}) async-start(bf16[32,20,8,128]{3,2,1,0:T(8,128)(2,1)} %bitcast.71), calls=%async_computation.2 | async-start | bytes 2621440 | tf_op jit(solution)/shard_map/all_to_all | solution.py:433
  120.7 0.0 copy-done.8
  120.7 0.0 copy-done
  120.7 0.0 copy-done.7
  120.7 0.3 convolution_multiply_fusion
  121.1 0.1 fusion.3
  121.2 0.1 div.54
  121.2 0.1 div.55
  121.3 0.2 fusion.2
  121.5 0.2 fusion
  121.7 0.2 fusion.1
  121.9 0.2 multiply_reduce_fusion.2
  122.1 0.2 multiply_reduce_fusion.1
  122.3 0.2 multiply_reduce_fusion
  122.5 0.1 multiply_subtract_fusion.2
  122.6 2.6 %channels_of.5 = bf16[64,2,8,128]{3,2,1,0:T(8,128)(2,1)} custom-call(bf16[16,8,2,64,256]{4,3,2,1,0:T(8,128)(2,1)} %get-tuple-element.11.high_ref, bf16[16,8,2,64,256]{4,3,2,1,0:T(8,128)(2,1)} %get-tuple-element.12.low_ref, bf16[17,128,256]{2,1,0:T(8,128)(2,1)} %constant.10.clone.mh_ref.ih_ref, bf16[17,128,256]{2,1,0:T(8,128)(2,1)} %constant.11.clone.ml_ref.il_ref, ...), custom_call_target="tpu_custom_call" | custom-call | flops 400000000 | bytes 1500000 | tf_op jit(solution)/shard_map/channels_of/pallas_call | solution.py:241
  125.3 0.0 copy-done.3
  125.3 27.6 %all-to-all-done.2 = bf16[32,20,8,128]{3,2,1,0:T(8,128)(2,1)S(1)} async-done(((bf16[32,20,8,128]{3,2,1,0:T(8,128)(2,1)}), bf16[32,20,8,128]{3,2,1,0:T(8,128)(2,1)S(1)}, u32[]{:S(2)}, u32[]{:S(2)}) %all-to-all-start.2) | async-done | bytes 1310752 | tf_op jit(solution)/shard_map/all_to_all | solution.py:433
  152.8 0.0 copy-start.1
  152.8 3.6 %all-to-all-start = ((bf16[32,4,8,128]{3,2,1,0:T(8,128)(2,1)}), bf16[32,4,8,128]{3,2,1,0:T(8,128)(2,1)S(1)}, u32[]{:S(2)}, u32[]{:S(2)}) async-start(bf16[32,4,8,128]{3,2,1,0:T(8,128)(2,1)} %bitcast.78), calls=%async_computation | async-start | bytes 524288 | tf_op jit(solution)/shard_map/all_to_all | solution.py:433
  156.4 0.6 subtract_divide_fusion
  157.0 0.9 select_maximum_fusion.q_ref
  157.9 5.3 %covariances.5.rest_0_ = f32[64,2,128,128]{3,2,1,0:T(8,128)} custom-call(bf16[16,2,8,8,128]{4,3,2,1,0:T(8,128)(2,1)} %bitcast.76, f32[64,8,128]{2,1,0:T(8,128)} %select_maximum_fusion.q_ref), custom_call_target="tpu_custom_call" | custom-call | flops 480000000 | bytes 2000000 | tf_op jit(solution)/shard_map/covariances/pallas_call | solution.py:335
  163.2 8.7 %covariances.6.rest_0_ = f32[64,2,128,128]{3,2,1,0:T(8,128)} custom-call(bf16[16,2,16,8,128]{4,3,2,1,0:T(8,128)(2,1)} %bitcast.73, f32[64,8,128]{2,1,0:T(8,128)} %select_maximum_fusion.q_ref, f32[64,2,128,128]{3,2,1,0:T(8,128)} %covariances.5.rest_0_), custom_call_target="tpu_custom_call", output_to_operand_aliasing={{}: (2, {})} | custom-call | flops 960000000 | bytes 4000000 | tf_op jit(solution)/shard_map/covariances/pallas_call | solution.py:335
  171.9 0.0 copy-done.1
  171.9 10.4 %covariances.7.rest_0_ = f32[64,2,128,128]{3,2,1,0:T(8,128)} custom-call(bf16[16,2,20,8,128]{4,3,2,1,0:T(8,128)(2,1)} %bitcast.70, f32[64,8,128]{2,1,0:T(8,128)} %select_maximum_fusion.q_ref, f32[64,2,128,128]{3,2,1,0:T(8,128)} %covariances.6.rest_0_), custom_call_target="tpu_custom_call", output_to_operand_aliasing={{}: (2, {})} | custom-call | flops 1200000000 | bytes 5000000 | tf_op jit(solution)/shard_map/covariances/pallas_call | solution.py:335
  182.4 8.7 %covariances.8.rest_0_ = f32[64,2,128,128]{3,2,1,0:T(8,128)} custom-call(bf16[16,2,16,8,128]{4,3,2,1,0:T(8,128)(2,1)} %bitcast.72, f32[64,8,128]{2,1,0:T(8,128)} %select_maximum_fusion.q_ref, f32[64,2,128,128]{3,2,1,0:T(8,128)} %covariances.7.rest_0_), custom_call_target="tpu_custom_call", output_to_operand_aliasing={{}: (2, {})} | custom-call | flops 960000000 | bytes 4000000 | tf_op jit(solution)/shard_map/covariances/pallas_call | solution.py:335
  191.1 0.0 all-to-all-done
  191.1 0.0 copy-start.5
  191.1 0.7 copy-done.5
  191.8 3.6 %covariances.9 = f32[64,2,128,128]{3,2,1,0:T(8,128)} custom-call(bf16[16,2,4,8,128]{4,3,2,1,0:T(8,128)(2,1)} %bitcast.79, f32[64,8,128]{2,1,0:T(8,128)} %select_maximum_fusion.q_ref, f32[64,2,128,128]{3,2,1,0:T(8,128)} %covariances.8.rest_0_), custom_call_target="tpu_custom_call", output_to_operand_aliasing={{}: (2, {})} | custom-call | flops 240000000 | bytes 1000000 | tf_op jit(solution)/shard_map/covariances/pallas_call | solution.py:335
  (6 shorter events, 0.0 us)
Async XLA Ops:
  0.0 120.7 %copy-start = (f32[8,128]{1,0:T(8,128)S(1)}, f32[8,128]{1,0:T(8,128)}, u32[]{:S(2)}) copy-start(f32[8,128]{1,0:T(8,128)} %param.9) | copy-start | bytes 12292
  1.3 20.8 %collective-permute-start = (bf16[8,65536]{1,0:T(8,128)(2,1)S(1)}, bf16[8,65536]{1,0:T(8,128)(2,1)S(1)}, u32[]{:S(2)}, u32[]{:S(2)}) collective-permute-start(bf16[8,65536]{1,0:T(8,128)(2,1)S(1)} %slice.15), channel_id=1, source_target_pairs={{0,1},{2,3},{4,5},{6,7},{8,9},{10,11},{12,13},{14,15},{16,17},{18,... | collective-permute-start | bytes 3145736 | tf_op jit(solution)/shard_map/ppermute | solution.py:394
  22.1 1.1 copy-start.6
  35.6 22.2 %all-to-all-start.4 = ((bf16[32,8,8,128]{3,2,1,0:T(8,128)(2,1)}), bf16[32,8,8,128]{3,2,1,0:T(8,128)(2,1)S(1)}, u32[]{:S(2)}, u32[]{:S(2)}) async-start(bf16[32,8,8,128]{3,2,1,0:T(8,128)(2,1)} %bitcast.77), calls=%async_computation.4 | async-start | bytes 1048576 | tf_op jit(solution)/shard_map/all_to_all | solution.py:433
  57.9 8.7 %copy-start.4 = (bf16[32,8,8,128]{3,2,1,0:T(8,128)(2,1)}, bf16[32,8,8,128]{3,2,1,0:T(8,128)(2,1)S(1)}, u32[]{:S(2)}) copy-start(bf16[32,8,8,128]{3,2,1,0:T(8,128)(2,1)S(1)} %all-to-all-done.4) | copy-start | bytes 1572868
  57.9 29.3 %all-to-all-start.1 = ((bf16[32,16,8,128]{3,2,1,0:T(8,128)(2,1)}), bf16[32,16,8,128]{3,2,1,0:T(8,128)(2,1)S(1)}, u32[]{:S(2)}, u32[]{:S(2)}) async-start(bf16[32,16,8,128]{3,2,1,0:T(8,128)(2,1)} %bitcast.74), calls=%async_computation.1 | async-start | bytes 2097152 | tf_op jit(solution)/shard_map/all_to_all | solution.py:433
  87.2 10.5 %copy-start.2 = (bf16[32,16,8,128]{3,2,1,0:T(8,128)(2,1)}, bf16[32,16,8,128]{3,2,1,0:T(8,128)(2,1)S(1)}, u32[]{:S(2)}) copy-start(bf16[32,16,8,128]{3,2,1,0:T(8,128)(2,1)S(1)} %all-to-all-done.1) | copy-start | bytes 3145732
  87.2 29.9 %all-to-all-start.3 = ((bf16[32,16,8,128]{3,2,1,0:T(8,128)(2,1)}), bf16[32,16,8,128]{3,2,1,0:T(8,128)(2,1)S(1)}, u32[]{:S(2)}, u32[]{:S(2)}) async-start(bf16[32,16,8,128]{3,2,1,0:T(8,128)(2,1)} %bitcast.75), calls=%async_computation.3 | async-start | bytes 2097152 | tf_op jit(solution)/shard_map/all_to_all | solution.py:433
  90.8 29.9 %copy-start.8 = (s32[64]{0:T(128)S(1)}, s32[64]{0:T(128)}, u32[]{:S(2)}) copy-start(s32[64]{0:T(128)} %param.11) | copy-start | bytes 772
  90.8 29.9 %copy-start.7 = (s32[64,4]{0,1:T(4,128)S(1)}, s32[64,4]{0,1:T(4,128)}, u32[]{:S(2)}) copy-start(s32[64,4]{0,1:T(4,128)} %param.10) | copy-start | bytes 3076
  117.1 8.2 %copy-start.3 = (bf16[32,16,8,128]{3,2,1,0:T(8,128)(2,1)}, bf16[32,16,8,128]{3,2,1,0:T(8,128)(2,1)S(1)}, u32[]{:S(2)}) copy-start(bf16[32,16,8,128]{3,2,1,0:T(8,128)(2,1)S(1)} %all-to-all-done.3) | copy-start | bytes 3145732
  117.1 35.8 %all-to-all-start.2 = ((bf16[32,20,8,128]{3,2,1,0:T(8,128)(2,1)}), bf16[32,20,8,128]{3,2,1,0:T(8,128)(2,1)S(1)}, u32[]{:S(2)}, u32[]{:S(2)}) async-start(bf16[32,20,8,128]{3,2,1,0:T(8,128)(2,1)} %bitcast.71), calls=%async_computation.2 | async-start | bytes 2621440 | tf_op jit(solution)/shard_map/all_to_all | solution.py:433
  152.8 19.1 %copy-start.1 = (bf16[32,20,8,128]{3,2,1,0:T(8,128)(2,1)}, bf16[32,20,8,128]{3,2,1,0:T(8,128)(2,1)S(1)}, u32[]{:S(2)}) copy-start(bf16[32,20,8,128]{3,2,1,0:T(8,128)(2,1)S(1)} %all-to-all-done.2) | copy-start | bytes 3932164
  152.8 38.3 %all-to-all-start = ((bf16[32,4,8,128]{3,2,1,0:T(8,128)(2,1)}), bf16[32,4,8,128]{3,2,1,0:T(8,128)(2,1)S(1)}, u32[]{:S(2)}, u32[]{:S(2)}) async-start(bf16[32,4,8,128]{3,2,1,0:T(8,128)(2,1)} %bitcast.78), calls=%async_computation | async-start | bytes 524288 | tf_op jit(solution)/shard_map/all_to_all | solution.py:433
  191.1 0.7 copy-start.5

commit v2 on v1

--- a/solution.py
+++ b/solution.py
@@ -84,39 +84,25 @@
             total = taps[0] * window[0]
             for t in range(1, tap_count):
                 total = total + taps[t] * window[t]
-            filtered[part, frame] = total
+            filtered[part, frame * octet : (frame + 1) * octet, :] = total
             window.pop(0)
 
-    @pl.loop(0, frame_block)
-    def _(frame):
-        bins = real_transform([filtered[part, frame] for part in range(radix)])
-        rows = pl.ds(frame, octet, stride=frame_block)
-        sections[0, rows, :] = bins[0][0]
-        sections[1, rows, :] = bins[radix // 2][0]
-        for k in range(1, radix // 2):
-            sections[2 * k, rows, :] = bins[k][0]
-            sections[2 * k + 1, rows, :] = bins[k][1]
-
-    def parts_of(group):
-        shape = (octet, frame_block, lanes)
-        real = sections[2 * group].reshape(shape)
-        imag = sections[2 * group + 1].reshape(shape)
-        return split_two(real), split_two(imag)
-
-    reals, imags = parts_of(0)
-    for ref, real, imag in zip((high_ref, low_ref), reals, imags):
-        for turn in range(2):
-            ref[0, :, turn, :, :lanes] = real
-            ref[0, :, turn, :, lanes:] = imag
-
-    @pl.loop(1, radix // 2)
-    def _(group):
-        reals, imags = parts_of(group)
-        for ref, real, imag in zip((high_ref, low_ref), reals, imags):
-            ref[group, :, 0, :, :lanes] = real
-            ref[group, :, 0, :, lanes:] = imag
-            ref[group, :, 1, :, :lanes] = imag
-            ref[group, :, 1, :, lanes:] = -real
+    @pl.loop(0, octet)
+    def _(antenna):
+        for half in range(frame_block // octet):
+            rows = pl.ds(half * octet * octet + antenna, octet, stride=octet)
+            bins = real_transform([filtered[part, rows, :] for part in range(radix)])
+            kept = pl.ds(half * octet, octet)
+            sections[0, kept, :] = bins[0][0]
+            sections[1, kept, :] = bins[radix // 2][0]
+            for k in range(1, radix // 2):
+                sections[2 * k, kept, :] = bins[k][0]
+                sections[2 * k + 1, kept, :] = bins[k][1]
+        for group in range(radix // 2):
+            for side in range(2):
+                high, low = split_two(sections[2 * group + side])
+                high_ref[group, antenna, :, side * lanes : (side + 1) * lanes] = high
+                low_ref[group, antenna, :, side * lanes : (side + 1) * lanes] = low
 
 
 def filter_sections(before, samples, taps, first, steps, previous=None):
@@ -124,9 +110,9 @@
     frames = samples.shape[1] // length
     groups = length // lanes // 2
     width = frame_block * length
-    shape = jax.ShapeDtypeStruct((groups, octet, 2, frames, 2 * lanes), bf16)
+    shape = jax.ShapeDtypeStruct((groups, octet, frames, 2 * lanes), bf16)
     block = pl.BlockSpec(
-        (groups, octet, 2, frame_block, 2 * lanes), lambda i: (0, 0, 0, i + first, 0)
+        (groups, octet, frame_block, 2 * lanes), lambda i: (0, 0, i + first, 0)
     )
     in_specs = [
         pl.BlockSpec((octet, width), lambda i: (0, i)),
@@ -146,8 +132,8 @@
         out_specs=[block, block],
         out_shape=[shape, shape],
         scratch_shapes=[
-            pltpu.VMEM((length // lanes, frame_block, octet, lanes), f32),
             pltpu.VMEM((length // lanes, frame_block * octet, lanes), f32),
+            pltpu.VMEM((length // lanes, frame_block, lanes), f32),
         ],
         input_output_aliases=aliases,
         compiler_params=pltpu.CompilerParams(vmem_limit_bytes=vmem_bytes),
@@ -164,16 +150,16 @@
     q = np.arange(lanes)
     m = np.arange(kept)
 
-    def angles(k):
-        return 2 * np.pi * ((np.outer(k + radix * m, q)) % length) / length
-
-    zero = np.zeros((kept, lanes))
-    first, middle = angles(0), angles(radix // 2)
-    tables = [np.block([[np.cos(first), zero], [zero, np.cos(middle)]])]
+    def waves(k):
+        angle = 2 * np.pi * (np.outer(q, k + radix * m) % length) / length
+        return np.cos(angle), np.sin(angle)
+
+    zero = np.zeros((lanes, kept))
+    (c, s), (oc, os) = waves(0), waves(radix // 2)
+    tables = [np.block([[c, zero, -s, zero], [zero, oc, zero, -os]])]
     for k in range(1, radix // 2):
-        one, other = angles(k), angles(radix - k)
-        tables.append(np.block([[np.cos(one), np.sin(one)], [np.cos(other), -np.sin(other)]]))
-    tables.append(np.block([[-np.sin(first), zero], [zero, -np.sin(middle)]]))
+        (c, s), (oc, os) = waves(k), waves(radix - k)
+        tables.append(np.block([[c, oc, -s, -os], [s, -os, c, -oc]]))
     tables = np.stack(tables).astype(np.float32)
     high = tables.astype(ml_dtypes.bfloat16)
     low = (tables - high.astype(np.float32)).astype(ml_dtypes.bfloat16)
@@ -184,73 +170,42 @@
     return lax.dot_general(left, right, (((1,), (1,)), ((), ())), preferred_element_type=f32)
 
 
-def channel_kernel(
-    with_zero, high_ref, low_ref, mh_ref, ml_ref, ih_ref, il_ref, out_ref, turned
-):
-    frames = high_ref.shape[3]
-    kept = mh_ref.shape[1] // 2
-    lane = lax.broadcasted_iota(jnp.int32, (1, lanes), 1)
-    imaginary = lane >= frames
-
-    def product(a, table_high, table_low):
-        rows = (2 * lanes, 2 * lanes)
-        high = high_ref[0, 2 * a : 2 * a + 2].reshape(rows)
-        low = low_ref[0, 2 * a : 2 * a + 2].reshape(rows)
-        total = contract_last(table_high, high) + contract_last(table_high, low)
-        return total + contract_last(table_low, high)
-
-    def body(zero):
-        flip = jnp.where(imaginary, -1.0, 1.0)
-        for a in range(octet // 2):
-            total = product(a, mh_ref[0], ml_ref[0])
-            if zero:
-                other = product(a, ih_ref[0], il_ref[0])
-            for side in range(2):
-                piece = total[:, side * lanes : (side + 1) * lanes]
-                if zero:
-                    piece = jnp.where(imaginary, other[:, side * lanes : (side + 1) * lanes], piece)
-                    lower = piece[kept:]
-                else:
-                    lower = piece[kept:] * flip
-                turned[0, pl.ds(2 * a + side, kept, stride=octet), :] = piece[:kept]
-                turned[1, pl.ds(2 * a + side, kept, stride=octet), :] = lower
-        for half in range(2):
-            out_ref[:, half] = turned[half].reshape(kept, octet, lanes).astype(bf16)
-
-    if with_zero:
-        step = pl.program_id(0)
-
-        @pl.when(step == 0)
-        def _():
-            body(True)
-
-        @pl.when(step != 0)
-        def _():
-            body(False)
-    else:
-        body(False)
+def channel_kernel(high_ref, low_ref, wh_ref, wl_ref, out_ref, turned):
+    frames = high_ref.shape[2]
+    kept = wh_ref.shape[2] // 4
+    rows = (octet * frames, 2 * lanes)
+    high = high_ref[0].reshape(rows)
+    low = low_ref[0].reshape(rows)
+    dot = functools.partial(jnp.dot, preferred_element_type=f32)
+    total = dot(high, wh_ref[0]) + (dot(low, wh_ref[0]) + dot(high, wl_ref[0]))
+    for a in range(octet):
+        piece = total[a * frames : (a + 1) * frames]
+        piece = jnp.concatenate([piece[:, :lanes], piece[:, lanes:]], axis=0)
+        turned[pl.ds(a, lanes, stride=octet), :] = piece.T
+    for half in range(2):
+        piece = turned[half * kept * octet : (half + 1) * kept * octet]
+        out_ref[:, half] = piece.reshape(kept, octet, lanes).astype(bf16)
 
 
 def channels_of(sections, tables, first, count):
     high, low = sections
-    groups, _, _, frames, _ = high.shape
-    kept = tables[0].shape[1] // 2
-    section = pl.BlockSpec((1, octet, 2, frames, 2 * lanes), lambda i: (i + first, 0, 0, 0, 0))
-    table = pl.BlockSpec((1, 2 * kept, 2 * lanes), lambda i: (i + first, 0, 0))
-    extra = pl.BlockSpec((1, 2 * kept, 2 * lanes), lambda i: (groups, 0, 0))
+    frames = high.shape[2]
+    kept = lanes // 2
+    section = pl.BlockSpec((1, octet, frames, 2 * lanes), lambda i: (i + first, 0, 0, 0))
+    table = pl.BlockSpec((1, 2 * lanes, 2 * lanes), lambda i: (i + first, 0, 0))
     return pl.pallas_call(
-        functools.partial(channel_kernel, first == 0),
+        channel_kernel,
         grid=(count,),
-        in_specs=[section, section, table, table, extra, extra],
+        in_specs=[section, section, table, table],
         out_specs=pl.BlockSpec((kept, 2, octet, lanes), lambda i: (0, i, 0, 0)),
         out_shape=jax.ShapeDtypeStruct((kept, 2 * count, octet, lanes), bf16),
-        scratch_shapes=[pltpu.VMEM((2, kept * octet, lanes), f32)],
+        scratch_shapes=[pltpu.VMEM((lanes * octet, lanes), f32)],
         compiler_params=pltpu.CompilerParams(vmem_limit_bytes=vmem_bytes),
         cost_estimate=pl.CostEstimate(
-            flops=count * 400_000_000, bytes_accessed=count * 1_500_000, transcendentals=0
+            flops=count * 400_000_000, bytes_accessed=count * 1_200_000, transcendentals=0
         ),
         name="channels_of",
-    )(high, low, *tables, *tables)
+    )(high, low, *tables)
 
 
 def covariance_kernel(place, scale, x_ref, q_ref, *rest):
@@ -406,13 +361,14 @@
     cuts = chunk_counts if whole_runs else (groups,)
     first = 0
     out = None
+    waiting = []
+
+    def finish(out):
+        received, place = waiting.pop(0)
+        return covariances(received, basis, place, frame_total, owned, out)
+
     for count in cuts:
         spectra = channels_of(sections, tables, first, count)
-        bins = [
-            k
-            for g in range(first, first + count)
-            for k in (g, radix - g if g else groups)
-        ]
         runs = owned // radix
         if whole_runs:
             spectra = spectra.reshape(devices, runs * 2 * count, octet, lanes)
@@ -424,12 +380,16 @@
                 mirrored = jnp.where(group == 0, groups, radix - group)
                 return run * radix + jnp.where(column % 2 == 0, group, mirrored)
         else:
+            bins = [k for g in range(groups) for k in (g, radix - g if g else groups)]
             spectra = spectra[:, np.argsort(bins)].reshape(devices, owned, octet, lanes)
 
             def place(index):
                 return index
         if antennas < octet:
             spectra = spectra[:, :, :antennas]
+        if len(waiting) == 2:
+            out = finish(out)
+            spectra, out = lax.optimization_barrier((spectra, out))
         received = lax.all_to_all(spectra, ("chan", "tm"), split_axis=0, concat_axis=0, tiled=True)
         channels = received.shape[1]
         received = received.reshape(spread, shards, channels, antennas, lanes)
@@ -437,12 +397,14 @@
             received = received.transpose(1, 2, 0, 3, 4).reshape(
                 shards, channels, spread * antennas // octet, octet, lanes
             ).transpose(2, 0, 1, 3, 4)
-        out = covariances(received, basis, place, frame_total, owned, out)
+        waiting.append((received, place))
         first += count
+    while waiting:
+        out = finish(out)
     return out
 
 
-chunk_counts = (2, 4, 5, 4, 1)
+chunk_counts = (3, 5, 6, 2)
 
 
 def solution(mesh):

time: 196 us -> 162 us (0.83)
  waiting for transfers between devices: 77.5 us -> 57.9 us
  Pallas kernels: 88.3 us -> 76.2 us
  starting transfers between devices: 23 us -> 20.1 us
    all_to_all x5 -> x4, waiting for transfers between devices: 77.5 us -> 57.9 us  [per_device(): lax.all_to_all(spectra, ('chan', 'tm'), split_axis=0, concat_axis=0, tile...]
    pallas_call x5 -> x4, Pallas kernels: 24.7 us -> 19.1 us  [channels_of(): pl.pallas_call(channel_kernel, grid=(count,), in_specs=[section, section,...]
    pallas_call x2, Pallas kernels: 26.9 us -> 22.2 us  [filter_sections(): pl.pallas_call(functools.partial(filter_kernel, length), grid=(steps,), i...]
    all_to_all x5 -> x4, starting transfers between devices: 20.6 us -> 17.6 us  [per_device(): lax.all_to_all(spectra, ('chan', 'tm'), split_axis=0, concat_axis=0, tile...]
    pallas_call x5 -> x4, Pallas kernels: 36.7 us -> 34.9 us  [covariances(): pl.pallas_call(functools.partial(covariance_kernel, place, 1.0 / frame_to...]
  transfers between devices with their start and end apart: 6 -> 5, of which waited for: 4 -> 4; matrix products, arithmetic and copies ran while one was open for 2% -> 2% of each run, Pallas kernels for 37% -> 37%
where the time goes in v2:
time: 162 us; the launch traced here: 161 us
  Pallas kernels  76.2 us (47%)
  waiting for transfers between devices  57.9 us (36%)
  starting transfers between devices  20.1 us (12%)
  local copies, waits for them, and re-layouts  3.16 us (2%)
  other arithmetic  2.91 us (2%)
    all_to_all x4, waiting for transfers between devices, per_device(): lax.all_to_all(spectra, ('chan', 'tm'), split_axis=0, concat_axis=0, tile...  57.9 us
    pallas_call x4, Pallas kernels, covariances(): pl.pallas_call(functools.partial(covariance_kernel, place, 1.0 / frame_to...  34.9 us
    pallas_call x2, Pallas kernels, filter_sections(): pl.pallas_call(functools.partial(filter_kernel, length), grid=(steps,), i...  22.2 us
    pallas_call x4, Pallas kernels, channels_of(): pl.pallas_call(channel_kernel, grid=(count,), in_specs=[section, section,...  19.1 us
    all_to_all x4, starting transfers between devices, per_device(): lax.all_to_all(spectra, ('chan', 'tm'), split_axis=0, concat_axis=0, tile...  17.6 us
  transfers between devices with their start and end apart: 5, of which 4 were waited for; matrix products, arithmetic and copies ran while one was open for 2% of the time, Pallas kernels for 37%

profile of v2, /device:TPU:0, one launch (start us, length us, event | category | flops | bytes accessed | tf_op | source)
XLA Modules:
  0.0 160.7 jit_solution(712999834481115494)
XLA Ops:
  0.0 0.0 copy-start
  0.0 1.3 slice.15
  1.3 2.4 %collective-permute-start = (bf16[8,65536]{1,0:T(8,128)(2,1)S(1)}, bf16[8,65536]{1,0:T(8,128)(2,1)S(1)}, u32[]{:S(2)}, u32[]{:S(2)}) collective-permute-start(bf16[8,65536]{1,0:T(8,128)(2,1)S(1)} %slice.15), channel_id=1, source_target_pairs={{0,1},{2,3},{4,5},{6,7},{8,9},{10,11},{12,13},{14,15},{16,17},{18,... | collective-permute-start | bytes 3145736 | tf_op jit(solution)/shard_map/ppermute | solution.py:349
  3.7 15.2 %filter_sections.2 = (bf16[16,8,64,256]{3,2,1,0:T(8,128)(2,1)}, bf16[16,8,64,256]{3,2,1,0:T(8,128)(2,1)}) custom-call(bf16[8,262144]{1,0:T(8,128)(2,1)} %block_ref.3, bf16[8,262144]{1,0:T(8,128)(2,1)} %block_ref.3, f32[16,4096]{1,0:T(8,128)} %taps_ref.3), custom_call_target="tpu_custom_call" | custom-call | flops 240000000 | bytes 18000000 | tf_op jit(solution)/shard_map/filter_sections/pallas_call | solution.py:128
  19.0 0.0 collective-permute-done.before_ref
  19.0 0.0 copy-start.5
  19.0 1.0 copy-done.5
  19.9 7.0 %filter_sections.3 = (bf16[16,8,64,256]{3,2,1,0:T(8,128)(2,1)}, bf16[16,8,64,256]{3,2,1,0:T(8,128)(2,1)}) custom-call(bf16[8,65536]{1,0:T(8,128)(2,1)} %copy-done.5, bf16[8,262144]{1,0:T(8,128)(2,1)} %block_ref.3, f32[16,4096]{1,0:T(8,128)} %taps_ref.3, ...), custom_call_target="tpu_custom_call", output_to_operand_aliasing={{0}: (3, {}), {1}: (4, {})} | custom-call | flops 80000000 | bytes 6000000 | tf_op jit(solution)/shard_map/filter_sections/pallas_call | solution.py:128
  26.9 0.0 copy-start.7
  26.9 0.0 copy-start.6
  26.9 4.0 %channels_of.7 = bf16[64,6,8,128]{3,2,1,0:T(8,128)(2,1)} custom-call(bf16[16,8,64,256]{3,2,1,0:T(8,128)(2,1)} %get-tuple-element.15.high_ref, bf16[16,8,64,256]{3,2,1,0:T(8,128)(2,1)} %get-tuple-element.16.low_ref, bf16[16,256,256]{2,1,0:T(8,128)(2,1)} %constant.10.clone.wh_ref, bf16[16,256,256]{2,1,0:T(8,128)(2,1)} %constant.11.clone.wl_ref), custom_call_target="tpu_custom_call" | custom-call | flops 1200000000 | bytes 3600000 | tf_op jit(solution)/shard_map/channels_of/pallas_call | solution.py:196
  30.9 6.7 %all-to-all-start.1 = ((bf16[32,12,8,128]{3,2,1,0:T(8,128)(2,1)}), bf16[32,12,8,128]{3,2,1,0:T(8,128)(2,1)S(1)}, u32[]{:S(2)}, u32[]{:S(2)}) async-start(bf16[32,12,8,128]{3,2,1,0:T(8,128)(2,1)} %bitcast.72), calls=%async_computation.1 | async-start | bytes 1572864 | tf_op jit(solution)/shard_map/all_to_all | solution.py:393
  37.6 0.0 copy-done.7
  37.6 0.0 copy-done
  37.6 0.0 copy-done.6
  37.6 0.3 convolution_multiply_fusion
  37.9 0.1 fusion.3
  38.0 5.8 %channels_of.5 = bf16[64,10,8,128]{3,2,1,0:T(8,128)(2,1)} custom-call(bf16[16,8,64,256]{3,2,1,0:T(8,128)(2,1)} %get-tuple-element.15.high_ref, bf16[16,8,64,256]{3,2,1,0:T(8,128)(2,1)} %get-tuple-element.16.low_ref, bf16[16,256,256]{2,1,0:T(8,128)(2,1)} %constant.10.clone.wh_ref, bf16[16,256,256]{2,1,0:T(8,128)(2,1)} %constant.11.clone.wl_ref), custom_call_target="tpu_custom_call" | custom-call | flops 2000000000 | bytes 6000000 | tf_op jit(solution)/shard_map/channels_of/pallas_call | solution.py:196
  43.8 14.4 %all-to-all-done.1 = bf16[32,12,8,128]{3,2,1,0:T(8,128)(2,1)S(1)} async-done(((bf16[32,12,8,128]{3,2,1,0:T(8,128)(2,1)}), bf16[32,12,8,128]{3,2,1,0:T(8,128)(2,1)S(1)}, u32[]{:S(2)}, u32[]{:S(2)}) %all-to-all-start.1) | async-done | bytes 786464 | tf_op jit(solution)/shard_map/all_to_all | solution.py:393
  58.2 0.0 copy-start.3
  58.2 3.6 %all-to-all-start = ((bf16[32,20,8,128]{3,2,1,0:T(8,128)(2,1)}), bf16[32,20,8,128]{3,2,1,0:T(8,128)(2,1)S(1)}, u32[]{:S(2)}, u32[]{:S(2)}) async-start(bf16[32,20,8,128]{3,2,1,0:T(8,128)(2,1)} %bitcast.70), calls=%async_computation | async-start | bytes 2621440 | tf_op jit(solution)/shard_map/all_to_all | solution.py:393
  61.9 0.1 div.54
  62.0 0.2 fusion.2
  62.2 0.2 fusion
  62.4 0.2 fusion.1
  62.6 0.2 multiply_reduce_fusion.2
  62.8 0.2 multiply_reduce_fusion.1
  63.0 0.2 multiply_reduce_fusion
  63.2 0.1 multiply_subtract_fusion.2
  63.3 0.6 subtract_divide_fusion
  63.9 0.8 select_maximum_fusion.q_ref
  64.8 6.5 %channels_of.6 = bf16[64,12,8,128]{3,2,1,0:T(8,128)(2,1)} custom-call(bf16[16,8,64,256]{3,2,1,0:T(8,128)(2,1)} %get-tuple-element.15.high_ref, bf16[16,8,64,256]{3,2,1,0:T(8,128)(2,1)} %get-tuple-element.16.low_ref, bf16[16,256,256]{2,1,0:T(8,128)(2,1)} %constant.10.clone.wh_ref, bf16[16,256,256]{2,1,0:T(8,128)(2,1)} %constant.11.clone.wl_ref), custom_call_target="tpu_custom_call" | custom-call | flops 2400000000 | bytes 7200000 | tf_op jit(solution)/shard_map/channels_of/pallas_call | solution.py:196
  71.2 0.0 copy-done.3
  71.2 7.0 %covariances.4.rest_0_ = f32[64,2,128,128]{3,2,1,0:T(8,128)} custom-call(bf16[16,2,12,8,128]{4,3,2,1,0:T(8,128)(2,1)} %bitcast.71, f32[64,8,128]{2,1,0:T(8,128)} %select_maximum_fusion.q_ref), custom_call_target="tpu_custom_call" | custom-call | flops 720000000 | bytes 3000000 | tf_op jit(solution)/shard_map/covariances/pallas_call | solution.py:290
  78.3 15.7 %all-to-all-done = bf16[32,20,8,128]{3,2,1,0:T(8,128)(2,1)S(1)} async-done(((bf16[32,20,8,128]{3,2,1,0:T(8,128)(2,1)}), bf16[32,20,8,128]{3,2,1,0:T(8,128)(2,1)S(1)}, u32[]{:S(2)}, u32[]{:S(2)}) %all-to-all-start) | async-done | bytes 1310752 | tf_op jit(solution)/shard_map/all_to_all | solution.py:393
  94.0 0.0 copy-start.2
  94.0 3.6 %all-to-all-start.3 = ((bf16[32,24,8,128]{3,2,1,0:T(8,128)(2,1)}), bf16[32,24,8,128]{3,2,1,0:T(8,128)(2,1)S(1)}, u32[]{:S(2)}, u32[]{:S(2)}) async-start(bf16[32,24,8,128]{3,2,1,0:T(8,128)(2,1)} %bitcast.13), calls=%async_computation.3 | async-start | bytes 3145728 | tf_op jit(solution)/shard_map/all_to_all | solution.py:393
  97.6 2.8 %channels_of.4 = bf16[64,4,8,128]{3,2,1,0:T(8,128)(2,1)} custom-call(bf16[16,8,64,256]{3,2,1,0:T(8,128)(2,1)} %get-tuple-element.15.high_ref, bf16[16,8,64,256]{3,2,1,0:T(8,128)(2,1)} %get-tuple-element.16.low_ref, bf16[16,256,256]{2,1,0:T(8,128)(2,1)} %constant.10.clone.wh_ref, bf16[16,256,256]{2,1,0:T(8,128)(2,1)} %constant.11.clone.wl_ref), custom_call_target="tpu_custom_call" | custom-call | flops 800000000 | bytes 2400000 | tf_op jit(solution)/shard_map/channels_of/pallas_call | solution.py:196
  100.4 0.0 copy-done.2
  100.4 10.4 %covariances.5.rest_0_ = f32[64,2,128,128]{3,2,1,0:T(8,128)} custom-call(bf16[16,2,20,8,128]{4,3,2,1,0:T(8,128)(2,1)} %bitcast.69, f32[64,8,128]{2,1,0:T(8,128)} %select_maximum_fusion.q_ref, f32[64,2,128,128]{3,2,1,0:T(8,128)} %covariances.4.rest_0_), custom_call_target="tpu_custom_call", output_to_operand_aliasing={{}: (2, {})} | custom-call | flops 1200000000 | bytes 5000000 | tf_op jit(solution)/shard_map/covariances/pallas_call | solution.py:290
  110.9 24.4 %all-to-all-done.3 = bf16[32,24,8,128]{3,2,1,0:T(8,128)(2,1)S(1)} async-done(((bf16[32,24,8,128]{3,2,1,0:T(8,128)(2,1)}), bf16[32,24,8,128]{3,2,1,0:T(8,128)(2,1)S(1)}, u32[]{:S(2)}, u32[]{:S(2)}) %all-to-all-start.3) | async-done | bytes 1572896 | tf_op jit(solution)/shard_map/all_to_all | solution.py:393
  135.3 0.0 copy-start.1
  135.3 3.8 %all-to-all-start.2 = ((bf16[32,8,8,128]{3,2,1,0:T(8,128)(2,1)}), bf16[32,8,8,128]{3,2,1,0:T(8,128)(2,1)S(1)}, u32[]{:S(2)}, u32[]{:S(2)}) async-start(bf16[32,8,8,128]{3,2,1,0:T(8,128)(2,1)} %bitcast), calls=%async_computation.2 | async-start | bytes 1048576 | tf_op jit(solution)/shard_map/all_to_all | solution.py:393
  139.1 0.0 copy-done.1
  139.1 12.2 %covariances.6.rest_0_ = f32[64,2,128,128]{3,2,1,0:T(8,128)} custom-call(bf16[16,2,24,8,128]{4,3,2,1,0:T(8,128)(2,1)} %bitcast.68, f32[64,8,128]{2,1,0:T(8,128)} %select_maximum_fusion.q_ref, f32[64,2,128,128]{3,2,1,0:T(8,128)} %covariances.5.rest_0_), custom_call_target="tpu_custom_call", output_to_operand_aliasing={{}: (2, {})} | custom-call | flops 1440000000 | bytes 6000000 | tf_op jit(solution)/shard_map/covariances/pallas_call | solution.py:290
  151.3 3.4 %all-to-all-done.2 = bf16[32,8,8,128]{3,2,1,0:T(8,128)(2,1)S(1)} async-done(((bf16[32,8,8,128]{3,2,1,0:T(8,128)(2,1)}), bf16[32,8,8,128]{3,2,1,0:T(8,128)(2,1)S(1)}, u32[]{:S(2)}, u32[]{:S(2)}) %all-to-all-start.2) | async-done | bytes 524320 | tf_op jit(solution)/shard_map/all_to_all | solution.py:393
  154.6 0.0 copy-start.4
  154.6 0.8 copy-done.4
  155.4 5.3 %covariances.7 = f32[64,2,128,128]{3,2,1,0:T(8,128)} custom-call(bf16[16,2,8,8,128]{4,3,2,1,0:T(8,128)(2,1)} %bitcast.73, f32[64,8,128]{2,1,0:T(8,128)} %select_maximum_fusion.q_ref, f32[64,2,128,128]{3,2,1,0:T(8,128)} %covariances.6.rest_0_), custom_call_target="tpu_custom_call", output_to_operand_aliasing={{}: (2, {})} | custom-call | flops 480000000 | bytes 2000000 | tf_op jit(solution)/shard_map/covariances/pallas_call | solution.py:290
  (7 shorter events, 0.1 us)
Async XLA Ops:
  0.0 37.6 %copy-start = (f32[8,128]{1,0:T(8,128)S(1)}, f32[8,128]{1,0:T(8,128)}, u32[]{:S(2)}) copy-start(f32[8,128]{1,0:T(8,128)} %param.9) | copy-start | bytes 12292
  1.3 17.6 %collective-permute-start = (bf16[8,65536]{1,0:T(8,128)(2,1)S(1)}, bf16[8,65536]{1,0:T(8,128)(2,1)S(1)}, u32[]{:S(2)}, u32[]{:S(2)}) collective-permute-start(bf16[8,65536]{1,0:T(8,128)(2,1)S(1)} %slice.15), channel_id=1, source_target_pairs={{0,1},{2,3},{4,5},{6,7},{8,9},{10,11},{12,13},{14,15},{16,17},{18,... | collective-permute-start | bytes 3145736 | tf_op jit(solution)/shard_map/ppermute | solution.py:349
  19.0 1.0 copy-start.5
  26.9 10.7 %copy-start.7 = (s32[64]{0:T(128)S(1)}, s32[64]{0:T(128)}, u32[]{:S(2)}) copy-start(s32[64]{0:T(128)} %param.11) | copy-start | bytes 772
  26.9 10.7 %copy-start.6 = (s32[64,4]{0,1:T(4,128)S(1)}, s32[64,4]{0,1:T(4,128)}, u32[]{:S(2)}) copy-start(s32[64,4]{0,1:T(4,128)} %param.10) | copy-start | bytes 3076
  30.9 27.3 %all-to-all-start.1 = ((bf16[32,12,8,128]{3,2,1,0:T(8,128)(2,1)}), bf16[32,12,8,128]{3,2,1,0:T(8,128)(2,1)S(1)}, u32[]{:S(2)}, u32[]{:S(2)}) async-start(bf16[32,12,8,128]{3,2,1,0:T(8,128)(2,1)} %bitcast.72), calls=%async_computation.1 | async-start | bytes 1572864 | tf_op jit(solution)/shard_map/all_to_all | solution.py:393
  58.2 13.0 %copy-start.3 = (bf16[32,12,8,128]{3,2,1,0:T(8,128)(2,1)}, bf16[32,12,8,128]{3,2,1,0:T(8,128)(2,1)S(1)}, u32[]{:S(2)}) copy-start(bf16[32,12,8,128]{3,2,1,0:T(8,128)(2,1)S(1)} %all-to-all-done.1) | copy-start | bytes 2359300
  58.2 35.8 %all-to-all-start = ((bf16[32,20,8,128]{3,2,1,0:T(8,128)(2,1)}), bf16[32,20,8,128]{3,2,1,0:T(8,128)(2,1)S(1)}, u32[]{:S(2)}, u32[]{:S(2)}) async-start(bf16[32,20,8,128]{3,2,1,0:T(8,128)(2,1)} %bitcast.70), calls=%async_computation | async-start | bytes 2621440 | tf_op jit(solution)/shard_map/all_to_all | solution.py:393
  94.0 6.4 %copy-start.2 = (bf16[32,20,8,128]{3,2,1,0:T(8,128)(2,1)}, bf16[32,20,8,128]{3,2,1,0:T(8,128)(2,1)S(1)}, u32[]{:S(2)}) copy-start(bf16[32,20,8,128]{3,2,1,0:T(8,128)(2,1)S(1)} %all-to-all-done) | copy-start | bytes 3932164
  94.0 41.3 %all-to-all-start.3 = ((bf16[32,24,8,128]{3,2,1,0:T(8,128)(2,1)}), bf16[32,24,8,128]{3,2,1,0:T(8,128)(2,1)S(1)}, u32[]{:S(2)}, u32[]{:S(2)}) async-start(bf16[32,24,8,128]{3,2,1,0:T(8,128)(2,1)} %bitcast.13), calls=%async_computation.3 | async-start | bytes 3145728 | tf_op jit(solution)/shard_map/all_to_all | solution.py:393
  135.3 3.8 %copy-start.1 = (bf16[32,24,8,128]{3,2,1,0:T(8,128)(2,1)}, bf16[32,24,8,128]{3,2,1,0:T(8,128)(2,1)S(1)}, u32[]{:S(2)}) copy-start(bf16[32,24,8,128]{3,2,1,0:T(8,128)(2,1)S(1)} %all-to-all-done.3) | copy-start | bytes 4718596
  135.3 19.3 %all-to-all-start.2 = ((bf16[32,8,8,128]{3,2,1,0:T(8,128)(2,1)}), bf16[32,8,8,128]{3,2,1,0:T(8,128)(2,1)S(1)}, u32[]{:S(2)}, u32[]{:S(2)}) async-start(bf16[32,8,8,128]{3,2,1,0:T(8,128)(2,1)} %bitcast), calls=%async_computation.2 | async-start | bytes 1048576 | tf_op jit(solution)/shard_map/all_to_all | solution.py:393
  154.6 0.8 copy-start.4

commit v3 on v2

v3 whole, which is shorter than its diff:
```python
import functools
import math

import jax
import jax.numpy as jnp
import ml_dtypes
import numpy as np
from jax import lax
from jax.experimental import pallas as pl
from jax.experimental.pallas import tpu as pltpu
from jax.sharding import PartitionSpec as P

lanes = 128
octet = 8
frame_block = 16
epsilon = 1e-06
highest = lax.Precision.HIGHEST
f32 = jnp.float32
bf16 = jnp.bfloat16


def real_transform(x):
    size = len(x)
    if size == 2:
        return [(x[0] + x[1], None), (x[0] - x[1], None)]
    even = real_transform(x[0::2])
    odd = real_transform(x[1::2])
    half = size // 2
    bins = [None] * (half + 1)
    bins[0] = (even[0][0] + odd[0][0], None)
    bins[half] = (even[0][0] - odd[0][0], None)
    bins[half // 2] = (even[half // 2][0], -odd[half // 2][0])
    for k in range(1, half // 2):
        er, ei = even[k]
        o_r, oi = odd[k]
        c = math.cos(2 * math.pi * k / size)
        s = math.sin(2 * math.pi * k / size)
        if 4 * k == half:
            tr = (o_r + oi) * c
            ti = (oi - o_r) * c
        else:
            tr = o_r * c + oi * s
            ti = oi * c - o_r * s
        bins[k] = (er + tr, ei + ti)
        bins[half - k] = (er - tr, ti - ei)
    return bins


def split_two(x):
    high = x.astype(bf16)
    low = (x - high.astype(f32)).astype(bf16)
    return high, low


def split_three(x):
    high = x.astype(bf16).astype(f32)
    rest = x - high
    middle = rest.astype(bf16).astype(f32)
    return high, middle, rest - middle


def filter_frames(length, step, block_ref, taps_ref, high, low, filtered, sections, history):
    tap_count = taps_ref.shape[0]
    radix = length // lanes

    @pl.loop(0, radix)
    def _(part):
        spot = pl.multiple_of(part * lanes, lanes)
        taps = [
            jnp.broadcast_to(taps_ref[pl.ds(t, 1), pl.ds(spot, lanes)], (octet, lanes))
            for t in range(tap_count)
        ]
        window = [history[part, j] for j in range(tap_count - 1)]
        for frame in range(frame_block):
            place = pl.multiple_of(spot + frame * length, lanes)
            window.append(block_ref[:, pl.ds(place, lanes)].astype(f32))
            total = taps[0] * window[0]
            for t in range(1, tap_count):
                total = total + taps[t] * window[t]
            filtered[part, frame * octet : (frame + 1) * octet, :] = total
            window.pop(0)
        for j in range(tap_count - 1):
            history[part, j] = window[j]

    kept = pl.ds(pl.multiple_of(step * frame_block, frame_block), frame_block)

    @pl.loop(0, octet)
    def _(antenna):
        for half in range(frame_block // octet):
            rows = pl.ds(half * octet * octet + antenna, octet, stride=octet)
            bins = real_transform([filtered[part, rows, :] for part in range(radix)])
            here = pl.ds(half * octet, octet)
            sections[0, here, :] = bins[0][0]
            sections[1, here, :] = bins[radix // 2][0]
            for k in range(1, radix // 2):
                sections[2 * k, here, :] = bins[k][0]
                sections[2 * k + 1, here, :] = bins[k][1]
        for group in range(radix // 2):
            for side in range(2):
                first, second = split_two(sections[2 * group + side])
                high[group, antenna, kept, side * lanes : (side + 1) * lanes] = first
                low[group, antenna, kept, side * lanes : (side + 1) * lanes] = second


def second_stage(high, low, wh_ref, wl_ref):
    dot = functools.partial(jnp.dot, preferred_element_type=f32)
    return dot(high, wh_ref[0]) + (dot(low, wh_ref[0]) + dot(high, wl_ref[0]))


def head_kernel(length, steps, count, with_edge, *refs):
    before_ref, block_ref, taps_ref, wh_ref, wl_ref = refs[:5]
    refs = refs[5:]
    high_out, low_out = refs[:2]
    refs = refs[2:]
    if with_edge:
        edge_out, refs = refs[0], refs[1:]
    if count:
        out_ref, refs = refs[0], refs[1:]
    filtered, sections, history, turned, high, low, done = refs
    step = pl.program_id(0)
    frames = high.shape[2]
    radix = length // lanes
    kept = lanes // 2
    copies = [
        pltpu.make_async_copy(high.at[pl.ds(count, radix // 2 - count)], high_out, done.at[0]),
        pltpu.make_async_copy(low.at[pl.ds(count, radix // 2 - count)], low_out, done.at[1]),
    ]
    if with_edge:
        copies.append(pltpu.make_async_copy(block_ref, edge_out, done.at[2]))

    @pl.when(step == 0)
    def _():
        past = history.shape[1]

        @pl.loop(0, radix)
        def _(part):
            for j in range(past):
                place = pl.multiple_of(part * lanes + (frame_block - past + j) * length, lanes)
                history[part, j] = before_ref[:, pl.ds(place, lanes)].astype(f32)

    @pl.when(step < steps)
    def _():
        filter_frames(
            length, step, block_ref, taps_ref, high, low, filtered, sections, history
        )

    @pl.when(step == steps - 1)
    def _():
        for copy in copies:
            copy.start()

    if count:

        @pl.when(step >= steps)
        def _():
            group = step - steps
            rows = (octet * frames, 2 * lanes)
            total = second_stage(
                high[group].reshape(rows), low[group].reshape(rows), wh_ref, wl_ref
            )
            for a in range(octet):
                piece = total[a * frames : (a + 1) * frames]
                piece = jnp.concatenate([piece[:, :lanes], piece[:, lanes:]], axis=0).T
                piece = jnp.concatenate([piece[:kept], piece[kept:]], axis=1)
                turned[pl.ds(a, kept, stride=octet), :] = piece
            out_ref[:, 0] = turned[...].reshape(kept, octet, lanes).astype(bf16)

    @pl.when(step == steps + count - 1)
    def _():
        for copy in copies:
            copy.wait()


def head(before, before_block, samples, taps, tables, first, steps, count, with_edge):
    length = taps.shape[1]
    radix = length // lanes
    groups = radix // 2
    kept = lanes // 2
    frames = steps * frame_block
    width = frame_block * length
    rest = jax.ShapeDtypeStruct((groups - count, octet, frames, 2 * lanes), bf16)
    anywhere = pl.BlockSpec(memory_space=pl.ANY)
    table = pl.BlockSpec((1, 2 * lanes, 2 * lanes), lambda i: (jnp.maximum(i - steps, 0), 0, 0))
    out_shape, out_specs = [rest, rest], [anywhere, anywhere]
    if with_edge:
        out_shape.append(jax.ShapeDtypeStruct((octet, width), bf16))
        out_specs.append(anywhere)
    if count:
        out_shape.append(jax.ShapeDtypeStruct((kept, count, octet, lanes), bf16))
        out_specs.append(
            pl.BlockSpec((kept, 1, octet, lanes), lambda i: (0, jnp.maximum(i - steps, 0), 0, 0))
        )
    return pl.pallas_call(
        functools.partial(head_kernel, length, steps, count, with_edge),
        grid=(steps + count,),
        in_specs=[
            pl.BlockSpec((octet, width), lambda i: (0, before_block)),
            pl.BlockSpec((octet, width), lambda i: (0, first + jnp.minimum(i, steps - 1))),
            pl.BlockSpec(taps.shape, lambda i: (0, 0)),
            table,
            table,
        ],
        out_specs=out_specs,
        out_shape=out_shape,
        scratch_shapes=[
            pltpu.VMEM((radix, frame_block * octet, lanes), f32),
            pltpu.VMEM((radix, frame_block, lanes), f32),
            pltpu.VMEM((radix, taps.shape[0] - 1, octet, lanes), f32),
            pltpu.VMEM((kept * octet, lanes), f32),
            pltpu.VMEM((groups, octet, frames, 2 * lanes), bf16),
            pltpu.VMEM((groups, octet, frames, 2 * lanes), bf16),
            pltpu.SemaphoreType.DMA((3,)),
        ],
        compiler_params=pltpu.CompilerParams(vmem_limit_bytes=head_vmem),
        cost_estimate=pl.CostEstimate(
            flops=steps * 3_000_000_000 + count * 600_000_000,
            bytes_accessed=steps * 3_000_000,
            transcendentals=0,
        ),
        name="head",
    )(before, samples, taps, *tables)


def phase_tables(length):
    radix = length // lanes
    kept = lanes // 2
    q = np.arange(lanes)
    m = np.arange(kept)

    def waves(k):
        angle = 2 * np.pi * (np.outer(q, k + radix * m) % length) / length
        return np.cos(angle), np.sin(angle)

    zero = np.zeros((lanes, kept))
    (c, s), (oc, os) = waves(0), waves(radix // 2)
    tables = [np.block([[c, zero, -s, zero], [zero, oc, zero, -os]])]
    for k in range(1, radix // 2):
        (c, s), (oc, os) = waves(k), waves(radix - k)
        tables.append(np.block([[c, oc, -s, -os], [s, -os, c, -oc]]))
    tables = np.stack(tables).astype(np.float32)
    high = tables.astype(ml_dtypes.bfloat16)
    low = (tables - high.astype(np.float32)).astype(ml_dtypes.bfloat16)
    return high, low


def contract_last(left, right):
    return lax.dot_general(left, right, (((1,), (1,)), ((), ())), preferred_element_type=f32)


def channel_kernel(ha_ref, la_ref, hb_ref, lb_ref, wh_ref, wl_ref, out_ref, turned):
    frames = ha_ref.shape[2]
    kept = lanes // 2
    rows = (octet * frames, 2 * lanes)
    high = jnp.concatenate([ha_ref[0].reshape(rows), hb_ref[0].reshape(rows)], axis=0)
    low = jnp.concatenate([la_ref[0].reshape(rows), lb_ref[0].reshape(rows)], axis=0)
    total = second_stage(high, low, wh_ref, wl_ref)
    for a in range(octet):
        one = total[a * frames : (a + 1) * frames]
        two = total[(octet + a) * frames : (octet + a + 1) * frames]
        piece = [one[:, :lanes], two[:, :lanes], one[:, lanes:], two[:, lanes:]]
        turned[pl.ds(a, lanes, stride=octet), :] = jnp.concatenate(piece, axis=0).T
    for half in range(2):
        piece = turned[half * kept * octet : (half + 1) * kept * octet]
        out_ref[:, half] = piece.reshape(kept, octet, lanes).astype(bf16)


def channels_of(first_half, second_half, tables, skipped, first, count):
    frames = first_half[0].shape[2]
    kept = lanes // 2
    section = pl.BlockSpec((1, octet, frames, 2 * lanes), lambda i: (i + first - skipped, 0, 0, 0))
    table = pl.BlockSpec((1, 2 * lanes, 2 * lanes), lambda i: (i + first, 0, 0))
    return pl.pallas_call(
        channel_kernel,
        grid=(count,),
        in_specs=[section] * 4 + [table] * 2,
        out_specs=pl.BlockSpec((kept, 2, octet, lanes), lambda i: (0, i, 0, 0)),
        out_shape=jax.ShapeDtypeStruct((kept, 2 * count, octet, lanes), bf16),
        scratch_shapes=[pltpu.VMEM((lanes * octet, lanes), f32)],
        compiler_params=pltpu.CompilerParams(vmem_limit_bytes=channel_vmem),
        cost_estimate=pl.CostEstimate(
            flops=count * 800_000_000, bytes_accessed=count * 1_200_000, transcendentals=0
        ),
        name="channels_of",
    )(*first_half, *second_half, *tables)


def swap(one, two, width):
    lane = lax.broadcasted_iota(jnp.int32, (1, lanes), 1)
    even = lax.rem(lane // width, 2) == 0
    return (
        jnp.where(even, one, pltpu.roll(two, width, 1)),
        jnp.where(even, pltpu.roll(one, lanes - width, 1), two),
    )


def covariance_kernel(place, scale, halves, *refs):
    x_refs, q_ref = refs[:halves], refs[halves]
    out_ref, ready, done = refs[-3:]
    step = pl.program_id(0)
    steps = pl.num_programs(0)
    slot = lax.rem(step, 2)
    octets, shards, blocks = x_refs[0].shape[:3]
    antennas = octets * octet
    half = lanes // 2
    count = blocks * halves

    def copies(at, which):
        return [
            pltpu.make_async_copy(
                ready.at[which, j], out_ref.at[place(at * count + j)], done.at[which, j]
            )
            for j in range(count)
        ]

    @pl.when(step >= 2)
    def _():
        for copy in copies(step - 2, slot):
            copy.wait()

    def load(ref, t, j):
        if t >= shards:
            return jnp.zeros((antennas, lanes), f32)
        return ref[:, t, j].astype(f32).reshape(antennas, lanes)

    def channels(j):
        parts = [([], []) for _ in range(halves)]
        for t in range(0, shards, 2):
            if halves == 1:
                real, imag = swap(load(x_refs[0], t, j), load(x_refs[0], t + 1, j), half)
                parts[0][0].append(real)
                parts[0][1].append(imag)
            else:
                a0, a1 = (load(x_refs[0], u, j) for u in (t, t + 1))
                b0, b1 = (load(x_refs[1], u, j) for u in (t, t + 1))
                a0, b0 = swap(a0, b0, half)
                a1, b1 = swap(a1, b1, half)
                for found, pair in zip(parts, ((a0, a1), (b0, b1))):
                    real, imag = swap(*pair, half // 2)
                    found[0].append(real)
                    found[1].append(imag)
        return [jnp.concatenate(real + imag, axis=1) for real, imag in parts]

    def project(x, q):
        qh, qm, ql = split_three(q)
        left = jnp.concatenate([qh, qm, ql, jnp.zeros_like(q)], axis=0).astype(bf16)
        z = jnp.dot(left, x.astype(bf16), preferred_element_type=f32)
        z = z[:octet] + z[octet : 2 * octet] + z[2 * octet : 3 * octet]
        zh, zm, zl = split_three(z)
        left = jnp.concatenate([qh, qh, qm, qm, qh, ql], axis=0).astype(bf16)
        right = jnp.concatenate([zh, zm, zh, zm, zl, zh], axis=0).astype(bf16)
        return x - lax.dot_general(
            left, right, (((0,), (0,)), ((), ())), preferred_element_type=f32
        )

    def turned(v):
        middle = v.shape[1] // 2
        return jnp.concatenate([v[:, middle:], -v[:, :middle]], axis=1)

    for j in range(blocks):
        for h, x in enumerate(channels(j)):
            at = j * halves + h
            high, low = split_two(project(x, q_ref[place(step * count + at)]))
            left = jnp.concatenate([high, turned(high), low, turned(low)], axis=0)
            total = contract_last(left, jnp.concatenate([high, low], axis=0))
            total = total[:, :antennas] + total[:, antennas:]
            total = (total[: 2 * antennas] + total[2 * antennas :]) * scale
            ready[slot, at] = total.reshape(2, antennas, antennas)

    for copy in copies(step, slot):
        copy.start()

    @pl.when(step == steps - 1)
    def _():
        @pl.when(step >= 1)
        def _():
            for copy in copies(step - 1, 1 - slot):
                copy.wait()

        for copy in copies(step, slot):
            copy.wait()


def covariances(received, basis, place, frame_total, total, previous):
    halves = len(received)
    octets, shards, blocks = received[0].shape[:3]
    antennas = octets * octet
    count = math.gcd(blocks, 4 // halves)
    in_specs = [
        pl.BlockSpec((octets, shards, count, octet, lanes), lambda i: (0, 0, i, 0, 0))
    ] * halves
    in_specs.append(pl.BlockSpec(basis.shape, lambda i: (0, 0, 0)))
    operands = [*received, basis]
    aliases = {}
    if previous is not None:
        in_specs.append(pl.BlockSpec(memory_space=pl.ANY))
        operands.append(previous)
        aliases = {halves + 1: 0}
    return pl.pallas_call(
        functools.partial(covariance_kernel, place, 1.0 / frame_total, halves),
        grid=(blocks // count,),
        in_specs=in_specs,
        out_specs=pl.BlockSpec(memory_space=pl.ANY),
        out_shape=jax.ShapeDtypeStruct((total, 2, antennas, antennas), f32),
        scratch_shapes=[
            pltpu.VMEM((2, count * halves, 2, antennas, antennas), f32),
            pltpu.SemaphoreType.DMA((2, count * halves)),
        ],
        input_output_aliases=aliases,
        compiler_params=pltpu.CompilerParams(vmem_limit_bytes=covariance_vmem),
        cost_estimate=pl.CostEstimate(
            flops=blocks * halves * 400_000_000,
            bytes_accessed=blocks * halves * 250_000,
            transcendentals=0,
        ),
        name="covariances",
    )(*operands)


def orthonormal(vectors):
    found = []
    for column in range(vectors.shape[1]):
        residue = vectors[:, column, :]
        for earlier in found:
            residue = residue - earlier * jnp.sum(earlier * residue, axis=-1, keepdims=True)
        found.append(
            residue / jnp.sqrt(jnp.sum(residue * residue, axis=-1, keepdims=True) + epsilon)
        )
    return jnp.stack(found, axis=1)


def basis_of(chosen, counted, steering):
    count, slots = chosen.shape
    directions = steering.shape[0]
    onehot = (
        chosen[:, :, None] == lax.broadcasted_iota(jnp.int32, (count, slots, directions), 2)
    ).astype(f32)
    live = (lax.broadcasted_iota(jnp.int32, (count, slots), 1) < counted[:, None]).astype(f32)
    vectors = jnp.einsum("crn,na->cra", onehot, steering, precision=highest) * live[:, :, None]
    basis = orthonormal(vectors)
    return jnp.pad(basis, ((0, 0), (0, octet - slots), (0, 0)))


def per_device(samples, taps, steering, interferer_ids, ranks):
    antennas, width = samples.shape
    length = taps.shape[1]
    frames = width // length
    radix = length // lanes
    groups = radix // 2
    kept = lanes // 2
    shards = lax.axis_size("tm")
    spread = lax.axis_size("chan")
    devices = spread * shards
    owned = interferer_ids.shape[0]
    frame_total = frames * shards

    padded = samples
    if antennas < octet:
        padded = jnp.pad(samples, ((0, octet - antennas), (0, 0)))
    tables = [jnp.asarray(table) for table in phase_tables(length)]
    blocks = frames // frame_block
    middle = blocks // 2
    whole_runs = owned % radix == 0
    runs = owned // radix
    early, cuts = (early_pairs, later_pairs) if whole_runs else (0, (groups,))

    def exchange(spectra):
        received = lax.all_to_all(spectra, ("chan", "tm"), split_axis=0, concat_axis=0, tiled=True)
        received = received.reshape(spread, shards, -1, antennas, lanes)
        if antennas < octet:
            received = received.transpose(1, 2, 0, 3, 4).reshape(
                shards, -1, spread * antennas // octet, octet, lanes
            ).transpose(2, 0, 1, 3, 4)
        return received

    def channel_at(first, count):
        def place(index):
            run = index // (2 * count)
            column = index - run * (2 * count)
            group = first + column // 2
            mirrored = jnp.where(group == 0, groups, radix - group)
            return run * radix + jnp.where(column % 2 == 0, group, mirrored)

        return place

    late_high, late_low, edge, *spectra = head(
        padded, middle - 1, padded, taps, tables, middle, blocks - middle, early, True
    )
    before = lax.ppermute(edge, "tm", [(i, i + 1) for i in range(shards - 1)])
    waiting = []
    if early:
        late_early = exchange(spectra[0].reshape(devices, -1, octet, lanes))
    basis = basis_of(interferer_ids, ranks, steering)
    soon_high, soon_low, *spectra = head(
        before, 0, padded, taps, tables, 0, middle, early, False
    )
    first = early
    out = None
    for count in cuts:
        fresh = channels_of(
            (soon_high, soon_low), (late_high, late_low), tables, early, first, count
        )
        if whole_runs:
            fresh = fresh.reshape(devices, -1, octet, lanes)
            sent = fresh
            if first == early and early:
                head_rows = spectra[0].reshape(devices, -1, octet, lanes)
                sent = jnp.concatenate([head_rows, fresh], axis=1)
            if len(waiting) == 2 and not early:
                out = covariances(*waiting.pop(0), frame_total, owned, out)
                sent, out = lax.optimization_barrier((sent, out))
            elif early and first == early:
                sent, late_early = lax.optimization_barrier((sent, late_early))
            received = exchange(sent)
            if first == early and early:
                cut = runs * early
                waiting.append(
                    ((received[:, :, :cut], late_early), basis, channel_at(0, early))
                )
                received = received[:, :, cut:]
            waiting.append(((received,), basis, channel_at(first, count)))
        else:
            bins = [k for g in range(groups) for k in (g, radix - g if g else groups)]
            fresh = fresh[:, np.argsort(bins)].reshape(devices, owned, octet, lanes)
            received = exchange(fresh[:, :, :antennas])
            waiting.append(((received,), basis, lambda index: index))
        first += count
    while waiting:
        out = covariances(*waiting.pop(0), frame_total, owned, out)
    return out


early_pairs = 6
later_pairs = (7, 3)
head_vmem = 56 * 1024 * 1024
channel_vmem = 56 * 1024 * 1024
covariance_vmem = 56 * 1024 * 1024


def solution(mesh):
    in_specs = (P("chan", "tm"), P(), P(), P(("chan", "tm"), None), P(("chan", "tm")))
    out_specs = P(("chan", "tm"), None, None, None)
    return jax.shard_map(
        per_device, mesh=mesh, in_specs=in_specs, out_specs=out_specs, check_vma=False
    )
```

time: 162 us -> 155 us (0.957)
  waiting for transfers between devices: 57.9 us -> 52.4 us
  Pallas kernels: 76.2 us -> 71.1 us
  other arithmetic: 2.91 us -> 6.16 us
  local copies, waits for them, and re-layouts: 3.16 us -> 5.2 us
    pallas_call x4 -> x3, Pallas kernels: 34.9 us -> 26.9 us  [covariances(): pl.pallas_call(functools.partial(covariance_kernel, place, 1.0 / frame_to...]
    all_to_all x4 -> x3, waiting for transfers between devices: 57.9 us -> 52.4 us  [exchange(): lax.all_to_all(spectra, ('chan', 'tm'), split_axis=0, concat_axis=0, tile...]
    concatenate x0 -> x1, other arithmetic: none -> 3.23 us  [per_device(): sent = jnp.concatenate([head_rows, fresh], axis=1)]
    pallas_call x6 -> x4, Pallas kernels: 41.3 us -> 44.1 us  [the longest x2 31.8 us: head(): pl.pallas_call(functools.partial(head_kernel, length, steps, count, with_...]
    all_to_all x4 -> x3, starting transfers between devices: 17.6 us -> 16.5 us  [exchange(): lax.all_to_all(spectra, ('chan', 'tm'), split_axis=0, concat_axis=0, tile...]
  transfers between devices with their start and end apart: 5 -> 4, of which waited for: 4 -> 1; matrix products, arithmetic and copies ran while one was open for 2% -> 6% of each run, Pallas kernels for 37% -> 32%
where the time goes in v3:
time: 155 us; the launch traced here: 154 us
  Pallas kernels  71.1 us (46%)
  waiting for transfers between devices  52.4 us (34%)
  starting transfers between devices  18.9 us (12%)
  other arithmetic  6.16 us (4%)
  local copies, waits for them, and re-layouts  5.2 us (3%)
    all_to_all x3, waiting for transfers between devices, exchange(): lax.all_to_all(spectra, ('chan', 'tm'), split_axis=0, concat_axis=0, tile...  52.4 us
    pallas_call x2, Pallas kernels, head(): pl.pallas_call(functools.partial(head_kernel, length, steps, count, with_...  31.8 us
    pallas_call x3, Pallas kernels, covariances(): pl.pallas_call(functools.partial(covariance_kernel, place, 1.0 / frame_to...  26.9 us
    all_to_all x3, starting transfers between devices, exchange(): lax.all_to_all(spectra, ('chan', 'tm'), split_axis=0, concat_axis=0, tile...  16.5 us
    pallas_call x2, Pallas kernels, channels_of(): pl.pallas_call(channel_kernel, grid=(count,), in_specs=[section] * 4 + [t...  12.3 us
    concatenate x1, other arithmetic, per_device(): sent = jnp.concatenate([head_rows, fresh], axis=1)  3.23 us
  transfers between devices with their start and end apart: 4, of which 1 were waited for; matrix products, arithmetic and copies ran while one was open for 6% of the time, Pallas kernels for 32%

profile of v3, /device:TPU:0, one launch (start us, length us, event | category | flops | bytes accessed | tf_op | source)
XLA Modules:
  0.0 154.3 jit_solution(8591918251604699507)
XLA Ops:
  0.0 0.0 copy-start
  0.0 15.9 %head.2 = (bf16[10,8,32,256]{3,2,1,0:T(8,128)(2,1)}, bf16[10,8,32,256]{3,2,1,0:T(8,128)(2,1)}, bf16[8,65536]{1,0:T(8,128)(2,1)}, bf16[64,6,8,128]{3,2,1,0:T(8,128)(2,1)}) custom-call(bf16[8,262144]{1,0:T(8,128)(2,1)} %refs_1_.3, bf16[8,262144]{1,0:T(8,128)(2,1)} %refs_1_.3, f32[16,4096]{1,0:T(8,128)} %refs_2_.3, ...), custom_call_target="tpu_custom_call" | custom-call | flops 9600000000 | bytes 6000000 | tf_op jit(solution)/shard_map/head/pallas_call | solution.py:193
  15.9 2.4 %collective-permute-start = (bf16[8,65536]{1,0:T(8,128)(2,1)}, bf16[8,65536]{1,0:T(8,128)(2,1)S(1)}, u32[]{:S(2)}, u32[]{:S(2)}) collective-permute-start(bf16[8,65536]{1,0:T(8,128)(2,1)} %get-tuple-element.14), channel_id=1, source_target_pairs={{0,1},{2,3},{4,5},{6,7},{8,9},{10,11},{12,13},{14,15},{16,17},{18,... | collective-permute-start | bytes 3145736 | tf_op jit(solution)/shard_map/ppermute | solution.py:488
  18.3 6.7 %all-to-all-start.1 = ((bf16[32,12,8,128]{3,2,1,0:T(8,128)(2,1)}), bf16[32,12,8,128]{3,2,1,0:T(8,128)(2,1)S(1)}, u32[]{:S(2)}, u32[]{:S(2)}) async-start(bf16[32,12,8,128]{3,2,1,0:T(8,128)(2,1)} %bitcast.74), calls=%async_computation.1 | async-start | bytes 1572864 | tf_op jit(solution)/shard_map/all_to_all | solution.py:467
  25.0 0.0 collective-permute-done.refs_0_
  25.0 0.0 copy-start.6
  25.1 1.0 copy-done.6
  26.0 15.9 %head.3 = (bf16[10,8,32,256]{3,2,1,0:T(8,128)(2,1)}, bf16[10,8,32,256]{3,2,1,0:T(8,128)(2,1)}, bf16[64,6,8,128]{3,2,1,0:T(8,128)(2,1)}) custom-call(bf16[8,65536]{1,0:T(8,128)(2,1)} %copy-done.6, bf16[8,262144]{1,0:T(8,128)(2,1)} %refs_1_.3, f32[16,4096]{1,0:T(8,128)} %refs_2_.3, bf16[16,256,256]{2,1,0:T(8,128)(2,1)} %constant.10.clone.refs_3_.wh_ref, ...), custom_call_target="tpu_custom_call" | custom-call | flops 9600000000 | bytes 6000000 | tf_op jit(solution)/shard_map/head/pallas_call | solution.py:193
  41.9 0.0 copy-start.2
  41.9 8.0 %channels_of.3 = bf16[64,14,8,128]{3,2,1,0:T(8,128)(2,1)} custom-call(bf16[10,8,32,256]{3,2,1,0:T(8,128)(2,1)} %get-tuple-element.15.ha_ref, bf16[10,8,32,256]{3,2,1,0:T(8,128)(2,1)} %get-tuple-element.16.la_ref, bf16[10,8,32,256]{3,2,1,0:T(8,128)(2,1)} %get-tuple-element.17.hb_ref, bf16[10,8,32,256]{3,2,1,0:T(8,128)(2,1)} %get-tuple-element.18.lb_ref, ...), custom_call_target="tpu_custom_call" | custom-call | flops 5600000000 | bytes 8400000 | tf_op jit(solution)/shard_map/channels_of/pallas_call | solution.py:272
  49.9 0.0 copy-done.2
  49.9 3.2 %pad_maximum_fusion = bf16[32,40,8,128]{3,2,1,0:T(8,128)(2,1)} fusion(bf16[32,28,8,128]{3,2,1,0:T(8,128)(2,1)} %bitcast.71, bf16[32,12,8,128]{3,2,1,0:T(8,128)(2,1)S(1)} %bitcast.72), kind=kLoop, calls=%fused_computation | loop fusion | flops 1310720 | bytes 5242880 | tf_op jit(solution)/shard_map/concatenate | solution.py:507
  53.2 0.0 all-to-all-done.1
  53.2 0.0 copy-start.3
  53.2 0.0 copy-start.5
  53.2 0.0 copy-start.4
  53.2 0.9 copy-done.3
  54.1 5.8 %all-to-all-start.2 = ((bf16[32,40,8,128]{3,2,1,0:T(8,128)(2,1)}), bf16[32,40,8,128]{3,2,1,0:T(8,128)(2,1)S(1)}, u32[]{:S(2)}, u32[]{:S(2)}) async-start(bf16[32,40,8,128]{3,2,1,0:T(8,128)(2,1)} %pad_maximum_fusion), calls=%async_computation.2 | async-start | bytes 5242880 | tf_op jit(solution)/shard_map/all_to_all | solution.py:467
  60.0 0.0 copy-done.5
  60.0 0.0 copy-done
  60.0 0.0 copy-done.4
  60.0 0.3 convolution_multiply_fusion
  60.3 0.1 fusion.3
  60.4 0.1 div.54
  60.5 0.1 div.55
  60.6 0.2 fusion.2
  60.8 0.2 fusion
  61.0 0.2 fusion.1
  61.2 0.2 multiply_reduce_fusion.2
  61.4 0.2 multiply_reduce_fusion.1
  61.6 0.2 multiply_reduce_fusion
  61.8 0.1 multiply_subtract_fusion.2
  61.9 0.6 subtract_divide_fusion
  62.5 0.9 select_maximum_fusion.refs_2_.refs_1_
  63.4 4.3 %channels_of.2 = bf16[64,6,8,128]{3,2,1,0:T(8,128)(2,1)} custom-call(bf16[10,8,32,256]{3,2,1,0:T(8,128)(2,1)} %get-tuple-element.15.ha_ref, bf16[10,8,32,256]{3,2,1,0:T(8,128)(2,1)} %get-tuple-element.16.la_ref, bf16[10,8,32,256]{3,2,1,0:T(8,128)(2,1)} %get-tuple-element.17.hb_ref, bf16[10,8,32,256]{3,2,1,0:T(8,128)(2,1)} %get-tuple-element.18.lb_ref, ...), custom_call_target="tpu_custom_call" | custom-call | flops 2400000000 | bytes 3600000 | tf_op jit(solution)/shard_map/channels_of/pallas_call | solution.py:272
  67.7 52.4 %all-to-all-done.2 = bf16[32,40,8,128]{3,2,1,0:T(8,128)(2,1)S(1)} async-done(((bf16[32,40,8,128]{3,2,1,0:T(8,128)(2,1)}), bf16[32,40,8,128]{3,2,1,0:T(8,128)(2,1)S(1)}, u32[]{:S(2)}, u32[]{:S(2)}) %all-to-all-start.2) | async-done | bytes 2621472 | tf_op jit(solution)/shard_map/all_to_all | solution.py:467
  120.1 4.0 %all-to-all-start = ((bf16[32,12,8,128]{3,2,1,0:T(8,128)(2,1)}), bf16[32,12,8,128]{3,2,1,0:T(8,128)(2,1)S(1)}, u32[]{:S(2)}, u32[]{:S(2)}) async-start(bf16[32,12,8,128]{3,2,1,0:T(8,128)(2,1)} %bitcast.70), calls=%async_computation | async-start | bytes 1572864 | tf_op jit(solution)/shard_map/all_to_all | solution.py:467
  124.1 1.0 slice.29.refs_0_
  125.1 1.4 slice.28.refs_0_
  126.5 10.2 %covariances.3.refs_2_ = f32[64,2,128,128]{3,2,1,0:T(8,128)} custom-call(bf16[16,2,12,8,128]{4,3,2,1,0:T(8,128)(2,1)} %slice.29.refs_0_, bf16[16,2,12,8,128]{4,3,2,1,0:T(8,128)(2,1)} %bitcast.73, f32[64,8,128]{2,1,0:T(8,128)} %select_maximum_fusion.refs_2_.refs_1_), custom_call_target="tpu_custom_call" | custom-call | flops 9600000000 | bytes 6000000 | tf_op jit(solution)/shard_map/covariances/pallas_call | solution.py:398
  136.6 11.0 %covariances.4.refs_2_ = f32[64,2,128,128]{3,2,1,0:T(8,128)} custom-call(bf16[16,2,28,8,128]{4,3,2,1,0:T(8,128)(2,1)} %slice.28.refs_0_, f32[64,8,128]{2,1,0:T(8,128)} %select_maximum_fusion.refs_2_.refs_1_, f32[64,2,128,128]{3,2,1,0:T(8,128)} %covariances.3.refs_2_), custom_call_target="tpu_custom_call", output_to_operand_aliasing={{}: (2, {})} | custom-call | flops 11200000000 | bytes 7000000 | tf_op jit(solution)/shard_map/covariances/pallas_call | solution.py:398
  147.7 0.0 all-to-all-done
  147.7 0.0 copy-start.1
  147.7 0.9 copy-done.1
  148.5 5.8 %covariances.5 = f32[64,2,128,128]{3,2,1,0:T(8,128)} custom-call(bf16[16,2,12,8,128]{4,3,2,1,0:T(8,128)(2,1)} %bitcast.69, f32[64,8,128]{2,1,0:T(8,128)} %select_maximum_fusion.refs_2_.refs_1_, f32[64,2,128,128]{3,2,1,0:T(8,128)} %covariances.4.refs_2_), custom_call_target="tpu_custom_call", output_to_operand_aliasing={{}: (2, {})} | custom-call | flops 4800000000 | bytes 3000000 | tf_op jit(solution)/shard_map/covariances/pallas_call | solution.py:398
  (6 shorter events, 0.0 us)
Async XLA Ops:
  0.0 60.0 %copy-start = (f32[8,128]{1,0:T(8,128)S(1)}, f32[8,128]{1,0:T(8,128)}, u32[]{:S(2)}) copy-start(f32[8,128]{1,0:T(8,128)} %param.9) | copy-start | bytes 12292
  15.9 9.1 %collective-permute-start = (bf16[8,65536]{1,0:T(8,128)(2,1)}, bf16[8,65536]{1,0:T(8,128)(2,1)S(1)}, u32[]{:S(2)}, u32[]{:S(2)}) collective-permute-start(bf16[8,65536]{1,0:T(8,128)(2,1)} %get-tuple-element.14), channel_id=1, source_target_pairs={{0,1},{2,3},{4,5},{6,7},{8,9},{10,11},{12,13},{14,15},{16,17},{18,... | collective-permute-start | bytes 3145736 | tf_op jit(solution)/shard_map/ppermute | solution.py:488
  18.3 34.8 %all-to-all-start.1 = ((bf16[32,12,8,128]{3,2,1,0:T(8,128)(2,1)}), bf16[32,12,8,128]{3,2,1,0:T(8,128)(2,1)S(1)}, u32[]{:S(2)}, u32[]{:S(2)}) async-start(bf16[32,12,8,128]{3,2,1,0:T(8,128)(2,1)} %bitcast.74), calls=%async_computation.1 | async-start | bytes 1572864 | tf_op jit(solution)/shard_map/all_to_all | solution.py:467
  25.0 1.0 copy-start.6
  41.9 8.0 %copy-start.2 = (bf16[64,6,8,128]{3,2,1,0:T(8,128)(2,1)S(1)}, bf16[64,6,8,128]{3,2,1,0:T(8,128)(2,1)}, u32[]{:S(2)}) copy-start(bf16[64,6,8,128]{3,2,1,0:T(8,128)(2,1)} %get-tuple-element.19) | copy-start | bytes 2359300
  53.2 0.9 copy-start.3
  53.2 6.8 %copy-start.5 = (s32[64]{0:T(128)S(1)}, s32[64]{0:T(128)}, u32[]{:S(2)}) copy-start(s32[64]{0:T(128)} %param.11) | copy-start | bytes 772
  53.2 6.8 %copy-start.4 = (s32[64,4]{0,1:T(4,128)S(1)}, s32[64,4]{0,1:T(4,128)}, u32[]{:S(2)}) copy-start(s32[64,4]{0,1:T(4,128)} %param.10) | copy-start | bytes 3076
  54.1 66.0 %all-to-all-start.2 = ((bf16[32,40,8,128]{3,2,1,0:T(8,128)(2,1)}), bf16[32,40,8,128]{3,2,1,0:T(8,128)(2,1)S(1)}, u32[]{:S(2)}, u32[]{:S(2)}) async-start(bf16[32,40,8,128]{3,2,1,0:T(8,128)(2,1)} %pad_maximum_fusion), calls=%async_computation.2 | async-start | bytes 5242880 | tf_op jit(solution)/shard_map/all_to_all | solution.py:467
  120.1 27.6 %all-to-all-start = ((bf16[32,12,8,128]{3,2,1,0:T(8,128)(2,1)}), bf16[32,12,8,128]{3,2,1,0:T(8,128)(2,1)S(1)}, u32[]{:S(2)}, u32[]{:S(2)}) async-start(bf16[32,12,8,128]{3,2,1,0:T(8,128)(2,1)} %bitcast.70), calls=%async_computation | async-start | bytes 1572864 | tf_op jit(solution)/shard_map/all_to_all | solution.py:467
  147.7 0.9 copy-start.1

commit v4 on v3

--- a/solution.py
+++ b/solution.py
@@ -102,9 +102,13 @@
                 low[group, antenna, kept, side * lanes : (side + 1) * lanes] = second
 
 
-def second_stage(high, low, wh_ref, wl_ref):
+def second_stage(high, low, wave_high, wave_low):
     dot = functools.partial(jnp.dot, preferred_element_type=f32)
-    return dot(high, wh_ref[0]) + (dot(low, wh_ref[0]) + dot(high, wl_ref[0]))
+    return dot(high, wave_high) + (dot(low, wave_high) + dot(high, wave_low))
+
+
+def divisor(*sizes, most=3):
+    return max(n for n in range(1, most + 1) if all(size % n == 0 for size in sizes))
 
 
 def head_kernel(length, steps, count, with_edge, *refs):
@@ -153,25 +157,28 @@
 
         @pl.when(step >= steps)
         def _():
-            group = step - steps
             rows = (octet * frames, 2 * lanes)
-            total = second_stage(
-                high[group].reshape(rows), low[group].reshape(rows), wh_ref, wl_ref
-            )
-            for a in range(octet):
-                piece = total[a * frames : (a + 1) * frames]
-                piece = jnp.concatenate([piece[:, :lanes], piece[:, lanes:]], axis=0).T
-                piece = jnp.concatenate([piece[:kept], piece[kept:]], axis=1)
-                turned[pl.ds(a, kept, stride=octet), :] = piece
-            out_ref[:, 0] = turned[...].reshape(kept, octet, lanes).astype(bf16)
-
-    @pl.when(step == steps + count - 1)
+            totals = []
+            for j in range(turned.shape[0]):
+                group = (step - steps) * turned.shape[0] + j
+                pair = high[group].reshape(rows), low[group].reshape(rows)
+                totals.append(second_stage(*pair, wh_ref[j], wl_ref[j]))
+            for j, total in enumerate(totals):
+                for a in range(octet):
+                    piece = total[a * frames : (a + 1) * frames]
+                    piece = jnp.concatenate([piece[:, :lanes], piece[:, lanes:]], axis=0).T
+                    piece = jnp.concatenate([piece[:kept], piece[kept:]], axis=1)
+                    turned[j, pl.ds(a, kept, stride=octet), :] = piece
+            for j in range(turned.shape[0]):
+                out_ref[:, j] = turned[j].reshape(kept, octet, lanes).astype(bf16)
+
+    @pl.when(step == pl.num_programs(0) - 1)
     def _():
         for copy in copies:
             copy.wait()
 
 
-def head(before, before_block, samples, taps, tables, first, steps, count, with_edge):
+def head(before, before_block, samples, taps, tables, first, steps, count, with_edge, columns):
     length = taps.shape[1]
     radix = length // lanes
     groups = radix // 2
@@ -180,19 +187,20 @@
     width = frame_block * length
     rest = jax.ShapeDtypeStruct((groups - count, octet, frames, 2 * lanes), bf16)
     anywhere = pl.BlockSpec(memory_space=pl.ANY)
-    table = pl.BlockSpec((1, 2 * lanes, 2 * lanes), lambda i: (jnp.maximum(i - steps, 0), 0, 0))
+    each = divisor(count)
+    table = pl.BlockSpec((each, 2 * lanes, 2 * lanes), lambda i: (jnp.maximum(i - steps, 0), 0, 0))
     out_shape, out_specs = [rest, rest], [anywhere, anywhere]
     if with_edge:
         out_shape.append(jax.ShapeDtypeStruct((octet, width), bf16))
         out_specs.append(anywhere)
     if count:
-        out_shape.append(jax.ShapeDtypeStruct((kept, count, octet, lanes), bf16))
+        out_shape.append(jax.ShapeDtypeStruct((kept, columns, octet, lanes), bf16))
         out_specs.append(
-            pl.BlockSpec((kept, 1, octet, lanes), lambda i: (0, jnp.maximum(i - steps, 0), 0, 0))
+            pl.BlockSpec((kept, each, octet, lanes), lambda i: (0, jnp.maximum(i - steps, 0), 0, 0))
         )
     return pl.pallas_call(
         functools.partial(head_kernel, length, steps, count, with_edge),
-        grid=(steps + count,),
+        grid=(steps + count // each,),
         in_specs=[
             pl.BlockSpec((octet, width), lambda i: (0, before_block)),
             pl.BlockSpec((octet, width), lambda i: (0, first + jnp.minimum(i, steps - 1))),
@@ -206,7 +214,7 @@
             pltpu.VMEM((radix, frame_block * octet, lanes), f32),
             pltpu.VMEM((radix, frame_block, lanes), f32),
             pltpu.VMEM((radix, taps.shape[0] - 1, octet, lanes), f32),
-            pltpu.VMEM((kept * octet, lanes), f32),
+            pltpu.VMEM((each, kept * octet, lanes), f32),
             pltpu.VMEM((groups, octet, frames, 2 * lanes), bf16),
             pltpu.VMEM((groups, octet, frames, 2 * lanes), bf16),
             pltpu.SemaphoreType.DMA((3,)),
@@ -247,41 +255,60 @@
     return lax.dot_general(left, right, (((1,), (1,)), ((), ())), preferred_element_type=f32)
 
 
-def channel_kernel(ha_ref, la_ref, hb_ref, lb_ref, wh_ref, wl_ref, out_ref, turned):
+def channel_kernel(ha_ref, la_ref, hb_ref, lb_ref, wh_ref, wl_ref, *refs):
+    out_ref, turned = refs[-2:]
     frames = ha_ref.shape[2]
     kept = lanes // 2
     rows = (octet * frames, 2 * lanes)
-    high = jnp.concatenate([ha_ref[0].reshape(rows), hb_ref[0].reshape(rows)], axis=0)
-    low = jnp.concatenate([la_ref[0].reshape(rows), lb_ref[0].reshape(rows)], axis=0)
-    total = second_stage(high, low, wh_ref, wl_ref)
-    for a in range(octet):
-        one = total[a * frames : (a + 1) * frames]
-        two = total[(octet + a) * frames : (octet + a + 1) * frames]
-        piece = [one[:, :lanes], two[:, :lanes], one[:, lanes:], two[:, lanes:]]
-        turned[pl.ds(a, lanes, stride=octet), :] = jnp.concatenate(piece, axis=0).T
-    for half in range(2):
-        piece = turned[half * kept * octet : (half + 1) * kept * octet]
-        out_ref[:, half] = piece.reshape(kept, octet, lanes).astype(bf16)
-
-
-def channels_of(first_half, second_half, tables, skipped, first, count):
+    totals = []
+    for j in range(turned.shape[0]):
+        high = jnp.concatenate([ha_ref[j].reshape(rows), hb_ref[j].reshape(rows)], axis=0)
+        low = jnp.concatenate([la_ref[j].reshape(rows), lb_ref[j].reshape(rows)], axis=0)
+        totals.append(second_stage(high, low, wh_ref[j], wl_ref[j]))
+    for j, total in enumerate(totals):
+        for a in range(octet):
+            one = total[a * frames : (a + 1) * frames]
+            two = total[(octet + a) * frames : (octet + a + 1) * frames]
+            piece = [one[:, :lanes], two[:, :lanes], one[:, lanes:], two[:, lanes:]]
+            turned[j, pl.ds(a, lanes, stride=octet), :] = jnp.concatenate(piece, axis=0).T
+    for j in range(turned.shape[0]):
+        for half in range(2):
+            piece = turned[j, half * kept * octet : (half + 1) * kept * octet]
+            out_ref[:, 2 * j + half] = piece.reshape(kept, octet, lanes).astype(bf16)
+
+
+def channels_of(first_half, second_half, tables, skipped, first, count, begun=None):
     frames = first_half[0].shape[2]
     kept = lanes // 2
-    section = pl.BlockSpec((1, octet, frames, 2 * lanes), lambda i: (i + first - skipped, 0, 0, 0))
-    table = pl.BlockSpec((1, 2 * lanes, 2 * lanes), lambda i: (i + first, 0, 0))
+    held = 0 if begun is None else begun.shape[1] - 2 * count
+    each = divisor(count, first, first - skipped, held // 2) if held % 2 == 0 else 0
+    section = pl.BlockSpec(
+        (each, octet, frames, 2 * lanes), lambda i: (i + (first - skipped) // each, 0, 0, 0)
+    )
+    table = pl.BlockSpec((each, 2 * lanes, 2 * lanes), lambda i: (i + first // each, 0, 0))
+    operands = [*first_half, *second_half, *tables]
+    in_specs = [section] * 4 + [table] * 2
+    aliases = {}
+    if begun is not None:
+        aliases = {len(operands): 0}
+        operands.append(begun)
+        in_specs.append(pl.BlockSpec(memory_space=pl.ANY))
     return pl.pallas_call(
         channel_kernel,
-        grid=(count,),
-        in_specs=[section] * 4 + [table] * 2,
-        out_specs=pl.BlockSpec((kept, 2, octet, lanes), lambda i: (0, i, 0, 0)),
-        out_shape=jax.ShapeDtypeStruct((kept, 2 * count, octet, lanes), bf16),
-        scratch_shapes=[pltpu.VMEM((lanes * octet, lanes), f32)],
+        grid=(count // each,),
+        in_specs=in_specs,
+        out_specs=pl.BlockSpec(
+            (kept, 2 * each, octet, lanes), lambda i: (0, i + held // (2 * each), 0, 0)
+        ),
+        out_shape=jax.ShapeDtypeStruct((kept, held + 2 * count, octet, lanes), bf16),
+        scratch_shapes=[pltpu.VMEM((each, lanes * octet, lanes), f32)],
+        input_output_aliases=aliases,
         compiler_params=pltpu.CompilerParams(vmem_limit_bytes=channel_vmem),
         cost_estimate=pl.CostEstimate(
             flops=count * 800_000_000, bytes_accessed=count * 1_200_000, transcendentals=0
         ),
         name="channels_of",
-    )(*first_half, *second_half, *tables)
+    )(*operands)
 
 
 def swap(one, two, width):
@@ -340,33 +367,29 @@
                     found[1].append(imag)
         return [jnp.concatenate(real + imag, axis=1) for real, imag in parts]
 
-    def project(x, q):
-        qh, qm, ql = split_three(q)
-        left = jnp.concatenate([qh, qm, ql, jnp.zeros_like(q)], axis=0).astype(bf16)
-        z = jnp.dot(left, x.astype(bf16), preferred_element_type=f32)
-        z = z[:octet] + z[octet : 2 * octet] + z[2 * octet : 3 * octet]
-        zh, zm, zl = split_three(z)
-        left = jnp.concatenate([qh, qh, qm, qm, qh, ql], axis=0).astype(bf16)
-        right = jnp.concatenate([zh, zm, zh, zm, zl, zh], axis=0).astype(bf16)
-        return x - lax.dot_general(
-            left, right, (((0,), (0,)), ((), ())), preferred_element_type=f32
-        )
-
     def turned(v):
         middle = v.shape[1] // 2
         return jnp.concatenate([v[:, middle:], -v[:, :middle]], axis=1)
 
-    for j in range(blocks):
-        for h, x in enumerate(channels(j)):
-            at = j * halves + h
-            high, low = split_two(project(x, q_ref[place(step * count + at)]))
-            left = jnp.concatenate([high, turned(high), low, turned(low)], axis=0)
-            total = contract_last(left, jnp.concatenate([high, low], axis=0))
-            total = total[:, :antennas] + total[:, antennas:]
-            total = (total[: 2 * antennas] + total[2 * antennas :]) * scale
-            ready[slot, at] = total.reshape(2, antennas, antennas)
-
-    for copy in copies(step, slot):
+    xs = [x for j in range(blocks) for x in channels(j)]
+    qs = [split_three(q_ref[place(step * count + at)]) for at in range(count)]
+    zs = []
+    for x, (qh, qm, ql) in zip(xs, qs):
+        left = jnp.concatenate([qh, qm, ql, jnp.zeros_like(qh)], axis=0).astype(bf16)
+        z = jnp.dot(left, x.astype(bf16), preferred_element_type=f32)
+        zs.append(split_three(z[:octet] + z[octet : 2 * octet] + z[2 * octet : 3 * octet]))
+    parts = []
+    for x, (qh, qm, ql), (zh, zm, zl) in zip(xs, qs, zs):
+        left = jnp.concatenate([qh, qh, qm, qm, qh, ql], axis=0).astype(bf16)
+        right = jnp.concatenate([zh, zm, zh, zm, zl, zh], axis=0).astype(bf16)
+        taken = lax.dot_general(left, right, (((0,), (0,)), ((), ())), preferred_element_type=f32)
+        parts.append(split_two(x - taken))
+    for at, ((high, low), copy) in enumerate(zip(parts, copies(step, slot))):
+        left = jnp.concatenate([high, turned(high), low, turned(low)], axis=0)
+        total = contract_last(left, jnp.concatenate([high, low], axis=0))
+        total = total[:, :antennas] + total[:, antennas:]
+        total = (total[: 2 * antennas] + total[2 * antennas :]) * scale
+        ready[slot, at] = total.reshape(2, antennas, antennas)
         copy.start()
 
     @pl.when(step == steps - 1)
@@ -382,14 +405,25 @@
 
 def covariances(received, basis, place, frame_total, total, previous):
     halves = len(received)
-    octets, shards, blocks = received[0].shape[:3]
+    array, runs, _, blocks = received[0]
+    octets, shards = array.shape[:2]
     antennas = octets * octet
-    count = math.gcd(blocks, 4 // halves)
-    in_specs = [
-        pl.BlockSpec((octets, shards, count, octet, lanes), lambda i: (0, 0, i, 0, 0))
-    ] * halves
+    sizes = [n for a, r, begin, _ in received for n in (a.shape[2] // r, begin)]
+    count = divisor(blocks, *sizes, most=8 // halves)
+    steps = blocks // count
+
+    def window(array, runs, begin, _):
+        stride = array.shape[2] // runs // count
+
+        def index(i):
+            run = i // steps
+            return (0, 0, run * stride + begin // count + i - run * steps, 0, 0)
+
+        return pl.BlockSpec((octets, shards, count, octet, lanes), index)
+
+    in_specs = [window(*one) for one in received]
     in_specs.append(pl.BlockSpec(basis.shape, lambda i: (0, 0, 0)))
-    operands = [*received, basis]
+    operands = [*(one[0] for one in received), basis]
     aliases = {}
     if previous is not None:
         in_specs.append(pl.BlockSpec(memory_space=pl.ANY))
@@ -397,7 +431,7 @@
         aliases = {halves + 1: 0}
     return pl.pallas_call(
         functools.partial(covariance_kernel, place, 1.0 / frame_total, halves),
-        grid=(blocks // count,),
+        grid=(runs * steps,),
         in_specs=in_specs,
         out_specs=pl.BlockSpec(memory_space=pl.ANY),
         out_shape=jax.ShapeDtypeStruct((total, 2, antennas, antennas), f32),
@@ -408,8 +442,8 @@
         input_output_aliases=aliases,
         compiler_params=pltpu.CompilerParams(vmem_limit_bytes=covariance_vmem),
         cost_estimate=pl.CostEstimate(
-            flops=blocks * halves * 400_000_000,
-            bytes_accessed=blocks * halves * 250_000,
+            flops=runs * blocks * halves * 400_000_000,
+            bytes_accessed=runs * blocks * halves * 250_000,
             transcendentals=0,
         ),
         name="covariances",
@@ -483,57 +517,54 @@
         return place
 
     late_high, late_low, edge, *spectra = head(
-        padded, middle - 1, padded, taps, tables, middle, blocks - middle, early, True
+        padded, middle - 1, padded, taps, tables, middle, blocks - middle, early, True, early
     )
     before = lax.ppermute(edge, "tm", [(i, i + 1) for i in range(shards - 1)])
-    waiting = []
     if early:
         late_early = exchange(spectra[0].reshape(devices, -1, octet, lanes))
     basis = basis_of(interferer_ids, ranks, steering)
     soon_high, soon_low, *spectra = head(
-        before, 0, padded, taps, tables, 0, middle, early, False
+        before, 0, padded, taps, tables, 0, middle, early, False, early + 2 * cuts[0]
     )
     first = early
     out = None
+    waiting = []
     for count in cuts:
-        fresh = channels_of(
-            (soon_high, soon_low), (late_high, late_low), tables, early, first, count
+        begun = spectra[0] if early and first == early else None
+        sent = channels_of(
+            (soon_high, soon_low), (late_high, late_low), tables, early, first, count, begun
         )
         if whole_runs:
-            fresh = fresh.reshape(devices, -1, octet, lanes)
-            sent = fresh
-            if first == early and early:
-                head_rows = spectra[0].reshape(devices, -1, octet, lanes)
-                sent = jnp.concatenate([head_rows, fresh], axis=1)
-            if len(waiting) == 2 and not early:
-                out = covariances(*waiting.pop(0), frame_total, owned, out)
-                sent, out = lax.optimization_barrier((sent, out))
-            elif early and first == early:
+            sent = sent.reshape(devices, -1, octet, lanes)
+            held = 0
+            if begun is not None:
                 sent, late_early = lax.optimization_barrier((sent, late_early))
+                held = early
+            else:
+                sent, basis = lax.optimization_barrier((sent, basis))
             received = exchange(sent)
-            if first == early and early:
-                cut = runs * early
-                waiting.append(
-                    ((received[:, :, :cut], late_early), basis, channel_at(0, early))
-                )
-                received = received[:, :, cut:]
-            waiting.append(((received,), basis, channel_at(first, count)))
+            if begun is not None:
+                pieces = ((received, runs, 0, early), (late_early, runs, 0, early))
+                waiting.append((pieces, basis, channel_at(0, early)))
+            waiting.append(
+                (((received, runs, held, 2 * count),), basis, channel_at(first, count))
+            )
         else:
             bins = [k for g in range(groups) for k in (g, radix - g if g else groups)]
-            fresh = fresh[:, np.argsort(bins)].reshape(devices, owned, octet, lanes)
-            received = exchange(fresh[:, :, :antennas])
-            waiting.append(((received,), basis, lambda index: index))
+            sent = sent[:, np.argsort(bins)].reshape(devices, owned, octet, lanes)
+            received = exchange(sent[:, :, :antennas])
+            waiting.append((((received, 1, 0, owned),), basis, lambda index: index))
         first += count
-    while waiting:
-        out = covariances(*waiting.pop(0), frame_total, owned, out)
+    for one in waiting:
+        out = covariances(*one, frame_total, owned, out)
     return out
 
 
-early_pairs = 6
-later_pairs = (7, 3)
+early_pairs = 10
+later_pairs = (3, 3)
 head_vmem = 56 * 1024 * 1024
 channel_vmem = 56 * 1024 * 1024
-covariance_vmem = 56 * 1024 * 1024
+covariance_vmem = 24 * 1024 * 1024
 
 
 def solution(mesh):

time: 155 us -> 138 us (0.89)
  Pallas kernels: 71.1 us -> 60.1 us
  other arithmetic: 6.16 us -> 2.22 us
  starting transfers between devices: 18.9 us -> 17.1 us
  local copies, waits for them, and re-layouts: 5.2 us -> 3.46 us
    pallas_call x3, Pallas kernels: 26.9 us -> 19.1 us  [covariances(): pl.pallas_call(functools.partial(covariance_kernel, place, 1.0 / frame_to...]
    pallas_call x2, Pallas kernels: 12.3 us -> 8.66 us  [channels_of(): pl.pallas_call(channel_kernel, grid=(count // each,), in_specs=in_specs,...]
    concatenate x1 -> x0, other arithmetic: 3.23 us -> none  [per_device(): sent = jnp.concatenate([head_rows, fresh], axis=1)]
    slice x2 -> x0, local copies, waits for them, and re-layouts: 2.35 us -> none  [the longest x1 1.4 us: per_device(): received = received[:, :, cut:]]
    ppermute x1, waiting for transfers between devices: 0.01 us -> 2.2 us  [per_device(): before = lax.ppermute(edge, 'tm', [(i, i + 1) for i in range(shards - 1)])]
    all_to_all x3, starting transfers between devices: 16.5 us -> 14.9 us  [exchange(): lax.all_to_all(spectra, ('chan', 'tm'), split_axis=0, concat_axis=0, tile...]
  transfers between devices with their start and end apart: 4 -> 4, of which waited for: 1 -> 4; matrix products, arithmetic and copies ran while one was open for 6% -> 2% of each run, Pallas kernels for 32% -> 30%
where the time goes in v4:
time: 138 us; the launch traced here: 137 us
  Pallas kernels  60.1 us (44%)
  waiting for transfers between devices  53.4 us (39%)
  starting transfers between devices  17.1 us (12%)
  local copies, waits for them, and re-layouts  3.46 us (3%)
  other arithmetic  2.22 us (2%)
    all_to_all x3, waiting for transfers between devices, exchange(): lax.all_to_all(spectra, ('chan', 'tm'), split_axis=0, concat_axis=0, tile...  51.2 us
    pallas_call x2, Pallas kernels, head(): pl.pallas_call(functools.partial(head_kernel, length, steps, count, with_...  32.4 us
    pallas_call x3, Pallas kernels, covariances(): pl.pallas_call(functools.partial(covariance_kernel, place, 1.0 / frame_to...  19.1 us
    all_to_all x3, starting transfers between devices, exchange(): lax.all_to_all(spectra, ('chan', 'tm'), split_axis=0, concat_axis=0, tile...  14.9 us
    pallas_call x2, Pallas kernels, channels_of(): pl.pallas_call(channel_kernel, grid=(count // each,), in_specs=in_specs,...  8.66 us
    unnamed x14, local copies, waits for them, and re-layouts  3.38 us
  transfers between devices with their start and end apart: 4, of which 4 were waited for; matrix products, arithmetic and copies ran while one was open for 2% of the time, Pallas kernels for 30%

profile of v4, /device:TPU:0, one launch (start us, length us, event | category | flops | bytes accessed | tf_op | source)
XLA Modules:
  0.0 136.8 jit_solution(14324163050926075957)
XLA Ops:
  0.0 0.0 copy-start
  0.0 16.2 %head.2 = (bf16[6,8,32,256]{3,2,1,0:T(8,128)(2,1)}, bf16[6,8,32,256]{3,2,1,0:T(8,128)(2,1)}, bf16[8,65536]{1,0:T(8,128)(2,1)}, bf16[64,10,8,128]{3,2,1,0:T(8,128)(2,1)}) custom-call(bf16[8,262144]{1,0:T(8,128)(2,1)} %refs_1_.3, bf16[8,262144]{1,0:T(8,128)(2,1)} %refs_1_.3, f32[16,4096]{1,0:T(8,128)} %refs_2_.3, ...), custom_call_target="tpu_custom_call" | custom-call | flops 12000000000 | bytes 6000000 | tf_op jit(solution)/shard_map/head/pallas_call | solution.py:201
  16.2 0.0 copy-start.5
  16.2 7.3 %all-to-all-start.1 = ((bf16[32,20,8,128]{3,2,1,0:T(8,128)(2,1)}), bf16[32,20,8,128]{3,2,1,0:T(8,128)(2,1)S(1)}, u32[]{:S(2)}, u32[]{:S(2)}) async-start(bf16[32,20,8,128]{3,2,1,0:T(8,128)(2,1)} %bitcast.71), calls=%async_computation.1 | async-start | bytes 2621440 | tf_op jit(solution)/shard_map/all_to_all | solution.py:501
  23.5 0.0 copy-done.5
  23.6 2.2 %collective-permute-start = (bf16[8,65536]{1,0:T(8,128)(2,1)S(1)}, bf16[8,65536]{1,0:T(8,128)(2,1)S(1)}, u32[]{:S(2)}, u32[]{:S(2)}) collective-permute-start(bf16[8,65536]{1,0:T(8,128)(2,1)S(1)} %copy-done.5), channel_id=1, source_target_pairs={{0,1},{2,3},{4,5},{6,7},{8,9},{10,11},{12,13},{14,15},{16,17},{18,... | collective-permute-start | bytes 3145736 | tf_op jit(solution)/shard_map/ppermute | solution.py:522
  25.8 2.2 %collective-permute-done.refs_0_ = bf16[8,65536]{1,0:T(8,128)(2,1)S(1)} collective-permute-done((bf16[8,65536]{1,0:T(8,128)(2,1)S(1)}, bf16[8,65536]{1,0:T(8,128)(2,1)S(1)}, u32[]{:S(2)}, u32[]{:S(2)}) %collective-permute-start) | collective-permute-done | bytes 1048608 | tf_op jit(solution)/shard_map/ppermute | solution.py:522
  28.0 0.0 copy-start.6
  28.0 1.0 copy-done.6
  29.0 16.2 %head.3 = (bf16[6,8,32,256]{3,2,1,0:T(8,128)(2,1)}, bf16[6,8,32,256]{3,2,1,0:T(8,128)(2,1)}, bf16[64,16,8,128]{3,2,1,0:T(8,128)(2,1)}) custom-call(bf16[8,65536]{1,0:T(8,128)(2,1)} %copy-done.6, bf16[8,262144]{1,0:T(8,128)(2,1)} %refs_1_.3, f32[16,4096]{1,0:T(8,128)} %refs_2_.3, bf16[16,256,256]{2,1,0:T(8,128)(2,1)} %constant.10.clone.refs_3_.wh_ref, ...), custom_call_target="tpu_custom_call" | custom-call | flops 12000000000 | bytes 6000000 | tf_op jit(solution)/shard_map/head/pallas_call | solution.py:201
  45.1 4.3 %channels_of.3 = bf16[64,16,8,128]{3,2,1,0:T(8,128)(2,1)} custom-call(bf16[6,8,32,256]{3,2,1,0:T(8,128)(2,1)} %get-tuple-element.17.ha_ref, bf16[6,8,32,256]{3,2,1,0:T(8,128)(2,1)} %get-tuple-element.18.la_ref, bf16[6,8,32,256]{3,2,1,0:T(8,128)(2,1)} %get-tuple-element.19.hb_ref, ...), custom_call_target="tpu_custom_call", output_to_operand_aliasing={{}: (6, {})} | custom-call | flops 2400000000 | bytes 3600000 | tf_op jit(solution)/shard_map/channels_of/pallas_call | solution.py:296
  49.5 6.2 %all-to-all-done.1 = bf16[32,20,8,128]{3,2,1,0:T(8,128)(2,1)S(1)} async-done(((bf16[32,20,8,128]{3,2,1,0:T(8,128)(2,1)}), bf16[32,20,8,128]{3,2,1,0:T(8,128)(2,1)S(1)}, u32[]{:S(2)}, u32[]{:S(2)}) %all-to-all-start.1) | async-done | bytes 1310752 | tf_op jit(solution)/shard_map/all_to_all | solution.py:501
  55.7 0.0 copy-start.1
  55.7 1.1 copy-done.1
  56.7 0.0 copy-start.4
  56.7 0.0 copy-start.3
  56.7 3.6 %all-to-all-start.2 = ((bf16[32,32,8,128]{3,2,1,0:T(8,128)(2,1)}), bf16[32,32,8,128]{3,2,1,0:T(8,128)(2,1)S(1)}, u32[]{:S(2)}, u32[]{:S(2)}) async-start(bf16[32,32,8,128]{3,2,1,0:T(8,128)(2,1)} %bitcast.70), calls=%async_computation.2 | async-start | bytes 4194304 | tf_op jit(solution)/shard_map/all_to_all | solution.py:501
  60.3 0.0 copy-done.4
  60.3 0.0 copy-done
  60.4 0.0 copy-done.3
  60.4 0.3 convolution_multiply_fusion
  60.7 0.1 fusion.3
  60.8 0.1 div.54
  60.9 0.1 div.55
  60.9 0.2 fusion.2
  61.1 0.2 fusion
  61.3 0.2 fusion.1
  61.5 0.2 multiply_reduce_fusion.2
  61.8 0.2 multiply_reduce_fusion.1
  62.0 0.2 multiply_reduce_fusion
  62.2 0.1 multiply_subtract_fusion.2
  62.2 0.6 subtract_divide_fusion
  62.9 0.2 select_maximum_fusion.refs_2_.refs_1_
  63.0 4.3 %channels_of.2 = bf16[64,6,8,128]{3,2,1,0:T(8,128)(2,1)} custom-call(bf16[6,8,32,256]{3,2,1,0:T(8,128)(2,1)} %get-tuple-element.17.ha_ref, bf16[6,8,32,256]{3,2,1,0:T(8,128)(2,1)} %get-tuple-element.18.la_ref, bf16[6,8,32,256]{3,2,1,0:T(8,128)(2,1)} %get-tuple-element.19.hb_ref, bf16[6,8,32,256]{3,2,1,0:T(8,128)(2,1)} %get-tuple-element.20.lb_ref, ...), custom_call_target="tpu_custom_call" | custom-call | flops 2400000000 | bytes 3600000 | tf_op jit(solution)/shard_map/channels_of/pallas_call | solution.py:296
  67.4 41.9 %all-to-all-done.2 = bf16[32,32,8,128]{3,2,1,0:T(8,128)(2,1)S(1)} async-done(((bf16[32,32,8,128]{3,2,1,0:T(8,128)(2,1)}), bf16[32,32,8,128]{3,2,1,0:T(8,128)(2,1)S(1)}, u32[]{:S(2)}, u32[]{:S(2)}) %all-to-all-start.2) | async-done | bytes 2097184 | tf_op jit(solution)/shard_map/all_to_all | solution.py:501
  109.2 4.0 %all-to-all-start = ((bf16[32,12,8,128]{3,2,1,0:T(8,128)(2,1)}), bf16[32,12,8,128]{3,2,1,0:T(8,128)(2,1)S(1)}, u32[]{:S(2)}, u32[]{:S(2)}) async-start(bf16[32,12,8,128]{3,2,1,0:T(8,128)(2,1)} %bitcast.72), calls=%async_computation | async-start | bytes 1572864 | tf_op jit(solution)/shard_map/all_to_all | solution.py:501
  113.2 0.0 copy-start.2
  113.2 1.3 copy-done.2
  114.6 10.9 %covariances.3.refs_2_ = f32[64,2,128,128]{3,2,1,0:T(8,128)} custom-call(bf16[16,2,32,8,128]{4,3,2,1,0:T(8,128)(2,1)S(1)} %bitcast.66, bf16[16,2,20,8,128]{4,3,2,1,0:T(8,128)(2,1)S(1)} %bitcast.69, f32[64,8,128]{2,1,0:T(8,128)S(1)} %select_maximum_fusion.refs_2_.refs_1_), custom_call_target="tpu_custom_call" | custom-call | flops 16000000000 | bytes 10000000 | tf_op jit(solution)/shard_map/covariances/pallas_call | solution.py:432
  125.4 5.3 %covariances.4.refs_2_ = f32[64,2,128,128]{3,2,1,0:T(8,128)} custom-call(bf16[16,2,32,8,128]{4,3,2,1,0:T(8,128)(2,1)S(1)} %bitcast.67, f32[64,8,128]{2,1,0:T(8,128)S(1)} %select_maximum_fusion.refs_2_.refs_1_, f32[64,2,128,128]{3,2,1,0:T(8,128)} %covariances.3.refs_2_), custom_call_target="tpu_custom_call", output_to_operand_aliasing={{}: (2, {})} | custom-call | flops 4800000000 | bytes 3000000 | tf_op jit(solution)/shard_map/covariances/pallas_call | solution.py:432
  130.7 3.1 %all-to-all-done = bf16[32,12,8,128]{3,2,1,0:T(8,128)(2,1)S(1)} async-done(((bf16[32,12,8,128]{3,2,1,0:T(8,128)(2,1)}), bf16[32,12,8,128]{3,2,1,0:T(8,128)(2,1)S(1)}, u32[]{:S(2)}, u32[]{:S(2)}) %all-to-all-start) | async-done | bytes 786464 | tf_op jit(solution)/shard_map/all_to_all | solution.py:501
  133.9 3.0 %covariances.5 = f32[64,2,128,128]{3,2,1,0:T(8,128)} custom-call(bf16[16,2,12,8,128]{4,3,2,1,0:T(8,128)(2,1)S(1)} %bitcast.68, f32[64,8,128]{2,1,0:T(8,128)S(1)} %select_maximum_fusion.refs_2_.refs_1_, f32[64,2,128,128]{3,2,1,0:T(8,128)} %covariances.4.refs_2_), custom_call_target="tpu_custom_call", output_to_operand_aliasing={{}: (2, {})} | custom-call | flops 4800000000 | bytes 3000000 | tf_op jit(solution)/shard_map/covariances/pallas_call | solution.py:432
  (6 shorter events, 0.0 us)
Async XLA Ops:
  0.0 60.3 %copy-start = (f32[8,128]{1,0:T(8,128)S(1)}, f32[8,128]{1,0:T(8,128)}, u32[]{:S(2)}) copy-start(f32[8,128]{1,0:T(8,128)} %param.9) | copy-start | bytes 12292
  16.2 7.3 %copy-start.5 = (bf16[8,65536]{1,0:T(8,128)(2,1)S(1)}, bf16[8,65536]{1,0:T(8,128)(2,1)}, u32[]{:S(2)}) copy-start(bf16[8,65536]{1,0:T(8,128)(2,1)} %get-tuple-element.16) | copy-start | bytes 3145732
  16.2 39.5 %all-to-all-start.1 = ((bf16[32,20,8,128]{3,2,1,0:T(8,128)(2,1)}), bf16[32,20,8,128]{3,2,1,0:T(8,128)(2,1)S(1)}, u32[]{:S(2)}, u32[]{:S(2)}) async-start(bf16[32,20,8,128]{3,2,1,0:T(8,128)(2,1)} %bitcast.71), calls=%async_computation.1 | async-start | bytes 2621440 | tf_op jit(solution)/shard_map/all_to_all | solution.py:501
  23.6 4.4 %collective-permute-start = (bf16[8,65536]{1,0:T(8,128)(2,1)S(1)}, bf16[8,65536]{1,0:T(8,128)(2,1)S(1)}, u32[]{:S(2)}, u32[]{:S(2)}) collective-permute-start(bf16[8,65536]{1,0:T(8,128)(2,1)S(1)} %copy-done.5), channel_id=1, source_target_pairs={{0,1},{2,3},{4,5},{6,7},{8,9},{10,11},{12,13},{14,15},{16,17},{18,... | collective-permute-start | bytes 3145736 | tf_op jit(solution)/shard_map/ppermute | solution.py:522
  28.0 1.0 copy-start.6
  55.7 1.1 copy-start.1
  56.7 3.6 %copy-start.4 = (s32[64]{0:T(128)S(1)}, s32[64]{0:T(128)}, u32[]{:S(2)}) copy-start(s32[64]{0:T(128)} %param.11) | copy-start | bytes 772
  56.7 3.6 %copy-start.3 = (s32[64,4]{0,1:T(4,128)S(1)}, s32[64,4]{0,1:T(4,128)}, u32[]{:S(2)}) copy-start(s32[64,4]{0,1:T(4,128)} %param.10) | copy-start | bytes 3076
  56.7 52.5 %all-to-all-start.2 = ((bf16[32,32,8,128]{3,2,1,0:T(8,128)(2,1)}), bf16[32,32,8,128]{3,2,1,0:T(8,128)(2,1)S(1)}, u32[]{:S(2)}, u32[]{:S(2)}) async-start(bf16[32,32,8,128]{3,2,1,0:T(8,128)(2,1)} %bitcast.70), calls=%async_computation.2 | async-start | bytes 4194304 | tf_op jit(solution)/shard_map/all_to_all | solution.py:501
  109.2 24.6 %all-to-all-start = ((bf16[32,12,8,128]{3,2,1,0:T(8,128)(2,1)}), bf16[32,12,8,128]{3,2,1,0:T(8,128)(2,1)S(1)}, u32[]{:S(2)}, u32[]{:S(2)}) async-start(bf16[32,12,8,128]{3,2,1,0:T(8,128)(2,1)} %bitcast.72), calls=%async_computation | async-start | bytes 1572864 | tf_op jit(solution)/shard_map/all_to_all | solution.py:501
  113.2 1.3 copy-start.2

commit v5 on v4

v5 whole, which is shorter than its diff:
```python
import functools
import math

import jax
import jax.numpy as jnp
import ml_dtypes
import numpy as np
from jax import lax
from jax.experimental import pallas as pl
from jax.experimental.pallas import tpu as pltpu
from jax.sharding import PartitionSpec as P

lanes = 128
octet = 8
frame_block = 16
epsilon = 1e-06
highest = lax.Precision.HIGHEST
f32 = jnp.float32
bf16 = jnp.bfloat16


def real_transform(x):
    size = len(x)
    if size == 2:
        return [(x[0] + x[1], None), (x[0] - x[1], None)]
    even = real_transform(x[0::2])
    odd = real_transform(x[1::2])
    half = size // 2
    bins = [None] * (half + 1)
    bins[0] = (even[0][0] + odd[0][0], None)
    bins[half] = (even[0][0] - odd[0][0], None)
    bins[half // 2] = (even[half // 2][0], -odd[half // 2][0])
    for k in range(1, half // 2):
        er, ei = even[k]
        o_r, oi = odd[k]
        c = math.cos(2 * math.pi * k / size)
        s = math.sin(2 * math.pi * k / size)
        if 4 * k == half:
            tr = (o_r + oi) * c
            ti = (oi - o_r) * c
        else:
            tr = o_r * c + oi * s
            ti = oi * c - o_r * s
        bins[k] = (er + tr, ei + ti)
        bins[half - k] = (er - tr, ti - ei)
    return bins


def split_two(x):
    high = x.astype(bf16)
    low = (x - high.astype(f32)).astype(bf16)
    return high, low


def split_three(x):
    high = x.astype(bf16).astype(f32)
    rest = x - high
    middle = rest.astype(bf16).astype(f32)
    return high, middle, rest - middle


def filter_frames(length, step, block_ref, taps_ref, high, low, filtered, sections, history):
    tap_count = taps_ref.shape[0]
    radix = length // lanes

    @pl.loop(0, radix)
    def _(part):
        spot = pl.multiple_of(part * lanes, lanes)
        taps = [
            jnp.broadcast_to(taps_ref[pl.ds(t, 1), pl.ds(spot, lanes)], (octet, lanes))
            for t in range(tap_count)
        ]
        past = tap_count - 1
        window = [history[part, j] for j in range(past)]
        for frame in range(frame_block):
            place = pl.multiple_of(spot + frame * length, lanes)
            window.append(block_ref[:, pl.ds(place, lanes)].astype(f32))
        for j in range(past):
            history[part, j] = window[frame_block + j]

        def convolve(weights, values):
            sums = []
            for j in range(len(values) - len(weights) + 1):
                total = weights[-1] * values[j]
                for i in range(1, len(weights)):
                    total = total + weights[-1 - i] * values[j + i]
                sums.append(total)
            return sums

        even_taps, odd_taps = taps[past::-2], taps[past - 1 :: -2]
        odd = window[0::2]
        even = window[1::2]
        evens = convolve(even_taps, even)
        odds = convolve(odd_taps, odd)
        both_taps = [one + two for one, two in zip(even_taps, odd_taps)]
        both = convolve(both_taps, [one + two for one, two in zip(even, odd[1:])])
        for j in range(frame_block // 2):
            pair = (evens[j] + odds[j], both[j] - evens[j] - odds[j + 1])
            for frame, total in zip((2 * j, 2 * j + 1), pair):
                filtered[part, frame * octet : (frame + 1) * octet, :] = total

    kept = pl.ds(pl.multiple_of(step * frame_block, frame_block), frame_block)

    @pl.loop(0, octet)
    def _(antenna):
        for half in range(frame_block // octet):
            rows = pl.ds(half * octet * octet + antenna, octet, stride=octet)
            bins = real_transform([filtered[part, rows, :] for part in range(radix)])
            here = pl.ds(half * octet, octet)
            sections[0, here, :] = bins[0][0]
            sections[1, here, :] = bins[radix // 2][0]
            for k in range(1, radix // 2):
                sections[2 * k, here, :] = bins[k][0]
                sections[2 * k + 1, here, :] = bins[k][1]
        for group in range(radix // 2):
            for side in range(2):
                first, second = split_two(sections[2 * group + side])
                high[group, antenna, kept, side * lanes : (side + 1) * lanes] = first
                low[group, antenna, kept, side * lanes : (side + 1) * lanes] = second


def second_stage(high, low, wave_high, wave_low):
    dot = functools.partial(jnp.dot, preferred_element_type=f32)
    return dot(high, wave_high) + (dot(low, wave_high) + dot(high, wave_low))


def divisor(*sizes, most=3):
    return max(n for n in range(1, most + 1) if all(size % n == 0 for size in sizes))


def swap(one, two, width):
    lane = lax.broadcasted_iota(jnp.int32, (1, lanes), 1)
    even = lax.rem(lane // width, 2) == 0
    return (
        jnp.where(even, one, pltpu.roll(two, width, 1)),
        jnp.where(even, pltpu.roll(one, lanes - width, 1), two),
    )


def head_kernel(length, steps, each, size, skipped, with_edge, *refs):
    before_ref, block_ref, taps_ref, wave_high_ref, wave_low_ref = refs[:5]
    refs = refs[5:]
    if with_edge:
        edge_out, refs = refs[0], refs[1:]
    out_ref, refs = refs[0], refs[1:]
    filtered, sections, history, turned, high, low, wave_high, wave_low, done = refs
    step = pl.program_id(0)
    frames = high.shape[2]
    radix = length // lanes
    kept = lanes // 2
    taken = pl.ds(2 * skipped, 2 * size)
    waves = [
        pltpu.make_async_copy(wave_high_ref.at[taken], wave_high, done.at[1]),
        pltpu.make_async_copy(wave_low_ref.at[taken], wave_low, done.at[2]),
    ]
    edge = pltpu.make_async_copy(block_ref, edge_out, done.at[0]) if with_edge else None

    @pl.when(step == 0)
    def _():
        for copy in waves:
            copy.start()
        past = history.shape[1]

        @pl.loop(0, radix)
        def _(part):
            for j in range(past):
                place = pl.multiple_of(part * lanes + (frame_block - past + j) * length, lanes)
                history[part, j] = before_ref[:, pl.ds(place, lanes)].astype(f32)

    @pl.when(step < steps)
    def _():
        filter_frames(
            length, step, block_ref, taps_ref, high, low, filtered, sections, history
        )

    if with_edge:

        @pl.when(step == steps - 1)
        def _():
            edge.start()

    @pl.when(step == steps)
    def _():
        for copy in waves:
            copy.wait()

    @pl.when(step >= steps)
    def _():
        rows = (octet * frames, 2 * lanes)
        totals = []
        for j in range(2 * each):
            at = (step - steps) * 2 * each + j
            pair = high[2 * skipped + at].reshape(rows), low[2 * skipped + at].reshape(rows)
            totals.append(second_stage(*pair, wave_high[at], wave_low[at]))
        for j in range(each):
            for block in range(steps):
                for a in range(0, octet, 2):
                    piece = []
                    for at in (a, a + 1):
                        begin = at * frames + block * frame_block
                        for total in totals[2 * j : 2 * j + 2]:
                            part = total[begin : begin + frame_block]
                            piece += [part[:, :lanes], part[:, lanes:]]
                    piece = jnp.concatenate(piece, axis=0).T
                    one, two = swap(piece[:kept], piece[kept:], kept)
                    turned[j * steps + block, pl.ds(a, kept, stride=octet), :] = one
                    turned[j * steps + block, pl.ds(a + 1, kept, stride=octet), :] = two
        for j in range(each * steps):
            out_ref[:, j] = turned[j].reshape(kept, octet, lanes).astype(bf16)

    if with_edge:

        @pl.when(step == pl.num_programs(0) - 1)
        def _():
            edge.wait()


def head(before, before_block, samples, taps, tables, first, steps, skipped, size, with_edge):
    length = taps.shape[1]
    radix = length // lanes
    groups = radix // 2
    kept = lanes // 2
    frames = steps * frame_block
    width = frame_block * length
    each = divisor(size, skipped, most=2 if steps == 1 else 1)
    anywhere = pl.BlockSpec(memory_space=pl.ANY)
    out_shape, out_specs = [], []
    if with_edge:
        out_shape.append(jax.ShapeDtypeStruct((octet, width), bf16))
        out_specs.append(anywhere)
    out_shape.append(jax.ShapeDtypeStruct((kept, size * steps, octet, lanes), bf16))
    out_specs.append(
        pl.BlockSpec(
            (kept, each * steps, octet, lanes), lambda i: (0, jnp.maximum(i - steps, 0), 0, 0)
        )
    )
    return pl.pallas_call(
        functools.partial(head_kernel, length, steps, each, size, skipped, with_edge),
        grid=(steps + size // each,),
        in_specs=[
            pl.BlockSpec((octet, width), lambda i: (0, before_block)),
            pl.BlockSpec((octet, width), lambda i: (0, first + jnp.minimum(i, steps - 1))),
            pl.BlockSpec(taps.shape, lambda i: (0, 0)),
            anywhere,
            anywhere,
        ],
        out_specs=out_specs,
        out_shape=out_shape,
        scratch_shapes=[
            pltpu.VMEM((radix, frame_block * octet, lanes), f32),
            pltpu.VMEM((radix, frame_block, lanes), f32),
            pltpu.VMEM((radix, taps.shape[0] - 1, octet, lanes), f32),
            pltpu.VMEM((each * steps, kept * octet, lanes), f32),
            pltpu.VMEM((groups, octet, frames, 2 * lanes), bf16),
            pltpu.VMEM((groups, octet, frames, 2 * lanes), bf16),
            pltpu.VMEM((2 * size, 2 * lanes, 2 * lanes), bf16),
            pltpu.VMEM((2 * size, 2 * lanes, 2 * lanes), bf16),
            pltpu.SemaphoreType.DMA((3,)),
        ],
        compiler_params=pltpu.CompilerParams(vmem_limit_bytes=later_vmem if skipped else head_vmem),
        cost_estimate=pl.CostEstimate(
            flops=steps * 1_000_000_000, bytes_accessed=steps * 1_000_000, transcendentals=0
        ),
        name="head",
    )(before, samples, taps, *tables)


def phase_tables(length):
    radix = length // lanes
    kept = lanes // 2
    q = np.arange(lanes)
    m = np.arange(kept)

    def waves(k):
        angle = 2 * np.pi * (np.outer(q, k + radix * m) % length) / length
        return np.cos(angle), np.sin(angle)

    zero = np.zeros((lanes, kept))
    (c, s), (oc, os) = waves(0), waves(radix // 2)
    tables = [np.block([[c, zero, -s, zero], [zero, oc, zero, -os]])]
    for k in range(1, radix // 2):
        (c, s), (oc, os) = waves(k), waves(radix - k)
        tables.append(np.block([[c, oc, -s, -os], [s, -os, c, -oc]]))
    tables = np.stack(tables).astype(np.float32)
    high = tables.astype(ml_dtypes.bfloat16)
    low = (tables - high.astype(np.float32)).astype(ml_dtypes.bfloat16)
    return high, low


def contract_last(left, right):
    return lax.dot_general(left, right, (((1,), (1,)), ((), ())), preferred_element_type=f32)


def covariance_kernel(place, scale, widths, *refs):
    x_refs, q_ref = refs[: len(widths)], refs[len(widths)]
    packed = len(widths) > 1
    out_ref, ready, done = refs[-3:]
    step = pl.program_id(0)
    steps = pl.num_programs(0)
    slot = lax.rem(step, 2)
    octets, shards = x_refs[0].shape[:2]
    antennas = octets * octet
    columns = x_refs[0].shape[2] // widths[0]
    count = columns * (4 if packed else 1)

    def copies(at, which):
        return [
            pltpu.make_async_copy(
                ready.at[which, j], out_ref.at[place(at * count + j)], done.at[which, j]
            )
            for j in range(count)
        ]

    @pl.when(step >= 2)
    def _():
        for copy in copies(step - 2, slot):
            copy.wait()

    def load(ref, t, j):
        if t >= shards:
            return jnp.zeros((antennas, lanes), f32)
        return ref[:, t, j].astype(f32).reshape(antennas, lanes)

    def channels(j):
        parts = [[] for _ in range(8 if packed else 2)]
        for t in range(0, shards, 2):
            tiles = [
                load(ref, u, j * width + at)
                for u in (t, t + 1)
                for ref, width in zip(x_refs, widths)
                for at in range(width)
            ]
            stride = len(tiles) // 2
            while stride:
                for low in range(len(tiles)):
                    if not low & stride:
                        tiles[low], tiles[low + stride] = swap(
                            tiles[low], tiles[low + stride], lanes * stride // len(tiles)
                        )
                stride //= 2
            for part, tile in zip(parts, tiles):
                part.append(tile)
        return [
            jnp.concatenate(real + imag, axis=1) for real, imag in zip(parts[0::2], parts[1::2])
        ]

    def turned(v):
        middle = v.shape[1] // 2
        return jnp.concatenate([v[:, middle:], -v[:, :middle]], axis=1)

    xs = [x for j in range(columns) for x in channels(j)]
    qs = [split_three(q_ref[place(step * count + at)]) for at in range(count)]
    zs = []
    for x, (qh, qm, ql) in zip(xs, qs):
        left = jnp.concatenate([qh, qm, ql, jnp.zeros_like(qh)], axis=0).astype(bf16)
        z = jnp.dot(left, x.astype(bf16), preferred_element_type=f32)
        zs.append(split_three(z[:octet] + z[octet : 2 * octet] + z[2 * octet : 3 * octet]))
    parts = []
    for x, (qh, qm, ql), (zh, zm, zl) in zip(xs, qs, zs):
        left = jnp.concatenate([qh, qh, qm, qm, qh, ql], axis=0).astype(bf16)
        right = jnp.concatenate([zh, zm, zh, zm, zl, zh], axis=0).astype(bf16)
        taken = lax.dot_general(left, right, (((0,), (0,)), ((), ())), preferred_element_type=f32)
        parts.append(split_two(x - taken))
    for at, ((high, low), copy) in enumerate(zip(parts, copies(step, slot))):
        left = jnp.concatenate([high, turned(high), low, turned(low)], axis=0)
        total = contract_last(left, jnp.concatenate([high, low], axis=0))
        total = total[:, :antennas] + total[:, antennas:]
        total = (total[: 2 * antennas] + total[2 * antennas :]) * scale
        ready[slot, at] = total.reshape(2, antennas, antennas)
        copy.start()

    @pl.when(step == steps - 1)
    def _():
        @pl.when(step >= 1)
        def _():
            for copy in copies(step - 1, 1 - slot):
                copy.wait()

        for copy in copies(step, slot):
            copy.wait()


def covariances(received, basis, place, frame_total, total, previous, last):
    array, runs, _, taken, _ = received[0]
    octets, shards = array.shape[:2]
    antennas = octets * octet
    widths = [one[4] for one in received]
    sizes = [n for a, r, begin, _, width in received for n in (a.shape[2] // (r * width), begin)]
    packed = len(received) > 1
    each = divisor(taken, *sizes, most=2 if packed else 8)
    count = each * (4 if packed else 1)
    steps = taken // each

    def window(array, runs, begin, _, width):
        stride = array.shape[2] // (runs * width * each)

        def index(i):
            run = i // steps
            return (0, 0, run * stride + begin // each + i - run * steps, 0, 0)

        return pl.BlockSpec((octets, shards, each * width, octet, lanes), index)

    in_specs = [window(*one) for one in received]
    in_specs.append(pl.BlockSpec(basis.shape, lambda i: (0, 0, 0)))
    operands = [*(one[0] for one in received), basis]
    aliases = {}
    if previous is not None:
        in_specs.append(pl.BlockSpec(memory_space=pl.ANY))
        aliases = {len(operands): 0}
        operands.append(previous)
    return pl.pallas_call(
        functools.partial(covariance_kernel, place, 1.0 / frame_total, widths),
        grid=(runs * steps,),
        in_specs=in_specs,
        out_specs=pl.BlockSpec(memory_space=pl.ANY),
        out_shape=jax.ShapeDtypeStruct((total, 2, antennas, antennas), f32),
        scratch_shapes=[
            pltpu.VMEM((2, count, 2, antennas, antennas), f32),
            pltpu.SemaphoreType.DMA((2, count)),
        ],
        input_output_aliases=aliases,
        compiler_params=pltpu.CompilerParams(vmem_limit_bytes=last_vmem if last else covariance_vmem),
        cost_estimate=pl.CostEstimate(
            flops=runs * steps * count * 200_000_000,
            bytes_accessed=runs * steps * count * 200_000,
            transcendentals=0,
        ),
        name="covariances",
    )(*operands)


def orthonormal(vectors):
    found = []
    for column in range(vectors.shape[1]):
        residue = vectors[:, column, :]
        for earlier in found:
            residue = residue - earlier * jnp.sum(earlier * residue, axis=-1, keepdims=True)
        found.append(
            residue / jnp.sqrt(jnp.sum(residue * residue, axis=-1, keepdims=True) + epsilon)
        )
    return jnp.stack(found, axis=1)


def basis_of(chosen, counted, steering):
    count, slots = chosen.shape
    directions = steering.shape[0]
    onehot = (
        chosen[:, :, None] == lax.broadcasted_iota(jnp.int32, (count, slots, directions), 2)
    ).astype(f32)
    live = (lax.broadcasted_iota(jnp.int32, (count, slots), 1) < counted[:, None]).astype(f32)
    vectors = jnp.einsum("crn,na->cra", onehot, steering, precision=highest) * live[:, :, None]
    basis = orthonormal(vectors)
    return jnp.pad(basis, ((0, 0), (0, octet - slots), (0, 0)))


def per_device(samples, taps, steering, interferer_ids, ranks):
    antennas, width = samples.shape
    length = taps.shape[1]
    frames = width // length
    radix = length // lanes
    groups = radix // 2
    kept = lanes // 2
    shards = lax.axis_size("tm")
    spread = lax.axis_size("chan")
    devices = spread * shards
    owned = interferer_ids.shape[0]
    frame_total = frames * shards

    padded = samples
    if antennas < octet:
        padded = jnp.pad(samples, ((0, octet - antennas), (0, 0)))
    tables = [jnp.asarray(table) for table in phase_tables(length)]
    blocks = frames // frame_block
    whole_runs = owned % radix == 0
    runs = owned // radix
    twos = groups // 2
    cuts = (twos - last_twos, last_twos) if whole_runs else (twos,)

    def exchange(spectra):
        received = lax.all_to_all(spectra, ("chan", "tm"), split_axis=0, concat_axis=0, tiled=True)
        received = received.reshape(spread, shards, -1, antennas, lanes)
        if antennas < octet:
            received = received.transpose(1, 2, 0, 3, 4).reshape(
                shards, -1, spread * antennas // octet, octet, lanes
            ).transpose(2, 0, 1, 3, 4)
        return received

    def channel_at(first, count):
        def place(index):
            run = index // (4 * count)
            two = (index - run * (4 * count)) // 4
            group = 2 * (first + two) + index % 2
            mirrored = jnp.where(group == 0, groups, radix - group)
            return run * radix + jnp.where(index % 4 < 2, group, mirrored)

        return place

    edge, early = head(padded, blocks - 2, padded, taps, tables, blocks - 1, 1, 0, twos, True)
    before = lax.ppermute(edge, "tm", [(i, i + 1) for i in range(shards - 1)])
    if whole_runs:
        arrived = exchange(early.reshape(devices, -1, octet, lanes))
    basis = basis_of(interferer_ids, ranks, steering)

    def later(first, count):
        return head(before, 0, padded, taps, tables, 0, blocks - 1, first, count, False)[0]

    out = None
    if whole_runs:
        first = 0
        pieces = []
        for count in cuts:
            if first:
                before, basis = lax.optimization_barrier((before, basis))
            sent = later(first, count).reshape(devices, -1, octet, lanes)
            if not first:
                sent, arrived = lax.optimization_barrier((sent, arrived))
            pieces.append((exchange(sent), first, count))
            first += count
        for received, first, count in pieces:
            parts = (
                (received, runs, 0, count, blocks - 1),
                (arrived, runs, first, count, 1),
            )
            out = covariances(
                parts, basis, channel_at(first, count), frame_total, owned, out, first > 0
            )
    else:
        tiles = jnp.concatenate(
            [
                later(0, twos).reshape(kept, twos, blocks - 1, octet, 4, 2, frame_block),
                early.reshape(kept, twos, 1, octet, 4, 2, frame_block),
            ],
            axis=2,
        )
        tiles = tiles.transpose(0, 1, 4, 3, 5, 2, 6).reshape(kept, radix, octet, lanes)
        order = [
            k
            for g in range(0, groups, 2)
            for k in (g, g + 1, radix - g if g else groups, radix - g - 1)
        ]
        tiles = tiles[:, np.argsort(order), :antennas].reshape(devices, owned, antennas, lanes)
        received = exchange(tiles)
        parts = ((received, 1, 0, owned, 1),)
        out = covariances(parts, basis, lambda index: index, frame_total, owned, None, True)
    return out


last_twos = 2
head_vmem = 56 * 1024 * 1024
later_vmem = 32 * 1024 * 1024
covariance_vmem = 24 * 1024 * 1024
last_vmem = 24 * 1024 * 1024


def solution(mesh):
    in_specs = (P("chan", "tm"), P(), P(), P(("chan", "tm"), None), P(("chan", "tm")))
    out_specs = P(("chan", "tm"), None, None, None)
    return jax.shard_map(
        per_device, mesh=mesh, in_specs=in_specs, out_specs=out_specs, check_vma=False
    )
```

time: 138 us -> 132 us (0.957)
  waiting for transfers between devices: 53.4 us -> 43.6 us
  local copies, waits for them, and re-layouts: 3.46 us -> 7.9 us
  starting transfers between devices: 17.1 us -> 19 us
  Pallas kernels: 60.1 us -> 58.7 us
    all_to_all x3, waiting for transfers between devices: 51.2 us -> 41.2 us  [exchange(): lax.all_to_all(spectra, ('chan', 'tm'), split_axis=0, concat_axis=0, tile...]
    unnamed x14 -> x20, local copies, waits for them, and re-layouts: 3.38 us -> 7.82 us
    pallas_call x3 -> x2, Pallas kernels: 19.1 us -> 15.2 us  [covariances(): pl.pallas_call(functools.partial(covariance_kernel, place, 1.0 / frame_to...]
    pallas_call x4 -> x3, Pallas kernels: 41 us -> 43.5 us  [head(): pl.pallas_call(functools.partial(head_kernel, length, steps, each, size,...]
    all_to_all x3, starting transfers between devices: 14.9 us -> 16.8 us  [exchange(): lax.all_to_all(spectra, ('chan', 'tm'), split_axis=0, concat_axis=0, tile...]
  transfers between devices with their start and end apart: 4 -> 4, of which waited for: 4 -> 4; matrix products, arithmetic and copies ran while one was open for 2% -> 2% of each run, Pallas kernels for 30% -> 34%
where the time goes in v5:
time: 132 us
  Pallas kernels  58.7 us (44%)
  waiting for transfers between devices  43.6 us (33%)
  starting transfers between devices  19 us (14%)
  local copies, waits for them, and re-layouts  7.9 us (6%)
  other arithmetic  2.22 us (2%)
    pallas_call x3, Pallas kernels, head(): pl.pallas_call(functools.partial(head_kernel, length, steps, each, size,...  43.5 us
    all_to_all x3, waiting for transfers between devices, exchange(): lax.all_to_all(spectra, ('chan', 'tm'), split_axis=0, concat_axis=0, tile...  41.2 us
    all_to_all x3, starting transfers between devices, exchange(): lax.all_to_all(spectra, ('chan', 'tm'), split_axis=0, concat_axis=0, tile...  16.8 us
    pallas_call x2, Pallas kernels, covariances(): pl.pallas_call(functools.partial(covariance_kernel, place, 1.0 / frame_to...  15.2 us
    unnamed x20, local copies, waits for them, and re-layouts  7.82 us
  transfers between devices with their start and end apart: 4, of which 4 were waited for; matrix products, arithmetic and copies ran while one was open for 2% of the time, Pallas kernels for 34%

profile of v5, /device:TPU:0, one launch (start us, length us, event | category | flops | bytes accessed | tf_op | source)
XLA Modules:
  0.0 131.9 jit_solution(8171766172537365230)
XLA Ops:
  0.0 0.0 copy-start
  0.0 9.7 %head.3 = (bf16[8,65536]{1,0:T(8,128)(2,1)}, bf16[64,8,8,128]{3,2,1,0:T(8,128)(2,1)}) custom-call(bf16[8,262144]{1,0:T(8,128)(2,1)} %refs_1_.5, bf16[8,262144]{1,0:T(8,128)(2,1)} %refs_1_.5, f32[16,4096]{1,0:T(8,128)} %refs_2_.5, bf16[16,256,256]{2,1,0:T(8,128)(2,1)} %constant.10.clone.refs_3_, bf16[16,256,256]{2,1,0:T(8,128)(2,1)} %constant.11.clone.refs_4_), custom_call_target="tpu_custom_call" | custom-call | flops 1000000000 | bytes 1000000 | tf_op jit(solution)/shard_map/head/pallas_call | solution.py:237
  9.8 7.3 %all-to-all-start.1 = ((bf16[32,16,8,128]{3,2,1,0:T(8,128)(2,1)}), bf16[32,16,8,128]{3,2,1,0:T(8,128)(2,1)S(1)}, u32[]{:S(2)}, u32[]{:S(2)}) async-start(bf16[32,16,8,128]{3,2,1,0:T(8,128)(2,1)} %bitcast.71), calls=%async_computation.1 | async-start | bytes 2097152 | tf_op jit(solution)/shard_map/all_to_all | solution.py:480
  17.1 2.2 %collective-permute-start = (bf16[8,65536]{1,0:T(8,128)(2,1)}, bf16[8,65536]{1,0:T(8,128)(2,1)S(1)}, u32[]{:S(2)}, u32[]{:S(2)}) collective-permute-start(bf16[8,65536]{1,0:T(8,128)(2,1)} %get-tuple-element.11), channel_id=1, source_target_pairs={{0,1},{2,3},{4,5},{6,7},{8,9},{10,11},{12,13},{14,15},{16,17},{18,... | collective-permute-start | bytes 3145736 | tf_op jit(solution)/shard_map/ppermute | solution.py:499
  19.3 2.4 %collective-permute-done.refs_0_ = bf16[8,65536]{1,0:T(8,128)(2,1)S(1)} collective-permute-done((bf16[8,65536]{1,0:T(8,128)(2,1)}, bf16[8,65536]{1,0:T(8,128)(2,1)S(1)}, u32[]{:S(2)}, u32[]{:S(2)}) %collective-permute-start) | collective-permute-done | bytes 1048608 | tf_op jit(solution)/shard_map/ppermute | solution.py:499
  21.7 0.0 copy-start.4
  21.7 1.0 copy-done.4
  22.7 20.2 %head.5 = bf16[64,18,8,128]{3,2,1,0:T(8,128)(2,1)} custom-call(bf16[8,65536]{1,0:T(8,128)(2,1)} %copy-done.4, bf16[8,262144]{1,0:T(8,128)(2,1)} %refs_1_.5, f32[16,4096]{1,0:T(8,128)} %refs_2_.5, bf16[16,256,256]{2,1,0:T(8,128)(2,1)} %constant.10.clone.refs_3_, bf16[16,256,256]{2,1,0:T(8,128)(2,1)} %constant.11.clone.refs_4_), custom_call_target="tpu_custom_call" | custom-call | flops 3000000000 | bytes 3000000 | tf_op jit(solution)/shard_map/head/pallas_call | solution.py:237
  42.9 0.4 all-to-all-done.1
  43.3 0.0 copy-start.9
  43.3 0.0 copy-start.8
  43.3 0.0 copy-start.2
  43.3 5.5 %all-to-all-start.2 = ((bf16[32,36,8,128]{3,2,1,0:T(8,128)(2,1)}), bf16[32,36,8,128]{3,2,1,0:T(8,128)(2,1)}, u32[]{:S(2)}, u32[]{:S(2)}) async-start(bf16[32,36,8,128]{3,2,1,0:T(8,128)(2,1)} %bitcast.70), calls=%async_computation.2 | async-start | bytes 4718592 | tf_op jit(solution)/shard_map/all_to_all | solution.py:480
  48.8 0.0 copy-done.9
  48.8 0.0 copy-done
  48.8 0.0 copy-done.8
  48.8 0.3 convolution_multiply_fusion
  49.1 0.1 fusion.3
  49.3 0.1 div.54
  49.3 0.1 div.55
  49.4 0.2 fusion.2
  49.6 0.2 fusion
  49.8 0.2 fusion.1
  50.0 0.2 multiply_reduce_fusion.2
  50.2 0.2 multiply_reduce_fusion.1
  50.4 0.2 multiply_reduce_fusion
  50.6 0.1 multiply_subtract_fusion.2
  50.7 0.6 subtract_divide_fusion
  51.3 0.2 select_maximum_fusion.refs_2_
  51.5 0.0 copy-done.2
  51.5 0.0 copy-start.1
  51.5 2.2 %copy-done.1 = bf16[8,262144]{1,0:T(8,128)(2,1)S(1)} copy-done((bf16[8,262144]{1,0:T(8,128)(2,1)S(1)}, bf16[8,262144]{1,0:T(8,128)(2,1)}, u32[]{:S(2)}) %copy-start.1) | copy-done | bytes 4194328
  53.7 0.0 copy-start.3
  53.7 1.6 %copy-done.3 = bf16[16,256,256]{2,1,0:T(8,128)(2,1)S(1)} copy-done((bf16[16,256,256]{2,1,0:T(8,128)(2,1)S(1)}, bf16[16,256,256]{2,1,0:T(8,128)(2,1)}, u32[]{:S(2)}) %copy-start.3) | copy-done | bytes 2097176
  55.3 0.0 copy-start.5
  55.3 1.2 copy-done.5
  56.5 0.0 copy-start.6
  56.5 0.9 copy-done.6
  57.5 13.6 %head.4 = bf16[64,6,8,128]{3,2,1,0:T(8,128)(2,1)S(1)} custom-call(bf16[8,65536]{1,0:T(8,128)(2,1)S(1)} %copy-done.5, bf16[8,262144]{1,0:T(8,128)(2,1)S(1)} %copy-done.1, f32[16,4096]{1,0:T(8,128)S(1)} %copy-done.6, bf16[16,256,256]{2,1,0:T(8,128)(2,1)S(1)} %copy-done.3, bf16[16,256,256]{2,1,0:T(8,128)(2,1)S(1)} %copy-done.2), custom_call_target="tpu_custom_call" | custom-call | flops 3000000000 | bytes 3000000 | tf_op jit(solution)/shard_map/head/pallas_call | solution.py:237
  71.1 0.0 copy-start.7
  71.1 0.9 copy-done.7
  72.0 31.4 %all-to-all-done.2 = bf16[32,36,8,128]{3,2,1,0:T(8,128)(2,1)} async-done(((bf16[32,36,8,128]{3,2,1,0:T(8,128)(2,1)}), bf16[32,36,8,128]{3,2,1,0:T(8,128)(2,1)}, u32[]{:S(2)}, u32[]{:S(2)}) %all-to-all-start.2) | async-done | bytes 2359328 | tf_op jit(solution)/shard_map/all_to_all | solution.py:480
  103.3 4.0 %all-to-all-start = ((bf16[32,12,8,128]{3,2,1,0:T(8,128)(2,1)}), bf16[32,12,8,128]{3,2,1,0:T(8,128)(2,1)S(1)}, u32[]{:S(2)}, u32[]{:S(2)}) async-start(bf16[32,12,8,128]{3,2,1,0:T(8,128)(2,1)} %bitcast.69), calls=%async_computation | async-start | bytes 1572864 | tf_op jit(solution)/shard_map/all_to_all | solution.py:480
  107.3 11.2 %covariances.2.refs_3_ = f32[64,2,128,128]{3,2,1,0:T(8,128)} custom-call(bf16[16,2,36,8,128]{4,3,2,1,0:T(8,128)(2,1)} %bitcast.15.refs_0_, bf16[16,2,16,8,128]{4,3,2,1,0:T(8,128)(2,1)S(1)} %bitcast.66, f32[64,8,128]{2,1,0:T(8,128)S(1)} %select_maximum_fusion.refs_2_), custom_call_target="tpu_custom_call" | custom-call | flops 9600000000 | bytes 9600000 | tf_op jit(solution)/shard_map/covariances/pallas_call | solution.py:411
  118.6 9.4 %all-to-all-done = bf16[32,12,8,128]{3,2,1,0:T(8,128)(2,1)S(1)} async-done(((bf16[32,12,8,128]{3,2,1,0:T(8,128)(2,1)}), bf16[32,12,8,128]{3,2,1,0:T(8,128)(2,1)S(1)}, u32[]{:S(2)}, u32[]{:S(2)}) %all-to-all-start) | async-done | bytes 786464 | tf_op jit(solution)/shard_map/all_to_all | solution.py:480
  127.9 4.0 %covariances.3 = f32[64,2,128,128]{3,2,1,0:T(8,128)} custom-call(bf16[16,2,12,8,128]{4,3,2,1,0:T(8,128)(2,1)S(1)} %bitcast.68, bf16[16,2,16,8,128]{4,3,2,1,0:T(8,128)(2,1)S(1)} %bitcast.67, f32[64,8,128]{2,1,0:T(8,128)S(1)} %select_maximum_fusion.refs_2_, f32[64,2,128,128]{3,2,1,0:T(8,128)} %covariances.2.refs_3_), custom_call_target="tpu_custom_call", output_to_operand_aliasing={{}: (3, {})} | custom-call | flops 3200000000 | bytes 3200000 | tf_op jit(solution)/shard_map/covariances/pallas_call | solution.py:411
  (6 shorter events, 0.0 us)
Async XLA Ops:
  0.0 48.8 %copy-start = (f32[8,128]{1,0:T(8,128)S(1)}, f32[8,128]{1,0:T(8,128)}, u32[]{:S(2)}) copy-start(f32[8,128]{1,0:T(8,128)} %param.9) | copy-start | bytes 12292
  9.8 33.6 %all-to-all-start.1 = ((bf16[32,16,8,128]{3,2,1,0:T(8,128)(2,1)}), bf16[32,16,8,128]{3,2,1,0:T(8,128)(2,1)S(1)}, u32[]{:S(2)}, u32[]{:S(2)}) async-start(bf16[32,16,8,128]{3,2,1,0:T(8,128)(2,1)} %bitcast.71), calls=%async_computation.1 | async-start | bytes 2097152 | tf_op jit(solution)/shard_map/all_to_all | solution.py:480
  17.1 4.6 %collective-permute-start = (bf16[8,65536]{1,0:T(8,128)(2,1)}, bf16[8,65536]{1,0:T(8,128)(2,1)S(1)}, u32[]{:S(2)}, u32[]{:S(2)}) collective-permute-start(bf16[8,65536]{1,0:T(8,128)(2,1)} %get-tuple-element.11), channel_id=1, source_target_pairs={{0,1},{2,3},{4,5},{6,7},{8,9},{10,11},{12,13},{14,15},{16,17},{18,... | collective-permute-start | bytes 3145736 | tf_op jit(solution)/shard_map/ppermute | solution.py:499
  21.7 1.0 copy-start.4
  43.3 5.5 %copy-start.9 = (s32[64]{0:T(128)S(1)}, s32[64]{0:T(128)}, u32[]{:S(2)}) copy-start(s32[64]{0:T(128)} %param.11) | copy-start | bytes 772
  43.3 5.5 %copy-start.8 = (s32[64,4]{0,1:T(4,128)S(1)}, s32[64,4]{0,1:T(4,128)}, u32[]{:S(2)}) copy-start(s32[64,4]{0,1:T(4,128)} %param.10) | copy-start | bytes 3076
  43.3 8.2 %copy-start.2 = (bf16[16,256,256]{2,1,0:T(8,128)(2,1)S(1)}, bf16[16,256,256]{2,1,0:T(8,128)(2,1)}, u32[]{:S(2)}) copy-start(bf16[16,256,256]{2,1,0:T(8,128)(2,1)} %constant.11.clone.refs_4_) | copy-start | bytes 6291460
  43.3 60.0 %all-to-all-start.2 = ((bf16[32,36,8,128]{3,2,1,0:T(8,128)(2,1)}), bf16[32,36,8,128]{3,2,1,0:T(8,128)(2,1)}, u32[]{:S(2)}, u32[]{:S(2)}) async-start(bf16[32,36,8,128]{3,2,1,0:T(8,128)(2,1)} %bitcast.70), calls=%async_computation.2 | async-start | bytes 4718592 | tf_op jit(solution)/shard_map/all_to_all | solution.py:480
  51.5 2.2 %copy-start.1 = (bf16[8,262144]{1,0:T(8,128)(2,1)S(1)}, bf16[8,262144]{1,0:T(8,128)(2,1)}, u32[]{:S(2)}) copy-start(bf16[8,262144]{1,0:T(8,128)(2,1)} %refs_1_.5) | copy-start | bytes 12582916
  53.7 1.6 %copy-start.3 = (bf16[16,256,256]{2,1,0:T(8,128)(2,1)S(1)}, bf16[16,256,256]{2,1,0:T(8,128)(2,1)}, u32[]{:S(2)}) copy-start(bf16[16,256,256]{2,1,0:T(8,128)(2,1)} %constant.10.clone.refs_3_) | copy-start | bytes 6291460
  55.3 1.2 copy-start.5
  56.5 0.9 copy-start.6
  71.1 0.9 copy-start.7
  103.3 24.6 %all-to-all-start = ((bf16[32,12,8,128]{3,2,1,0:T(8,128)(2,1)}), bf16[32,12,8,128]{3,2,1,0:T(8,128)(2,1)S(1)}, u32[]{:S(2)}, u32[]{:S(2)}) async-start(bf16[32,12,8,128]{3,2,1,0:T(8,128)(2,1)} %bitcast.69), calls=%async_computation | async-start | bytes 1572864 | tf_op jit(solution)/shard_map/all_to_all | solution.py:480

commit v6 on v5

--- a/solution.py
+++ b/solution.py
@@ -59,11 +59,11 @@
     return high, middle, rest - middle
 
 
-def filter_frames(length, step, block_ref, taps_ref, high, low, filtered, sections, history):
+def filter_frames(length, step, before_ref, block_ref, taps_ref, high, low, filtered, sections, history):
     tap_count = taps_ref.shape[0]
     radix = length // lanes
 
-    @pl.loop(0, radix)
+    @pl.loop(0, radix, unroll=2)
     def _(part):
         spot = pl.multiple_of(part * lanes, lanes)
         taps = [
@@ -71,12 +71,21 @@
             for t in range(tap_count)
         ]
         past = tap_count - 1
-        window = [history[part, j] for j in range(past)]
-        for frame in range(frame_block):
-            place = pl.multiple_of(spot + frame * length, lanes)
-            window.append(block_ref[:, pl.ds(place, lanes)].astype(f32))
-        for j in range(past):
-            history[part, j] = window[frame_block + j]
+
+        def frames_of(ref, begin):
+            places = [spot + frame * length for frame in range(begin, frame_block)]
+            return [
+                ref[:, pl.ds(pl.multiple_of(place, lanes), lanes)].astype(f32) for place in places
+            ]
+
+        if history is None:
+            window = frames_of(before_ref, frame_block - past)
+        else:
+            window = [history[part, j] for j in range(past)]
+        window += frames_of(block_ref, 0)
+        if history is not None:
+            for j in range(past):
+                history[part, j] = window[frame_block + j]
 
         def convolve(weights, values):
             sums = []
@@ -159,18 +168,29 @@
     def _():
         for copy in waves:
             copy.start()
-        past = history.shape[1]
-
-        @pl.loop(0, radix)
-        def _(part):
-            for j in range(past):
-                place = pl.multiple_of(part * lanes + (frame_block - past + j) * length, lanes)
-                history[part, j] = before_ref[:, pl.ds(place, lanes)].astype(f32)
+        if steps > 1:
+            past = history.shape[1]
+
+            @pl.loop(0, radix, unroll=4)
+            def _(part):
+                for j in range(past):
+                    place = part * lanes + (frame_block - past + j) * length
+                    place = pl.ds(pl.multiple_of(place, lanes), lanes)
+                    history[part, j] = before_ref[:, place].astype(f32)
 
     @pl.when(step < steps)
     def _():
         filter_frames(
-            length, step, block_ref, taps_ref, high, low, filtered, sections, history
+            length,
+            step,
+            before_ref,
+            block_ref,
+            taps_ref,
+            high,
+            low,
+            filtered,
+            sections,
+            history if steps > 1 else None,
         )
 
     if with_edge:
@@ -222,7 +242,7 @@
     kept = lanes // 2
     frames = steps * frame_block
     width = frame_block * length
-    each = divisor(size, skipped, most=2 if steps == 1 else 1)
+    each = divisor(size, skipped, most=4 if steps == 1 else 2)
     anywhere = pl.BlockSpec(memory_space=pl.ANY)
     out_shape, out_specs = [], []
     if with_edge:
@@ -362,10 +382,12 @@
         taken = lax.dot_general(left, right, (((0,), (0,)), ((), ())), preferred_element_type=f32)
         parts.append(split_two(x - taken))
     for at, ((high, low), copy) in enumerate(zip(parts, copies(step, slot))):
-        left = jnp.concatenate([high, turned(high), low, turned(low)], axis=0)
+        left = jnp.concatenate([high, turned(high)], axis=0)
         total = contract_last(left, jnp.concatenate([high, low], axis=0))
-        total = total[:, :antennas] + total[:, antennas:]
-        total = (total[: 2 * antennas] + total[2 * antennas :]) * scale
+        same, cross = total[:, :antennas], total[:, antennas:]
+        real, imag = cross[:antennas], cross[antennas:]
+        cross = jnp.concatenate([real + real.T, imag - imag.T], axis=0)
+        total = (same + cross) * scale
         ready[slot, at] = total.reshape(2, antennas, antennas)
         copy.start()
 

time: 132 us -> 129 us (0.977)
  Pallas kernels: 58.7 us -> 52.7 us
  waiting for transfers between devices: 43.6 us -> 47.9 us
  starting transfers between devices: 19 us -> 17.3 us
    pallas_call x3, Pallas kernels: 43.5 us -> 38.6 us  [head(): pl.pallas_call(functools.partial(head_kernel, length, steps, each, size,...]
    all_to_all x3, waiting for transfers between devices: 41.2 us -> 45.5 us  [exchange(): lax.all_to_all(spectra, ('chan', 'tm'), split_axis=0, concat_axis=0, tile...]
    all_to_all x3, starting transfers between devices: 16.8 us -> 15.1 us  [exchange(): lax.all_to_all(spectra, ('chan', 'tm'), split_axis=0, concat_axis=0, tile...]
  transfers between devices with their start and end apart: 4 -> 4, of which waited for: 4 -> 4; matrix products, arithmetic and copies ran while one was open for 2% -> 2% of each run, Pallas kernels for 34% -> 32%
where the time goes in v6:
time: 129 us
  Pallas kernels  52.7 us (41%)
  waiting for transfers between devices  47.9 us (37%)
  starting transfers between devices  17.3 us (13%)
  local copies, waits for them, and re-layouts  7.9 us (6%)
  other arithmetic  2.22 us (2%)
    all_to_all x3, waiting for transfers between devices, exchange(): lax.all_to_all(spectra, ('chan', 'tm'), split_axis=0, concat_axis=0, tile...  45.5 us
    pallas_call x3, Pallas kernels, head(): pl.pallas_call(functools.partial(head_kernel, length, steps, each, size,...  38.6 us
    all_to_all x3, starting transfers between devices, exchange(): lax.all_to_all(spectra, ('chan', 'tm'), split_axis=0, concat_axis=0, tile...  15.1 us
    pallas_call x2, Pallas kernels, covariances(): pl.pallas_call(functools.partial(covariance_kernel, place, 1.0 / frame_to...  14.1 us
    unnamed x20, local copies, waits for them, and re-layouts  7.82 us
  transfers between devices with their start and end apart: 4, of which 4 were waited for; matrix products, arithmetic and copies ran while one was open for 2% of the time, Pallas kernels for 32%

profile of v6, /device:TPU:0, one launch (start us, length us, event | category | flops | bytes accessed | tf_op | source)
XLA Modules:
  0.0 128.5 jit_solution(9922000940942206394)
XLA Ops:
  0.0 0.0 copy-start
  0.0 8.3 %head.3 = (bf16[8,65536]{1,0:T(8,128)(2,1)}, bf16[64,8,8,128]{3,2,1,0:T(8,128)(2,1)}) custom-call(bf16[8,262144]{1,0:T(8,128)(2,1)} %refs_1_.5, bf16[8,262144]{1,0:T(8,128)(2,1)} %refs_1_.5, f32[16,4096]{1,0:T(8,128)} %refs_2_.5, bf16[16,256,256]{2,1,0:T(8,128)(2,1)} %constant.10.clone.refs_3_, bf16[16,256,256]{2,1,0:T(8,128)(2,1)} %constant.11.clone.refs_4_), custom_call_target="tpu_custom_call" | custom-call | flops 1000000000 | bytes 1000000 | tf_op jit(solution)/shard_map/head/pallas_call | solution.py:257
  8.3 7.3 %all-to-all-start.1 = ((bf16[32,16,8,128]{3,2,1,0:T(8,128)(2,1)}), bf16[32,16,8,128]{3,2,1,0:T(8,128)(2,1)S(1)}, u32[]{:S(2)}, u32[]{:S(2)}) async-start(bf16[32,16,8,128]{3,2,1,0:T(8,128)(2,1)} %bitcast.71), calls=%async_computation.1 | async-start | bytes 2097152 | tf_op jit(solution)/shard_map/all_to_all | solution.py:502
  15.6 2.2 %collective-permute-start = (bf16[8,65536]{1,0:T(8,128)(2,1)}, bf16[8,65536]{1,0:T(8,128)(2,1)S(1)}, u32[]{:S(2)}, u32[]{:S(2)}) collective-permute-start(bf16[8,65536]{1,0:T(8,128)(2,1)} %get-tuple-element.11), channel_id=1, source_target_pairs={{0,1},{2,3},{4,5},{6,7},{8,9},{10,11},{12,13},{14,15},{16,17},{18,... | collective-permute-start | bytes 3145736 | tf_op jit(solution)/shard_map/ppermute | solution.py:521
  17.9 2.4 %collective-permute-done.refs_0_ = bf16[8,65536]{1,0:T(8,128)(2,1)S(1)} collective-permute-done((bf16[8,65536]{1,0:T(8,128)(2,1)}, bf16[8,65536]{1,0:T(8,128)(2,1)S(1)}, u32[]{:S(2)}, u32[]{:S(2)}) %collective-permute-start) | collective-permute-done | bytes 1048608 | tf_op jit(solution)/shard_map/ppermute | solution.py:521
  20.3 0.0 copy-start.4
  20.3 1.0 copy-done.4
  21.3 17.9 %head.5 = bf16[64,18,8,128]{3,2,1,0:T(8,128)(2,1)} custom-call(bf16[8,65536]{1,0:T(8,128)(2,1)} %copy-done.4, bf16[8,262144]{1,0:T(8,128)(2,1)} %refs_1_.5, f32[16,4096]{1,0:T(8,128)} %refs_2_.5, bf16[16,256,256]{2,1,0:T(8,128)(2,1)} %constant.10.clone.refs_3_, bf16[16,256,256]{2,1,0:T(8,128)(2,1)} %constant.11.clone.refs_4_), custom_call_target="tpu_custom_call" | custom-call | flops 3000000000 | bytes 3000000 | tf_op jit(solution)/shard_map/head/pallas_call | solution.py:257
  39.2 2.7 %all-to-all-done.1 = bf16[32,16,8,128]{3,2,1,0:T(8,128)(2,1)S(1)} async-done(((bf16[32,16,8,128]{3,2,1,0:T(8,128)(2,1)}), bf16[32,16,8,128]{3,2,1,0:T(8,128)(2,1)S(1)}, u32[]{:S(2)}, u32[]{:S(2)}) %all-to-all-start.1) | async-done | bytes 1048608 | tf_op jit(solution)/shard_map/all_to_all | solution.py:502
  41.9 0.0 copy-start.9
  41.9 0.0 copy-start.8
  41.9 0.0 copy-start.2
  41.9 3.7 %all-to-all-start.2 = ((bf16[32,36,8,128]{3,2,1,0:T(8,128)(2,1)}), bf16[32,36,8,128]{3,2,1,0:T(8,128)(2,1)}, u32[]{:S(2)}, u32[]{:S(2)}) async-start(bf16[32,36,8,128]{3,2,1,0:T(8,128)(2,1)} %bitcast.70), calls=%async_computation.2 | async-start | bytes 4718592 | tf_op jit(solution)/shard_map/all_to_all | solution.py:502
  45.6 0.0 copy-done.9
  45.6 0.0 copy-done
  45.7 0.0 copy-done.8
  45.7 0.3 convolution_multiply_fusion
  46.0 0.1 fusion.3
  46.1 0.1 div.54
  46.2 0.1 div.55
  46.2 0.2 fusion.2
  46.4 0.2 fusion
  46.6 0.2 fusion.1
  46.8 0.2 multiply_reduce_fusion.2
  47.1 0.2 multiply_reduce_fusion.1
  47.3 0.2 multiply_reduce_fusion
  47.5 0.1 multiply_subtract_fusion.2
  47.5 0.6 subtract_divide_fusion
  48.2 0.2 select_maximum_fusion.refs_2_
  48.3 0.0 copy-done.2
  48.3 0.0 copy-start.1
  48.3 2.2 %copy-done.1 = bf16[8,262144]{1,0:T(8,128)(2,1)S(1)} copy-done((bf16[8,262144]{1,0:T(8,128)(2,1)S(1)}, bf16[8,262144]{1,0:T(8,128)(2,1)}, u32[]{:S(2)}) %copy-start.1) | copy-done | bytes 4194328
  50.5 0.0 copy-start.3
  50.5 1.6 %copy-done.3 = bf16[16,256,256]{2,1,0:T(8,128)(2,1)S(1)} copy-done((bf16[16,256,256]{2,1,0:T(8,128)(2,1)S(1)}, bf16[16,256,256]{2,1,0:T(8,128)(2,1)}, u32[]{:S(2)}) %copy-start.3) | copy-done | bytes 2097176
  52.1 0.0 copy-start.5
  52.1 1.2 copy-done.5
  53.3 0.0 copy-start.6
  53.3 0.9 copy-done.6
  54.3 12.4 %head.4 = bf16[64,6,8,128]{3,2,1,0:T(8,128)(2,1)S(1)} custom-call(bf16[8,65536]{1,0:T(8,128)(2,1)S(1)} %copy-done.5, bf16[8,262144]{1,0:T(8,128)(2,1)S(1)} %copy-done.1, f32[16,4096]{1,0:T(8,128)S(1)} %copy-done.6, bf16[16,256,256]{2,1,0:T(8,128)(2,1)S(1)} %copy-done.3, bf16[16,256,256]{2,1,0:T(8,128)(2,1)S(1)} %copy-done.2), custom_call_target="tpu_custom_call" | custom-call | flops 3000000000 | bytes 3000000 | tf_op jit(solution)/shard_map/head/pallas_call | solution.py:257
  66.7 0.0 copy-start.7
  66.7 0.9 copy-done.7
  67.6 32.5 %all-to-all-done.2 = bf16[32,36,8,128]{3,2,1,0:T(8,128)(2,1)} async-done(((bf16[32,36,8,128]{3,2,1,0:T(8,128)(2,1)}), bf16[32,36,8,128]{3,2,1,0:T(8,128)(2,1)}, u32[]{:S(2)}, u32[]{:S(2)}) %all-to-all-start.2) | async-done | bytes 2359328 | tf_op jit(solution)/shard_map/all_to_all | solution.py:502
  100.1 4.0 %all-to-all-start = ((bf16[32,12,8,128]{3,2,1,0:T(8,128)(2,1)}), bf16[32,12,8,128]{3,2,1,0:T(8,128)(2,1)S(1)}, u32[]{:S(2)}, u32[]{:S(2)}) async-start(bf16[32,12,8,128]{3,2,1,0:T(8,128)(2,1)} %bitcast.69), calls=%async_computation | async-start | bytes 1572864 | tf_op jit(solution)/shard_map/all_to_all | solution.py:502
  104.2 10.4 %covariances.2.refs_3_ = f32[64,2,128,128]{3,2,1,0:T(8,128)} custom-call(bf16[16,2,36,8,128]{4,3,2,1,0:T(8,128)(2,1)} %bitcast.15.refs_0_, bf16[16,2,16,8,128]{4,3,2,1,0:T(8,128)(2,1)S(1)} %bitcast.66, f32[64,8,128]{2,1,0:T(8,128)S(1)} %select_maximum_fusion.refs_2_), custom_call_target="tpu_custom_call" | custom-call | flops 9600000000 | bytes 9600000 | tf_op jit(solution)/shard_map/covariances/pallas_call | solution.py:433
  114.5 10.2 %all-to-all-done = bf16[32,12,8,128]{3,2,1,0:T(8,128)(2,1)S(1)} async-done(((bf16[32,12,8,128]{3,2,1,0:T(8,128)(2,1)}), bf16[32,12,8,128]{3,2,1,0:T(8,128)(2,1)S(1)}, u32[]{:S(2)}, u32[]{:S(2)}) %all-to-all-start) | async-done | bytes 786464 | tf_op jit(solution)/shard_map/all_to_all | solution.py:502
  124.8 3.7 %covariances.3 = f32[64,2,128,128]{3,2,1,0:T(8,128)} custom-call(bf16[16,2,12,8,128]{4,3,2,1,0:T(8,128)(2,1)S(1)} %bitcast.68, bf16[16,2,16,8,128]{4,3,2,1,0:T(8,128)(2,1)S(1)} %bitcast.67, f32[64,8,128]{2,1,0:T(8,128)S(1)} %select_maximum_fusion.refs_2_, f32[64,2,128,128]{3,2,1,0:T(8,128)} %covariances.2.refs_3_), custom_call_target="tpu_custom_call", output_to_operand_aliasing={{}: (3, {})} | custom-call | flops 3200000000 | bytes 3200000 | tf_op jit(solution)/shard_map/covariances/pallas_call | solution.py:433
  (6 shorter events, 0.0 us)
Async XLA Ops:
  0.0 45.7 %copy-start = (f32[8,128]{1,0:T(8,128)S(1)}, f32[8,128]{1,0:T(8,128)}, u32[]{:S(2)}) copy-start(f32[8,128]{1,0:T(8,128)} %param.9) | copy-start | bytes 12292
  8.3 33.6 %all-to-all-start.1 = ((bf16[32,16,8,128]{3,2,1,0:T(8,128)(2,1)}), bf16[32,16,8,128]{3,2,1,0:T(8,128)(2,1)S(1)}, u32[]{:S(2)}, u32[]{:S(2)}) async-start(bf16[32,16,8,128]{3,2,1,0:T(8,128)(2,1)} %bitcast.71), calls=%async_computation.1 | async-start | bytes 2097152 | tf_op jit(solution)/shard_map/all_to_all | solution.py:502
  15.6 4.6 %collective-permute-start = (bf16[8,65536]{1,0:T(8,128)(2,1)}, bf16[8,65536]{1,0:T(8,128)(2,1)S(1)}, u32[]{:S(2)}, u32[]{:S(2)}) collective-permute-start(bf16[8,65536]{1,0:T(8,128)(2,1)} %get-tuple-element.11), channel_id=1, source_target_pairs={{0,1},{2,3},{4,5},{6,7},{8,9},{10,11},{12,13},{14,15},{16,17},{18,... | collective-permute-start | bytes 3145736 | tf_op jit(solution)/shard_map/ppermute | solution.py:521
  20.3 1.0 copy-start.4
  41.9 3.8 %copy-start.9 = (s32[64]{0:T(128)S(1)}, s32[64]{0:T(128)}, u32[]{:S(2)}) copy-start(s32[64]{0:T(128)} %param.11) | copy-start | bytes 772
  41.9 3.8 %copy-start.8 = (s32[64,4]{0,1:T(4,128)S(1)}, s32[64,4]{0,1:T(4,128)}, u32[]{:S(2)}) copy-start(s32[64,4]{0,1:T(4,128)} %param.10) | copy-start | bytes 3076
  41.9 6.4 %copy-start.2 = (bf16[16,256,256]{2,1,0:T(8,128)(2,1)S(1)}, bf16[16,256,256]{2,1,0:T(8,128)(2,1)}, u32[]{:S(2)}) copy-start(bf16[16,256,256]{2,1,0:T(8,128)(2,1)} %constant.11.clone.refs_4_) | copy-start | bytes 6291460
  41.9 58.3 %all-to-all-start.2 = ((bf16[32,36,8,128]{3,2,1,0:T(8,128)(2,1)}), bf16[32,36,8,128]{3,2,1,0:T(8,128)(2,1)}, u32[]{:S(2)}, u32[]{:S(2)}) async-start(bf16[32,36,8,128]{3,2,1,0:T(8,128)(2,1)} %bitcast.70), calls=%async_computation.2 | async-start | bytes 4718592 | tf_op jit(solution)/shard_map/all_to_all | solution.py:502
  48.3 2.2 %copy-start.1 = (bf16[8,262144]{1,0:T(8,128)(2,1)S(1)}, bf16[8,262144]{1,0:T(8,128)(2,1)}, u32[]{:S(2)}) copy-start(bf16[8,262144]{1,0:T(8,128)(2,1)} %refs_1_.5) | copy-start | bytes 12582916
  50.5 1.6 %copy-start.3 = (bf16[16,256,256]{2,1,0:T(8,128)(2,1)S(1)}, bf16[16,256,256]{2,1,0:T(8,128)(2,1)}, u32[]{:S(2)}) copy-start(bf16[16,256,256]{2,1,0:T(8,128)(2,1)} %constant.10.clone.refs_3_) | copy-start | bytes 6291460
  52.1 1.2 copy-start.5
  53.3 0.9 copy-start.6
  66.7 0.9 copy-start.7
  100.1 24.6 %all-to-all-start = ((bf16[32,12,8,128]{3,2,1,0:T(8,128)(2,1)}), bf16[32,12,8,128]{3,2,1,0:T(8,128)(2,1)S(1)}, u32[]{:S(2)}, u32[]{:S(2)}) async-start(bf16[32,12,8,128]{3,2,1,0:T(8,128)(2,1)} %bitcast.69), calls=%async_computation | async-start | bytes 1572864 | tf_op jit(solution)/shard_map/all_to_all | solution.py:502

commit v7 on v6

--- a/solution.py
+++ b/solution.py
@@ -106,14 +106,14 @@
         for j in range(frame_block // 2):
             pair = (evens[j] + odds[j], both[j] - evens[j] - odds[j + 1])
             for frame, total in zip((2 * j, 2 * j + 1), pair):
-                filtered[part, frame * octet : (frame + 1) * octet, :] = total
+                filtered[part, pl.ds(frame, octet, stride=frame_block), :] = total
 
     kept = pl.ds(pl.multiple_of(step * frame_block, frame_block), frame_block)
 
     @pl.loop(0, octet)
     def _(antenna):
         for half in range(frame_block // octet):
-            rows = pl.ds(half * octet * octet + antenna, octet, stride=octet)
+            rows = pl.ds(pl.multiple_of(antenna * frame_block + half * octet, octet), octet)
             bins = real_transform([filtered[part, rows, :] for part in range(radix)])
             here = pl.ds(half * octet, octet)
             sections[0, here, :] = bins[0][0]
@@ -146,12 +146,9 @@
     )
 
 
-def head_kernel(length, steps, each, size, skipped, with_edge, *refs):
+def head_kernel(length, steps, each, size, skipped, *refs):
     before_ref, block_ref, taps_ref, wave_high_ref, wave_low_ref = refs[:5]
-    refs = refs[5:]
-    if with_edge:
-        edge_out, refs = refs[0], refs[1:]
-    out_ref, refs = refs[0], refs[1:]
+    out_ref, *refs = refs[5:]
     filtered, sections, history, turned, high, low, wave_high, wave_low, done = refs
     step = pl.program_id(0)
     frames = high.shape[2]
@@ -159,10 +156,9 @@
     kept = lanes // 2
     taken = pl.ds(2 * skipped, 2 * size)
     waves = [
-        pltpu.make_async_copy(wave_high_ref.at[taken], wave_high, done.at[1]),
-        pltpu.make_async_copy(wave_low_ref.at[taken], wave_low, done.at[2]),
+        pltpu.make_async_copy(wave_high_ref.at[taken], wave_high, done.at[0]),
+        pltpu.make_async_copy(wave_low_ref.at[taken], wave_low, done.at[1]),
     ]
-    edge = pltpu.make_async_copy(block_ref, edge_out, done.at[0]) if with_edge else None
 
     @pl.when(step == 0)
     def _():
@@ -192,12 +188,6 @@
             sections,
             history if steps > 1 else None,
         )
-
-    if with_edge:
-
-        @pl.when(step == steps - 1)
-        def _():
-            edge.start()
 
     @pl.when(step == steps)
     def _():
@@ -228,14 +218,8 @@
         for j in range(each * steps):
             out_ref[:, j] = turned[j].reshape(kept, octet, lanes).astype(bf16)
 
-    if with_edge:
-
-        @pl.when(step == pl.num_programs(0) - 1)
-        def _():
-            edge.wait()
-
-
-def head(before, before_block, samples, taps, tables, first, steps, skipped, size, with_edge):
+
+def head(before, before_block, samples, taps, tables, first, steps, skipped, size):
     length = taps.shape[1]
     radix = length // lanes
     groups = radix // 2
@@ -244,18 +228,8 @@
     width = frame_block * length
     each = divisor(size, skipped, most=4 if steps == 1 else 2)
     anywhere = pl.BlockSpec(memory_space=pl.ANY)
-    out_shape, out_specs = [], []
-    if with_edge:
-        out_shape.append(jax.ShapeDtypeStruct((octet, width), bf16))
-        out_specs.append(anywhere)
-    out_shape.append(jax.ShapeDtypeStruct((kept, size * steps, octet, lanes), bf16))
-    out_specs.append(
-        pl.BlockSpec(
-            (kept, each * steps, octet, lanes), lambda i: (0, jnp.maximum(i - steps, 0), 0, 0)
-        )
-    )
     return pl.pallas_call(
-        functools.partial(head_kernel, length, steps, each, size, skipped, with_edge),
+        functools.partial(head_kernel, length, steps, each, size, skipped),
         grid=(steps + size // each,),
         in_specs=[
             pl.BlockSpec((octet, width), lambda i: (0, before_block)),
@@ -264,8 +238,10 @@
             anywhere,
             anywhere,
         ],
-        out_specs=out_specs,
-        out_shape=out_shape,
+        out_specs=pl.BlockSpec(
+            (kept, each * steps, octet, lanes), lambda i: (0, jnp.maximum(i - steps, 0), 0, 0)
+        ),
+        out_shape=jax.ShapeDtypeStruct((kept, size * steps, octet, lanes), bf16),
         scratch_shapes=[
             pltpu.VMEM((radix, frame_block * octet, lanes), f32),
             pltpu.VMEM((radix, frame_block, lanes), f32),
@@ -275,7 +251,7 @@
             pltpu.VMEM((groups, octet, frames, 2 * lanes), bf16),
             pltpu.VMEM((2 * size, 2 * lanes, 2 * lanes), bf16),
             pltpu.VMEM((2 * size, 2 * lanes, 2 * lanes), bf16),
-            pltpu.SemaphoreType.DMA((3,)),
+            pltpu.SemaphoreType.DMA((2,)),
         ],
         compiler_params=pltpu.CompilerParams(vmem_limit_bytes=later_vmem if skipped else head_vmem),
         cost_estimate=pl.CostEstimate(
@@ -318,15 +294,22 @@
     step = pl.program_id(0)
     steps = pl.num_programs(0)
     slot = lax.rem(step, 2)
-    octets, shards = x_refs[0].shape[:2]
+    octets, shards, runs = x_refs[0].shape[:3]
     antennas = octets * octet
-    columns = x_refs[0].shape[2] // widths[0]
-    count = columns * (4 if packed else 1)
+    columns = x_refs[0].shape[3] // widths[0]
+    held = [
+        (run, j, c) for run in range(runs) for j in range(columns) for c in range(4 if packed else 1)
+    ]
+    count = len(held)
+
+    def target(at, index):
+        run, j, c = held[index]
+        return place(run, at * columns + j, c)
 
     def copies(at, which):
         return [
             pltpu.make_async_copy(
-                ready.at[which, j], out_ref.at[place(at * count + j)], done.at[which, j]
+                ready.at[which, j], out_ref.at[target(at, j)], done.at[which, j]
             )
             for j in range(count)
         ]
@@ -336,16 +319,16 @@
         for copy in copies(step - 2, slot):
             copy.wait()
 
-    def load(ref, t, j):
+    def load(ref, t, run, j):
         if t >= shards:
             return jnp.zeros((antennas, lanes), f32)
-        return ref[:, t, j].astype(f32).reshape(antennas, lanes)
-
-    def channels(j):
+        return ref[:, t, run, j].astype(f32).reshape(antennas, lanes)
+
+    def channels(run, j):
         parts = [[] for _ in range(8 if packed else 2)]
         for t in range(0, shards, 2):
             tiles = [
-                load(ref, u, j * width + at)
+                load(ref, u, run, j * width + at)
                 for u in (t, t + 1)
                 for ref, width in zip(x_refs, widths)
                 for at in range(width)
@@ -368,8 +351,8 @@
         middle = v.shape[1] // 2
         return jnp.concatenate([v[:, middle:], -v[:, :middle]], axis=1)
 
-    xs = [x for j in range(columns) for x in channels(j)]
-    qs = [split_three(q_ref[place(step * count + at)]) for at in range(count)]
+    xs = [x for run in range(runs) for j in range(columns) for x in channels(run, j)]
+    qs = [split_three(q_ref[target(step, at)]) for at in range(count)]
     zs = []
     for x, (qh, qm, ql) in zip(xs, qs):
         left = jnp.concatenate([qh, qm, ql, jnp.zeros_like(qh)], axis=0).astype(bf16)
@@ -407,24 +390,22 @@
     octets, shards = array.shape[:2]
     antennas = octets * octet
     widths = [one[4] for one in received]
-    sizes = [n for a, r, begin, _, width in received for n in (a.shape[2] // (r * width), begin)]
     packed = len(received) > 1
-    each = divisor(taken, *sizes, most=2 if packed else 8)
-    count = each * (4 if packed else 1)
+    sizes = [begin for _, _, begin, _, _ in received]
+    each = divisor(taken, *sizes, most=max(1, 4 // runs) if packed else 8)
+    count = runs * each * (4 if packed else 1)
     steps = taken // each
 
-    def window(array, runs, begin, _, width):
-        stride = array.shape[2] // (runs * width * each)
-
-        def index(i):
-            run = i // steps
-            return (0, 0, run * stride + begin // each + i - run * steps, 0, 0)
-
-        return pl.BlockSpec((octets, shards, each * width, octet, lanes), index)
-
-    in_specs = [window(*one) for one in received]
+    def window(begin, width):
+        return pl.BlockSpec(
+            (octets, shards, runs, each * width, octet, lanes),
+            lambda i: (0, 0, 0, begin // each + i, 0, 0),
+        )
+
+    in_specs = [window(begin, width) for _, _, begin, _, width in received]
     in_specs.append(pl.BlockSpec(basis.shape, lambda i: (0, 0, 0)))
-    operands = [*(one[0] for one in received), basis]
+    operands = [one[0].reshape(octets, shards, runs, -1, octet, lanes) for one in received]
+    operands.append(basis)
     aliases = {}
     if previous is not None:
         in_specs.append(pl.BlockSpec(memory_space=pl.ANY))
@@ -432,7 +413,7 @@
         operands.append(previous)
     return pl.pallas_call(
         functools.partial(covariance_kernel, place, 1.0 / frame_total, widths),
-        grid=(runs * steps,),
+        grid=(steps,),
         in_specs=in_specs,
         out_specs=pl.BlockSpec(memory_space=pl.ANY),
         out_shape=jax.ShapeDtypeStruct((total, 2, antennas, antennas), f32),
@@ -443,8 +424,8 @@
         input_output_aliases=aliases,
         compiler_params=pltpu.CompilerParams(vmem_limit_bytes=last_vmem if last else covariance_vmem),
         cost_estimate=pl.CostEstimate(
-            flops=runs * steps * count * 200_000_000,
-            bytes_accessed=runs * steps * count * 200_000,
+            flops=steps * count * 200_000_000,
+            bytes_accessed=steps * count * 200_000,
             transcendentals=0,
         ),
         name="covariances",
@@ -507,24 +488,24 @@
             ).transpose(2, 0, 1, 3, 4)
         return received
 
-    def channel_at(first, count):
-        def place(index):
-            run = index // (4 * count)
-            two = (index - run * (4 * count)) // 4
-            group = 2 * (first + two) + index % 2
+    def channel_at(first):
+        def place(run, column, c):
+            group = 2 * (first + column) + c % 2
             mirrored = jnp.where(group == 0, groups, radix - group)
-            return run * radix + jnp.where(index % 4 < 2, group, mirrored)
+            return run * radix + (group if c < 2 else mirrored)
 
         return place
 
-    edge, early = head(padded, blocks - 2, padded, taps, tables, blocks - 1, 1, 0, twos, True)
+    early = head(padded, blocks - 2, padded, taps, tables, blocks - 1, 1, 0, twos)
+    early, behind = lax.optimization_barrier((early, padded))
+    edge = behind[:, width - frame_block * length :]
     before = lax.ppermute(edge, "tm", [(i, i + 1) for i in range(shards - 1)])
     if whole_runs:
         arrived = exchange(early.reshape(devices, -1, octet, lanes))
     basis = basis_of(interferer_ids, ranks, steering)
 
     def later(first, count):
-        return head(before, 0, padded, taps, tables, 0, blocks - 1, first, count, False)[0]
+        return head(before, 0, padded, taps, tables, 0, blocks - 1, first, count)
 
     out = None
     if whole_runs:
@@ -544,7 +525,7 @@
                 (arrived, runs, first, count, 1),
             )
             out = covariances(
-                parts, basis, channel_at(first, count), frame_total, owned, out, first > 0
+                parts, basis, channel_at(first), frame_total, owned, out, first > 0
             )
     else:
         tiles = jnp.concatenate(
@@ -563,7 +544,7 @@
         tiles = tiles[:, np.argsort(order), :antennas].reshape(devices, owned, antennas, lanes)
         received = exchange(tiles)
         parts = ((received, 1, 0, owned, 1),)
-        out = covariances(parts, basis, lambda index: index, frame_total, owned, None, True)
+        out = covariances(parts, basis, lambda run, column, c: column, frame_total, owned, None, True)
     return out
 
 

time: 129 us -> 129 us (level)
  Pallas kernels: 52.7 us -> 49.9 us
    pallas_call x2, Pallas kernels: 14.1 us -> 12.6 us  [covariances(): pl.pallas_call(functools.partial(covariance_kernel, place, 1.0 / frame_to...]
    slice x0 -> x1, local copies, waits for them, and re-layouts: none -> 1.3 us  [per_device(): edge = behind[:, width - frame_block * length:]]
  transfers between devices with their start and end apart: 4 -> 4, of which waited for: 4 -> 4; matrix products, arithmetic and copies ran while one was open for 2% -> 3% of each run, Pallas kernels for 32% -> 30%
where the time goes in v7:
time: 129 us; the launch traced here: 128 us
  Pallas kernels  49.9 us (39%)
  waiting for transfers between devices  48.6 us (38%)
  starting transfers between devices  17.5 us (14%)
  local copies, waits for them, and re-layouts  9.19 us (7%)
  other arithmetic  2.22 us (2%)
    all_to_all x3, waiting for transfers between devices, exchange(): lax.all_to_all(spectra, ('chan', 'tm'), split_axis=0, concat_axis=0, tile...  46.4 us
    pallas_call x3, Pallas kernels, head(): pl.pallas_call(functools.partial(head_kernel, length, steps, each, size,...  37.4 us
    all_to_all x3, starting transfers between devices, exchange(): lax.all_to_all(spectra, ('chan', 'tm'), split_axis=0, concat_axis=0, tile...  15.3 us
    pallas_call x2, Pallas kernels, covariances(): pl.pallas_call(functools.partial(covariance_kernel, place, 1.0 / frame_to...  12.6 us
    unnamed x20, local copies, waits for them, and re-layouts  7.82 us
  transfers between devices with their start and end apart: 4, of which 4 were waited for; matrix products, arithmetic and copies ran while one was open for 3% of the time, Pallas kernels for 30%

profile of v7, /device:TPU:0, one launch (start us, length us, event | category | flops | bytes accessed | tf_op | source)
XLA Modules:
  0.0 128.1 jit_solution(2366863009634535244)
XLA Ops:
  0.0 0.0 copy-start
  0.0 8.1 %head.3 = bf16[64,8,8,128]{3,2,1,0:T(8,128)(2,1)} custom-call(bf16[8,262144]{1,0:T(8,128)(2,1)} %refs_1_.5, bf16[8,262144]{1,0:T(8,128)(2,1)} %refs_1_.5, f32[16,4096]{1,0:T(8,128)} %refs_2_.5, bf16[16,256,256]{2,1,0:T(8,128)(2,1)} %constant.10.clone.refs_3_, bf16[16,256,256]{2,1,0:T(8,128)(2,1)} %constant.11.clone.refs_4_), custom_call_target="tpu_custom_call" | custom-call | flops 1000000000 | bytes 1000000 | tf_op jit(solution)/shard_map/head/pallas_call | solution.py:231
  8.1 7.3 %all-to-all-start.1 = ((bf16[32,16,8,128]{3,2,1,0:T(8,128)(2,1)}), bf16[32,16,8,128]{3,2,1,0:T(8,128)(2,1)S(1)}, u32[]{:S(2)}, u32[]{:S(2)}) async-start(bf16[32,16,8,128]{3,2,1,0:T(8,128)(2,1)} %bitcast.72), calls=%async_computation.1 | async-start | bytes 2097152 | tf_op jit(solution)/shard_map/all_to_all | solution.py:483
  15.4 1.3 %slice.15 = bf16[8,65536]{1,0:T(8,128)(2,1)S(1)} slice(bf16[8,262144]{1,0:T(8,128)(2,1)} %refs_1_.5), slice={[0:8], [196608:262144]} | slice | bytes 2097152 | tf_op jit(solution)/shard_map/slice | solution.py:501
  16.7 2.2 %collective-permute-start = (bf16[8,65536]{1,0:T(8,128)(2,1)S(1)}, bf16[8,65536]{1,0:T(8,128)(2,1)S(1)}, u32[]{:S(2)}, u32[]{:S(2)}) collective-permute-start(bf16[8,65536]{1,0:T(8,128)(2,1)S(1)} %slice.15), channel_id=1, source_target_pairs={{0,1},{2,3},{4,5},{6,7},{8,9},{10,11},{12,13},{14,15},{16,17},{18,... | collective-permute-start | bytes 3145736 | tf_op jit(solution)/shard_map/ppermute | solution.py:502
  18.9 2.2 %collective-permute-done.refs_0_ = bf16[8,65536]{1,0:T(8,128)(2,1)S(1)} collective-permute-done((bf16[8,65536]{1,0:T(8,128)(2,1)S(1)}, bf16[8,65536]{1,0:T(8,128)(2,1)S(1)}, u32[]{:S(2)}, u32[]{:S(2)}) %collective-permute-start) | collective-permute-done | bytes 1048608 | tf_op jit(solution)/shard_map/ppermute | solution.py:502
  21.1 0.0 copy-start.4
  21.1 1.0 copy-done.4
  22.1 17.4 %head.5 = bf16[64,18,8,128]{3,2,1,0:T(8,128)(2,1)} custom-call(bf16[8,65536]{1,0:T(8,128)(2,1)} %copy-done.4, bf16[8,262144]{1,0:T(8,128)(2,1)} %refs_1_.5, f32[16,4096]{1,0:T(8,128)} %refs_2_.5, bf16[16,256,256]{2,1,0:T(8,128)(2,1)} %constant.10.clone.refs_3_, bf16[16,256,256]{2,1,0:T(8,128)(2,1)} %constant.11.clone.refs_4_), custom_call_target="tpu_custom_call" | custom-call | flops 3000000000 | bytes 3000000 | tf_op jit(solution)/shard_map/head/pallas_call | solution.py:231
  39.5 2.1 %all-to-all-done.1 = bf16[32,16,8,128]{3,2,1,0:T(8,128)(2,1)S(1)} async-done(((bf16[32,16,8,128]{3,2,1,0:T(8,128)(2,1)}), bf16[32,16,8,128]{3,2,1,0:T(8,128)(2,1)S(1)}, u32[]{:S(2)}, u32[]{:S(2)}) %all-to-all-start.1) | async-done | bytes 1048608 | tf_op jit(solution)/shard_map/all_to_all | solution.py:483
  41.6 0.0 copy-start.9
  41.6 0.0 copy-start.8
  41.6 0.0 copy-start.2
  41.6 3.8 %all-to-all-start.2 = ((bf16[32,36,8,128]{3,2,1,0:T(8,128)(2,1)}), bf16[32,36,8,128]{3,2,1,0:T(8,128)(2,1)}, u32[]{:S(2)}, u32[]{:S(2)}) async-start(bf16[32,36,8,128]{3,2,1,0:T(8,128)(2,1)} %bitcast.71), calls=%async_computation.2 | async-start | bytes 4718592 | tf_op jit(solution)/shard_map/all_to_all | solution.py:483
  45.4 0.0 copy-done.9
  45.5 0.0 copy-done
  45.5 0.0 copy-done.8
  45.5 0.3 convolution_multiply_fusion
  45.8 0.1 fusion.3
  45.9 0.1 div.54
  46.0 0.1 div.55
  46.1 0.2 fusion.2
  46.2 0.2 fusion
  46.4 0.2 fusion.1
  46.7 0.2 multiply_reduce_fusion.2
  46.9 0.2 multiply_reduce_fusion.1
  47.1 0.2 multiply_reduce_fusion
  47.3 0.1 multiply_subtract_fusion.2
  47.4 0.6 subtract_divide_fusion
  48.0 0.2 select_maximum_fusion.refs_2_
  48.1 0.0 copy-done.2
  48.1 0.0 copy-start.1
  48.2 2.2 %copy-done.1 = bf16[8,262144]{1,0:T(8,128)(2,1)S(1)} copy-done((bf16[8,262144]{1,0:T(8,128)(2,1)S(1)}, bf16[8,262144]{1,0:T(8,128)(2,1)}, u32[]{:S(2)}) %copy-start.1) | copy-done | bytes 4194328
  50.3 0.0 copy-start.3
  50.3 1.6 %copy-done.3 = bf16[16,256,256]{2,1,0:T(8,128)(2,1)S(1)} copy-done((bf16[16,256,256]{2,1,0:T(8,128)(2,1)S(1)}, bf16[16,256,256]{2,1,0:T(8,128)(2,1)}, u32[]{:S(2)}) %copy-start.3) | copy-done | bytes 2097176
  51.9 0.0 copy-start.5
  51.9 1.2 copy-done.5
  53.2 0.0 copy-start.6
  53.2 0.9 copy-done.6
  54.1 11.9 %head.4 = bf16[64,6,8,128]{3,2,1,0:T(8,128)(2,1)S(1)} custom-call(bf16[8,65536]{1,0:T(8,128)(2,1)S(1)} %copy-done.5, bf16[8,262144]{1,0:T(8,128)(2,1)S(1)} %copy-done.1, f32[16,4096]{1,0:T(8,128)S(1)} %copy-done.6, bf16[16,256,256]{2,1,0:T(8,128)(2,1)S(1)} %copy-done.3, bf16[16,256,256]{2,1,0:T(8,128)(2,1)S(1)} %copy-done.2), custom_call_target="tpu_custom_call" | custom-call | flops 3000000000 | bytes 3000000 | tf_op jit(solution)/shard_map/head/pallas_call | solution.py:231
  66.0 0.0 copy-start.7
  66.0 0.9 copy-done.7
  66.9 33.1 %all-to-all-done.2 = bf16[32,36,8,128]{3,2,1,0:T(8,128)(2,1)} async-done(((bf16[32,36,8,128]{3,2,1,0:T(8,128)(2,1)}), bf16[32,36,8,128]{3,2,1,0:T(8,128)(2,1)}, u32[]{:S(2)}, u32[]{:S(2)}) %all-to-all-start.2) | async-done | bytes 2359328 | tf_op jit(solution)/shard_map/all_to_all | solution.py:483
  100.0 4.2 %all-to-all-start = ((bf16[32,12,8,128]{3,2,1,0:T(8,128)(2,1)}), bf16[32,12,8,128]{3,2,1,0:T(8,128)(2,1)S(1)}, u32[]{:S(2)}, u32[]{:S(2)}) async-start(bf16[32,12,8,128]{3,2,1,0:T(8,128)(2,1)} %bitcast.70), calls=%async_computation | async-start | bytes 1572864 | tf_op jit(solution)/shard_map/all_to_all | solution.py:483
  104.2 9.2 %covariances.2.refs_3_ = f32[64,2,128,128]{3,2,1,0:T(8,128)} custom-call(bf16[16,2,2,18,8,128]{5,4,3,2,1,0:T(8,128)(2,1)} %bitcast.16.refs_0_, bf16[16,2,2,8,8,128]{5,4,3,2,1,0:T(8,128)(2,1)S(1)} %bitcast.67, f32[64,8,128]{2,1,0:T(8,128)S(1)} %select_maximum_fusion.refs_2_), custom_call_target="tpu_custom_call" | custom-call | flops 9600000000 | bytes 9600000 | tf_op jit(solution)/shard_map/covariances/pallas_call | solution.py:414
  113.4 11.2 %all-to-all-done = bf16[32,12,8,128]{3,2,1,0:T(8,128)(2,1)S(1)} async-done(((bf16[32,12,8,128]{3,2,1,0:T(8,128)(2,1)}), bf16[32,12,8,128]{3,2,1,0:T(8,128)(2,1)S(1)}, u32[]{:S(2)}, u32[]{:S(2)}) %all-to-all-start) | async-done | bytes 786464 | tf_op jit(solution)/shard_map/all_to_all | solution.py:483
  124.6 3.4 %covariances.3 = f32[64,2,128,128]{3,2,1,0:T(8,128)} custom-call(bf16[16,2,2,6,8,128]{5,4,3,2,1,0:T(8,128)(2,1)S(1)} %bitcast.69, bf16[16,2,2,8,8,128]{5,4,3,2,1,0:T(8,128)(2,1)S(1)} %bitcast.68, f32[64,8,128]{2,1,0:T(8,128)S(1)} %select_maximum_fusion.refs_2_, f32[64,2,128,128]{3,2,1,0:T(8,128)} %covariances.2.refs_3_), custom_call_target="tpu_custom_call", output_to_operand_aliasing={{}: (3, {})} | custom-call | flops 3200000000 | bytes 3200000 | tf_op jit(solution)/shard_map/covariances/pallas_call | solution.py:414
  (6 shorter events, 0.0 us)
Async XLA Ops:
  0.0 45.5 %copy-start = (f32[8,128]{1,0:T(8,128)S(1)}, f32[8,128]{1,0:T(8,128)}, u32[]{:S(2)}) copy-start(f32[8,128]{1,0:T(8,128)} %param.9) | copy-start | bytes 12292
  8.1 33.6 %all-to-all-start.1 = ((bf16[32,16,8,128]{3,2,1,0:T(8,128)(2,1)}), bf16[32,16,8,128]{3,2,1,0:T(8,128)(2,1)S(1)}, u32[]{:S(2)}, u32[]{:S(2)}) async-start(bf16[32,16,8,128]{3,2,1,0:T(8,128)(2,1)} %bitcast.72), calls=%async_computation.1 | async-start | bytes 2097152 | tf_op jit(solution)/shard_map/all_to_all | solution.py:483
  16.7 4.4 %collective-permute-start = (bf16[8,65536]{1,0:T(8,128)(2,1)S(1)}, bf16[8,65536]{1,0:T(8,128)(2,1)S(1)}, u32[]{:S(2)}, u32[]{:S(2)}) collective-permute-start(bf16[8,65536]{1,0:T(8,128)(2,1)S(1)} %slice.15), channel_id=1, source_target_pairs={{0,1},{2,3},{4,5},{6,7},{8,9},{10,11},{12,13},{14,15},{16,17},{18,... | collective-permute-start | bytes 3145736 | tf_op jit(solution)/shard_map/ppermute | solution.py:502
  21.1 1.0 copy-start.4
  41.6 3.8 %copy-start.9 = (s32[64]{0:T(128)S(1)}, s32[64]{0:T(128)}, u32[]{:S(2)}) copy-start(s32[64]{0:T(128)} %param.11) | copy-start | bytes 772
  41.6 3.8 %copy-start.8 = (s32[64,4]{0,1:T(4,128)S(1)}, s32[64,4]{0,1:T(4,128)}, u32[]{:S(2)}) copy-start(s32[64,4]{0,1:T(4,128)} %param.10) | copy-start | bytes 3076
  41.6 6.5 %copy-start.2 = (bf16[16,256,256]{2,1,0:T(8,128)(2,1)S(1)}, bf16[16,256,256]{2,1,0:T(8,128)(2,1)}, u32[]{:S(2)}) copy-start(bf16[16,256,256]{2,1,0:T(8,128)(2,1)} %constant.11.clone.refs_4_) | copy-start | bytes 6291460
  41.6 58.3 %all-to-all-start.2 = ((bf16[32,36,8,128]{3,2,1,0:T(8,128)(2,1)}), bf16[32,36,8,128]{3,2,1,0:T(8,128)(2,1)}, u32[]{:S(2)}, u32[]{:S(2)}) async-start(bf16[32,36,8,128]{3,2,1,0:T(8,128)(2,1)} %bitcast.71), calls=%async_computation.2 | async-start | bytes 4718592 | tf_op jit(solution)/shard_map/all_to_all | solution.py:483
  48.1 2.2 %copy-start.1 = (bf16[8,262144]{1,0:T(8,128)(2,1)S(1)}, bf16[8,262144]{1,0:T(8,128)(2,1)}, u32[]{:S(2)}) copy-start(bf16[8,262144]{1,0:T(8,128)(2,1)} %refs_1_.5) | copy-start | bytes 12582916
  50.3 1.6 %copy-start.3 = (bf16[16,256,256]{2,1,0:T(8,128)(2,1)S(1)}, bf16[16,256,256]{2,1,0:T(8,128)(2,1)}, u32[]{:S(2)}) copy-start(bf16[16,256,256]{2,1,0:T(8,128)(2,1)} %constant.10.clone.refs_3_) | copy-start | bytes 6291460
  51.9 1.2 copy-start.5
  53.2 0.9 copy-start.6
  66.0 0.9 copy-start.7
  100.0 24.6 %all-to-all-start = ((bf16[32,12,8,128]{3,2,1,0:T(8,128)(2,1)}), bf16[32,12,8,128]{3,2,1,0:T(8,128)(2,1)S(1)}, u32[]{:S(2)}, u32[]{:S(2)}) async-start(bf16[32,12,8,128]{3,2,1,0:T(8,128)(2,1)} %bitcast.70), calls=%async_computation | async-start | bytes 1572864 | tf_op jit(solution)/shard_map/all_to_all | solution.py:483

commit v8 on v7

--- a/solution.py
+++ b/solution.py
@@ -226,7 +226,7 @@
     kept = lanes // 2
     frames = steps * frame_block
     width = frame_block * length
-    each = divisor(size, skipped, most=4 if steps == 1 else 2)
+    each = divisor(size, skipped, most=8 if steps == 1 else 2)
     anywhere = pl.BlockSpec(memory_space=pl.ANY)
     return pl.pallas_call(
         functools.partial(head_kernel, length, steps, each, size, skipped),

time: 129 us -> 128 us (level)
  no operation moved by 1% of the time
where the time goes in v8:
time: 128 us
  Pallas kernels  49.7 us (39%)
  waiting for transfers between devices  48.6 us (38%)
  starting transfers between devices  17.5 us (14%)
  local copies, waits for them, and re-layouts  9.19 us (7%)
  other arithmetic  2.22 us (2%)
    all_to_all x3, waiting for transfers between devices, exchange(): lax.all_to_all(spectra, ('chan', 'tm'), split_axis=0, concat_axis=0, tile...  46.4 us
    pallas_call x3, Pallas kernels, head(): pl.pallas_call(functools.partial(head_kernel, length, steps, each, size,...  37.1 us
    all_to_all x3, starting transfers between devices, exchange(): lax.all_to_all(spectra, ('chan', 'tm'), split_axis=0, concat_axis=0, tile...  15.3 us
    pallas_call x2, Pallas kernels, covariances(): pl.pallas_call(functools.partial(covariance_kernel, place, 1.0 / frame_to...  12.6 us
    unnamed x20, local copies, waits for them, and re-layouts  7.82 us
  transfers between devices with their start and end apart: 4, of which 4 were waited for; matrix products, arithmetic and copies ran while one was open for 3% of the time, Pallas kernels for 30%

profile of v8, /device:TPU:0, one launch (start us, length us, event | category | flops | bytes accessed | tf_op | source)
XLA Modules:
  0.0 127.9 jit_solution(17478698643311905380)
XLA Ops:
  0.0 0.0 copy-start
  0.0 7.8 %head.3 = bf16[64,8,8,128]{3,2,1,0:T(8,128)(2,1)} custom-call(bf16[8,262144]{1,0:T(8,128)(2,1)} %refs_1_.5, bf16[8,262144]{1,0:T(8,128)(2,1)} %refs_1_.5, f32[16,4096]{1,0:T(8,128)} %refs_2_.5, bf16[16,256,256]{2,1,0:T(8,128)(2,1)} %constant.10.clone.refs_3_, bf16[16,256,256]{2,1,0:T(8,128)(2,1)} %constant.11.clone.refs_4_), custom_call_target="tpu_custom_call" | custom-call | flops 1000000000 | bytes 1000000 | tf_op jit(solution)/shard_map/head/pallas_call | solution.py:231
  7.9 7.3 %all-to-all-start.1 = ((bf16[32,16,8,128]{3,2,1,0:T(8,128)(2,1)}), bf16[32,16,8,128]{3,2,1,0:T(8,128)(2,1)S(1)}, u32[]{:S(2)}, u32[]{:S(2)}) async-start(bf16[32,16,8,128]{3,2,1,0:T(8,128)(2,1)} %bitcast.72), calls=%async_computation.1 | async-start | bytes 2097152 | tf_op jit(solution)/shard_map/all_to_all | solution.py:483
  15.2 1.3 %slice.15 = bf16[8,65536]{1,0:T(8,128)(2,1)S(1)} slice(bf16[8,262144]{1,0:T(8,128)(2,1)} %refs_1_.5), slice={[0:8], [196608:262144]} | slice | bytes 2097152 | tf_op jit(solution)/shard_map/slice | solution.py:501
  16.5 2.2 %collective-permute-start = (bf16[8,65536]{1,0:T(8,128)(2,1)S(1)}, bf16[8,65536]{1,0:T(8,128)(2,1)S(1)}, u32[]{:S(2)}, u32[]{:S(2)}) collective-permute-start(bf16[8,65536]{1,0:T(8,128)(2,1)S(1)} %slice.15), channel_id=1, source_target_pairs={{0,1},{2,3},{4,5},{6,7},{8,9},{10,11},{12,13},{14,15},{16,17},{18,... | collective-permute-start | bytes 3145736 | tf_op jit(solution)/shard_map/ppermute | solution.py:502
  18.7 2.2 %collective-permute-done.refs_0_ = bf16[8,65536]{1,0:T(8,128)(2,1)S(1)} collective-permute-done((bf16[8,65536]{1,0:T(8,128)(2,1)S(1)}, bf16[8,65536]{1,0:T(8,128)(2,1)S(1)}, u32[]{:S(2)}, u32[]{:S(2)}) %collective-permute-start) | collective-permute-done | bytes 1048608 | tf_op jit(solution)/shard_map/ppermute | solution.py:502
  20.9 0.0 copy-start.4
  20.9 1.0 copy-done.4
  21.9 17.4 %head.5 = bf16[64,18,8,128]{3,2,1,0:T(8,128)(2,1)} custom-call(bf16[8,65536]{1,0:T(8,128)(2,1)} %copy-done.4, bf16[8,262144]{1,0:T(8,128)(2,1)} %refs_1_.5, f32[16,4096]{1,0:T(8,128)} %refs_2_.5, bf16[16,256,256]{2,1,0:T(8,128)(2,1)} %constant.10.clone.refs_3_, bf16[16,256,256]{2,1,0:T(8,128)(2,1)} %constant.11.clone.refs_4_), custom_call_target="tpu_custom_call" | custom-call | flops 3000000000 | bytes 3000000 | tf_op jit(solution)/shard_map/head/pallas_call | solution.py:231
  39.3 2.1 %all-to-all-done.1 = bf16[32,16,8,128]{3,2,1,0:T(8,128)(2,1)S(1)} async-done(((bf16[32,16,8,128]{3,2,1,0:T(8,128)(2,1)}), bf16[32,16,8,128]{3,2,1,0:T(8,128)(2,1)S(1)}, u32[]{:S(2)}, u32[]{:S(2)}) %all-to-all-start.1) | async-done | bytes 1048608 | tf_op jit(solution)/shard_map/all_to_all | solution.py:483
  41.4 0.0 copy-start.9
  41.4 0.0 copy-start.8
  41.4 0.0 copy-start.2
  41.4 3.8 %all-to-all-start.2 = ((bf16[32,36,8,128]{3,2,1,0:T(8,128)(2,1)}), bf16[32,36,8,128]{3,2,1,0:T(8,128)(2,1)}, u32[]{:S(2)}, u32[]{:S(2)}) async-start(bf16[32,36,8,128]{3,2,1,0:T(8,128)(2,1)} %bitcast.71), calls=%async_computation.2 | async-start | bytes 4718592 | tf_op jit(solution)/shard_map/all_to_all | solution.py:483
  45.2 0.0 copy-done.9
  45.2 0.0 copy-done
  45.2 0.0 copy-done.8
  45.3 0.3 convolution_multiply_fusion
  45.6 0.1 fusion.3
  45.7 0.1 div.54
  45.8 0.1 div.55
  45.8 0.2 fusion.2
  46.0 0.2 fusion
  46.2 0.2 fusion.1
  46.4 0.2 multiply_reduce_fusion.2
  46.6 0.2 multiply_reduce_fusion.1
  46.8 0.2 multiply_reduce_fusion
  47.1 0.1 multiply_subtract_fusion.2
  47.1 0.6 subtract_divide_fusion
  47.8 0.2 select_maximum_fusion.refs_2_
  47.9 0.0 copy-done.2
  47.9 0.0 copy-start.1
  47.9 2.2 %copy-done.1 = bf16[8,262144]{1,0:T(8,128)(2,1)S(1)} copy-done((bf16[8,262144]{1,0:T(8,128)(2,1)S(1)}, bf16[8,262144]{1,0:T(8,128)(2,1)}, u32[]{:S(2)}) %copy-start.1) | copy-done | bytes 4194328
  50.1 0.0 copy-start.3
  50.1 1.6 %copy-done.3 = bf16[16,256,256]{2,1,0:T(8,128)(2,1)S(1)} copy-done((bf16[16,256,256]{2,1,0:T(8,128)(2,1)S(1)}, bf16[16,256,256]{2,1,0:T(8,128)(2,1)}, u32[]{:S(2)}) %copy-start.3) | copy-done | bytes 2097176
  51.7 0.0 copy-start.5
  51.7 1.2 copy-done.5
  52.9 0.0 copy-start.6
  52.9 0.9 copy-done.6
  53.9 11.9 %head.4 = bf16[64,6,8,128]{3,2,1,0:T(8,128)(2,1)S(1)} custom-call(bf16[8,65536]{1,0:T(8,128)(2,1)S(1)} %copy-done.5, bf16[8,262144]{1,0:T(8,128)(2,1)S(1)} %copy-done.1, f32[16,4096]{1,0:T(8,128)S(1)} %copy-done.6, bf16[16,256,256]{2,1,0:T(8,128)(2,1)S(1)} %copy-done.3, bf16[16,256,256]{2,1,0:T(8,128)(2,1)S(1)} %copy-done.2), custom_call_target="tpu_custom_call" | custom-call | flops 3000000000 | bytes 3000000 | tf_op jit(solution)/shard_map/head/pallas_call | solution.py:231
  65.8 0.0 copy-start.7
  65.8 0.9 copy-done.7
  66.7 33.1 %all-to-all-done.2 = bf16[32,36,8,128]{3,2,1,0:T(8,128)(2,1)} async-done(((bf16[32,36,8,128]{3,2,1,0:T(8,128)(2,1)}), bf16[32,36,8,128]{3,2,1,0:T(8,128)(2,1)}, u32[]{:S(2)}, u32[]{:S(2)}) %all-to-all-start.2) | async-done | bytes 2359328 | tf_op jit(solution)/shard_map/all_to_all | solution.py:483
  99.7 4.2 %all-to-all-start = ((bf16[32,12,8,128]{3,2,1,0:T(8,128)(2,1)}), bf16[32,12,8,128]{3,2,1,0:T(8,128)(2,1)S(1)}, u32[]{:S(2)}, u32[]{:S(2)}) async-start(bf16[32,12,8,128]{3,2,1,0:T(8,128)(2,1)} %bitcast.70), calls=%async_computation | async-start | bytes 1572864 | tf_op jit(solution)/shard_map/all_to_all | solution.py:483
  103.9 9.2 %covariances.2.refs_3_ = f32[64,2,128,128]{3,2,1,0:T(8,128)} custom-call(bf16[16,2,2,18,8,128]{5,4,3,2,1,0:T(8,128)(2,1)} %bitcast.16.refs_0_, bf16[16,2,2,8,8,128]{5,4,3,2,1,0:T(8,128)(2,1)S(1)} %bitcast.67, f32[64,8,128]{2,1,0:T(8,128)S(1)} %select_maximum_fusion.refs_2_), custom_call_target="tpu_custom_call" | custom-call | flops 9600000000 | bytes 9600000 | tf_op jit(solution)/shard_map/covariances/pallas_call | solution.py:414
  113.2 11.2 %all-to-all-done = bf16[32,12,8,128]{3,2,1,0:T(8,128)(2,1)S(1)} async-done(((bf16[32,12,8,128]{3,2,1,0:T(8,128)(2,1)}), bf16[32,12,8,128]{3,2,1,0:T(8,128)(2,1)S(1)}, u32[]{:S(2)}, u32[]{:S(2)}) %all-to-all-start) | async-done | bytes 786464 | tf_op jit(solution)/shard_map/all_to_all | solution.py:483
  124.4 3.4 %covariances.3 = f32[64,2,128,128]{3,2,1,0:T(8,128)} custom-call(bf16[16,2,2,6,8,128]{5,4,3,2,1,0:T(8,128)(2,1)S(1)} %bitcast.69, bf16[16,2,2,8,8,128]{5,4,3,2,1,0:T(8,128)(2,1)S(1)} %bitcast.68, f32[64,8,128]{2,1,0:T(8,128)S(1)} %select_maximum_fusion.refs_2_, f32[64,2,128,128]{3,2,1,0:T(8,128)} %covariances.2.refs_3_), custom_call_target="tpu_custom_call", output_to_operand_aliasing={{}: (3, {})} | custom-call | flops 3200000000 | bytes 3200000 | tf_op jit(solution)/shard_map/covariances/pallas_call | solution.py:414
  (6 shorter events, 0.0 us)
Async XLA Ops:
  0.0 45.2 %copy-start = (f32[8,128]{1,0:T(8,128)S(1)}, f32[8,128]{1,0:T(8,128)}, u32[]{:S(2)}) copy-start(f32[8,128]{1,0:T(8,128)} %param.9) | copy-start | bytes 12292
  7.9 33.6 %all-to-all-start.1 = ((bf16[32,16,8,128]{3,2,1,0:T(8,128)(2,1)}), bf16[32,16,8,128]{3,2,1,0:T(8,128)(2,1)S(1)}, u32[]{:S(2)}, u32[]{:S(2)}) async-start(bf16[32,16,8,128]{3,2,1,0:T(8,128)(2,1)} %bitcast.72), calls=%async_computation.1 | async-start | bytes 2097152 | tf_op jit(solution)/shard_map/all_to_all | solution.py:483
  16.5 4.4 %collective-permute-start = (bf16[8,65536]{1,0:T(8,128)(2,1)S(1)}, bf16[8,65536]{1,0:T(8,128)(2,1)S(1)}, u32[]{:S(2)}, u32[]{:S(2)}) collective-permute-start(bf16[8,65536]{1,0:T(8,128)(2,1)S(1)} %slice.15), channel_id=1, source_target_pairs={{0,1},{2,3},{4,5},{6,7},{8,9},{10,11},{12,13},{14,15},{16,17},{18,... | collective-permute-start | bytes 3145736 | tf_op jit(solution)/shard_map/ppermute | solution.py:502
  20.9 1.0 copy-start.4
  41.4 3.8 %copy-start.9 = (s32[64]{0:T(128)S(1)}, s32[64]{0:T(128)}, u32[]{:S(2)}) copy-start(s32[64]{0:T(128)} %param.11) | copy-start | bytes 772
  41.4 3.8 %copy-start.8 = (s32[64,4]{0,1:T(4,128)S(1)}, s32[64,4]{0,1:T(4,128)}, u32[]{:S(2)}) copy-start(s32[64,4]{0,1:T(4,128)} %param.10) | copy-start | bytes 3076
  41.4 6.5 %copy-start.2 = (bf16[16,256,256]{2,1,0:T(8,128)(2,1)S(1)}, bf16[16,256,256]{2,1,0:T(8,128)(2,1)}, u32[]{:S(2)}) copy-start(bf16[16,256,256]{2,1,0:T(8,128)(2,1)} %constant.11.clone.refs_4_) | copy-start | bytes 6291460
  41.4 58.3 %all-to-all-start.2 = ((bf16[32,36,8,128]{3,2,1,0:T(8,128)(2,1)}), bf16[32,36,8,128]{3,2,1,0:T(8,128)(2,1)}, u32[]{:S(2)}, u32[]{:S(2)}) async-start(bf16[32,36,8,128]{3,2,1,0:T(8,128)(2,1)} %bitcast.71), calls=%async_computation.2 | async-start | bytes 4718592 | tf_op jit(solution)/shard_map/all_to_all | solution.py:483
  47.9 2.2 %copy-start.1 = (bf16[8,262144]{1,0:T(8,128)(2,1)S(1)}, bf16[8,262144]{1,0:T(8,128)(2,1)}, u32[]{:S(2)}) copy-start(bf16[8,262144]{1,0:T(8,128)(2,1)} %refs_1_.5) | copy-start | bytes 12582916
  50.1 1.6 %copy-start.3 = (bf16[16,256,256]{2,1,0:T(8,128)(2,1)S(1)}, bf16[16,256,256]{2,1,0:T(8,128)(2,1)}, u32[]{:S(2)}) copy-start(bf16[16,256,256]{2,1,0:T(8,128)(2,1)} %constant.10.clone.refs_3_) | copy-start | bytes 6291460
  51.7 1.2 copy-start.5
  52.9 0.9 copy-start.6
  65.8 0.9 copy-start.7
  99.7 24.6 %all-to-all-start = ((bf16[32,12,8,128]{3,2,1,0:T(8,128)(2,1)}), bf16[32,12,8,128]{3,2,1,0:T(8,128)(2,1)S(1)}, u32[]{:S(2)}, u32[]{:S(2)}) async-start(bf16[32,12,8,128]{3,2,1,0:T(8,128)(2,1)} %bitcast.70), calls=%async_computation | async-start | bytes 1572864 | tf_op jit(solution)/shard_map/all_to_all | solution.py:483
